TPU v7x, 32 devices: a whole 2x2x4 slice. The times are simulated.
32 devices in a mesh: dp: 8 (over z, y), ctx: 4 (over x, core).
Axes of the slice: x: 2, y: 2, z: 4, core: 2. Of those that a mesh axis runs over, the one named last changes fastest.
Arguments:
- tokens: bfloat16 [16, 256, 1152], P('dp', 'ctx'), may hold values from -6 to 6
- lengths: int32 [16], P('dp'), may hold values from 64 to 256, as said below
- gain_one: bfloat16 [1152], P('dp'), may hold values from 0.099609375 to 1.8984375
- w_qkv: bfloat16 [1152, 1920], P('dp', 'ctx'), may hold values from -0.25 to 0.25
- w_out: bfloat16 [1152, 1152], P('dp', 'ctx'), may hold values from -0.75 to 0.75
- gain_two: bfloat16 [1152], P('dp'), may hold values from 0.099609375 to 1.8984375
- w_gate_up: bfloat16 [1152, 6144], P('dp', 'ctx'), may hold values from -0.1875 to 0.1875
- w_down: bfloat16 [3072, 1152], P('dp', 'ctx'), may hold values from -0.109375 to 0.109375
- cotangent: bfloat16 [16, 256, 1152], P('dp', 'ctx'), may hold values from -6 to 6
Outputs:
- output: bfloat16 [16, 256, 1152], P('dp', 'ctx')
- grad_tokens: bfloat16 [16, 256, 1152], P('dp', 'ctx')
- grad_norm_one: float32 [1152], P('dp')
- grad_qkv: float32 [1152, 1920], P('dp', 'ctx')
- grad_out_proj: float32 [1152, 1152], P('dp', 'ctx')
- grad_norm_two: float32 [1152], P('dp')
- grad_gate_up: float32 [1152, 6144], P('dp', 'ctx')
- grad_down: float32 [3072, 1152], P('dp', 'ctx')
Inputs may be any that keep to these rules, and one draw needn't show every extreme that they name: `lengths`: in each run of 4 consecutive sequences (those of one dp index) one, which is drawn, fills all 256 slots; the others hold 64 slots or more.
All inputs are finite; a program needn't handle non-finite values.
Results may differ from a plain program's by a relative error of at most 0.02.
Values may be sent and summed in bfloat16 or wider, within the bound.
A program may use at most 128 MiB of HBM per device.

v0:
```python
import math

import jax
import jax.numpy as jnp
from jax import lax
from jax.sharding import PartitionSpec as P

QH = 18
KVH = 6
HD = 64
FF = 3072


EPS = 1e-05
NEGATIVE = -1e30


def angles(position, head_width):
    frequency = 10000.0 ** (-jnp.arange(head_width // 2, dtype=jnp.float32) * 2.0 / head_width)
    angle_table = position.astype(jnp.float32)[:, None] * frequency[None, :]
    return (jnp.cos(angle_table), jnp.sin(angle_table))


def rotate(values_in, cosine, sine_table):
    half_width = values_in.shape[-1] // 2
    first_half = values_in[..., :half_width]
    second = values_in[..., half_width:]
    return jnp.concatenate(
        [first_half * cosine - second * sine_table, second * cosine + first_half * sine_table],
        axis=-1,
    )


def split_heads(values_in, head_count):
    seq_count, row_count, col_count = values_in.shape
    head_width = col_count // head_count
    moved = values_in.reshape(seq_count, row_count, head_count, head_width).transpose(0, 2, 1, 3)
    return moved.reshape(seq_count * head_count, row_count, head_width)


def join_heads(values_in, seq_count):
    item_count, row_count, head_width = values_in.shape
    head_count = item_count // seq_count
    moved = values_in.reshape(seq_count, head_count, row_count, head_width).transpose(0, 2, 1, 3)
    return moved.reshape(seq_count, row_count, head_count * head_width)


def norm_back(source, inverse, gain, grad_in):
    scaled = grad_in * gain
    mean_term = jnp.mean(scaled * source, axis=-1, keepdims=True)
    back_rows = inverse * scaled - source * (inverse * inverse * inverse) * mean_term
    return (back_rows, jnp.sum(grad_in * source * inverse, axis=(0, 1)))


def block_scores(query_rows, key_rows, position, length, group_count, score_scale):
    raw_scores = (
        jnp.einsum("nd,td->nt", query_rows, key_rows, preferred_element_type=jnp.float32)
        * score_scale
    )
    raw_scores = raw_scores.reshape(group_count, position.shape[0], key_rows.shape[0])
    keyidx = jnp.arange(key_rows.shape[0], dtype=jnp.int32)
    allowed = (keyidx[None, :] <= position[:, None]) & (keyidx[None, :] < length)
    return jnp.where(allowed[None], raw_scores, NEGATIVE)


def on_device(tokens, lengths, gain_one, w_qkv, w_out, gain_two, w_gate_up, w_down, cotangent):
    forward_wide = (
        lax.all_gather(w_qkv, "ctx", axis=1, tiled=True),
        lax.all_gather(w_out, "ctx", axis=1, tiled=True),
        lax.all_gather(w_gate_up, "ctx", axis=1, tiled=True),
        lax.all_gather(w_down, "ctx", axis=1, tiled=True),
    )
    qkv_full, out_full, gate_up_full, down_full, gain_fa, gain_fb = (
        lax.all_gather(forward_wide[0], "dp", axis=0, tiled=True),
        lax.all_gather(forward_wide[1], "dp", axis=0, tiled=True),
        lax.all_gather(forward_wide[2], "dp", axis=0, tiled=True),
        lax.all_gather(forward_wide[3], "dp", axis=0, tiled=True),
        lax.all_gather(gain_one, "dp", axis=0, tiled=True),
        lax.all_gather(gain_two, "dp", axis=0, tiled=True),
    )
    seq_count, row_count, model_width = tokens.shape
    query_cols = QH * HD
    key_cols = KVH * HD
    group_count = QH // KVH
    score_scale = 1.0 / math.sqrt(HD)
    position = lax.axis_index("ctx") * row_count + jnp.arange(row_count, dtype=jnp.int32)
    valid_rows = position[None, :] < lengths[:, None]
    cosine, sine_table = angles(position, HD)
    cosine = cosine[:, None, :]
    sine_table = sine_table[:, None, :]
    source = tokens.astype(jnp.float32)
    inverse_one = lax.rsqrt(jnp.mean(source * source, axis=-1, keepdims=True) + EPS)
    normed_one = (source * inverse_one * gain_fa.astype(jnp.float32)).astype(jnp.bfloat16)
    projected = jnp.einsum("bsd,de->bse", normed_one, qkv_full, preferred_element_type=jnp.float32)
    queries = rotate(
        projected[..., :query_cols].reshape(seq_count, row_count, QH, HD), cosine, sine_table
    )
    queries = queries.astype(jnp.bfloat16).reshape(seq_count, row_count, query_cols)
    key_heads = rotate(
        projected[..., query_cols : query_cols + key_cols].reshape(seq_count, row_count, KVH, HD),
        cosine,
        sine_table,
    )
    key_heads = key_heads.astype(jnp.bfloat16).reshape(seq_count, row_count, key_cols)
    value_heads = projected[..., query_cols + key_cols :].astype(jnp.bfloat16)
    keys_all, values_all = (
        lax.all_gather(key_heads, "ctx", axis=1, tiled=True),
        lax.all_gather(value_heads, "ctx", axis=1, tiled=True),
    )
    query_blocks = split_heads(queries, QH).reshape(seq_count * KVH, group_count * row_count, HD)
    key_blocks = split_heads(keys_all, KVH)
    value_blocks = split_heads(values_all, KVH)
    pair_lengths = jnp.repeat(lengths, KVH)

    def forward_block(block_in):
        query_rows, key_rows, value_rows, length = block_in
        scores = block_scores(query_rows, key_rows, position, length, group_count, score_scale)
        row_max = jnp.max(scores, axis=-1, keepdims=True)
        exp_terms = jnp.exp(scores - row_max)
        row_total = jnp.sum(exp_terms, axis=-1, keepdims=True)
        prob_rows = (exp_terms / row_total).astype(jnp.bfloat16)
        result = jnp.einsum(
            "gst,td->gsd", prob_rows, value_rows, preferred_element_type=jnp.float32
        )
        return (result.reshape(-1, HD), (row_max + jnp.log(row_total))[..., 0])

    context_blocks, log_totals = lax.map(
        forward_block, (query_blocks, key_blocks, value_blocks, pair_lengths)
    )
    context = join_heads(context_blocks.reshape(seq_count * QH, row_count, HD), seq_count).astype(
        jnp.bfloat16
    )
    hidden = source + jnp.einsum(
        "bse,ed->bsd", context, out_full, preferred_element_type=jnp.float32
    )
    inverse_two = lax.rsqrt(jnp.mean(hidden * hidden, axis=-1, keepdims=True) + EPS)
    normed_two = (hidden * inverse_two * gain_fb.astype(jnp.float32)).astype(jnp.bfloat16)
    gate_up = jnp.einsum(
        "bsd,df->bsf", normed_two, gate_up_full, preferred_element_type=jnp.float32
    )
    gate_part = gate_up[..., :FF]
    up_part = gate_up[..., FF:]
    gate_sig = jax.nn.sigmoid(gate_part)
    swish_part = gate_part * gate_sig
    activation = (swish_part * up_part).astype(jnp.bfloat16)
    result_rows = hidden + jnp.einsum(
        "bsf,fd->bsd", activation, down_full, preferred_element_type=jnp.float32
    )
    output = jnp.where(valid_rows[..., None], result_rows, 0.0).astype(jnp.bfloat16)
    back_wide = (
        lax.all_gather(w_qkv, "ctx", axis=1, tiled=True),
        lax.all_gather(w_out, "ctx", axis=1, tiled=True),
        lax.all_gather(w_gate_up, "ctx", axis=1, tiled=True),
        lax.all_gather(w_down, "ctx", axis=1, tiled=True),
    )
    qkv_back, out_back, gate_up_back, down_back, gain_ba, gain_bb = (
        lax.all_gather(back_wide[0], "dp", axis=0, tiled=True),
        lax.all_gather(back_wide[1], "dp", axis=0, tiled=True),
        lax.all_gather(back_wide[2], "dp", axis=0, tiled=True),
        lax.all_gather(back_wide[3], "dp", axis=0, tiled=True),
        lax.all_gather(gain_one, "dp", axis=0, tiled=True),
        lax.all_gather(gain_two, "dp", axis=0, tiled=True),
    )
    grad_rows = jnp.where(valid_rows[..., None], cotangent, jnp.zeros_like(cotangent))
    grad_activation = jnp.einsum(
        "bsd,fd->bsf", grad_rows, down_back, preferred_element_type=jnp.float32
    )
    grad_gate = grad_activation * up_part * gate_sig * (1.0 + gate_part * (1.0 - gate_sig))
    grad_up = grad_activation * swish_part
    grad_mix = jnp.concatenate([grad_gate, grad_up], axis=-1).astype(jnp.bfloat16)
    grad_normed_two = jnp.einsum(
        "bsf,df->bsd", grad_mix, gate_up_back, preferred_element_type=jnp.float32
    )
    back_two, grad_gain_two = norm_back(
        hidden, inverse_two, gain_bb.astype(jnp.float32), grad_normed_two
    )
    grad_hidden = grad_rows.astype(jnp.float32) + back_two
    grad_branch = grad_hidden.astype(jnp.bfloat16)
    grad_context = jnp.einsum(
        "bsd,ed->bse", grad_branch, out_back, preferred_element_type=jnp.float32
    ).astype(jnp.bfloat16)
    grad_blocks = split_heads(grad_context, QH).reshape(
        seq_count * KVH, group_count * row_count, HD
    )

    def backward_block(block_in):
        query_rows, key_rows, value_rows, length, log_total, grad_in = block_in
        scores = block_scores(query_rows, key_rows, position, length, group_count, score_scale)
        prob_rows = jnp.exp(scores - log_total[..., None])
        grad_grouped = grad_in.reshape(group_count, -1, HD)
        grad_probs = jnp.einsum(
            "gsd,td->gst", grad_grouped, value_rows, preferred_element_type=jnp.float32
        )
        grad_value = jnp.einsum(
            "gst,gsd->td",
            prob_rows.astype(jnp.bfloat16),
            grad_grouped,
            preferred_element_type=jnp.float32,
        )
        row_delta = jnp.sum(prob_rows * grad_probs, axis=-1, keepdims=True)
        grad_scores = (prob_rows * (grad_probs - row_delta)).astype(jnp.bfloat16)
        grad_query = (
            jnp.einsum("gst,td->gsd", grad_scores, key_rows, preferred_element_type=jnp.float32)
            * score_scale
        )
        grad_key = (
            jnp.einsum(
                "gst,gsd->td",
                grad_scores,
                query_rows.reshape(group_count, -1, HD),
                preferred_element_type=jnp.float32,
            )
            * score_scale
        )
        return (grad_query.reshape(-1, HD), grad_key, grad_value)

    query_grads, key_grads, value_grads = lax.map(
        backward_block,
        (query_blocks, key_blocks, value_blocks, pair_lengths, log_totals, grad_blocks),
    )
    key_sums, value_sums = (
        lax.psum_scatter(
            join_heads(key_grads, seq_count).astype(jnp.bfloat16),
            "ctx",
            scatter_dimension=1,
            tiled=True,
        ).astype(jnp.float32),
        lax.psum_scatter(
            join_heads(value_grads, seq_count).astype(jnp.bfloat16),
            "ctx",
            scatter_dimension=1,
            tiled=True,
        ).astype(jnp.float32),
    )
    grad_queries = join_heads(query_grads.reshape(seq_count * QH, row_count, HD), seq_count)
    turned_queries = rotate(grad_queries.reshape(seq_count, row_count, QH, HD), cosine, -sine_table)
    turned_keys = rotate(key_sums.reshape(seq_count, row_count, KVH, HD), cosine, -sine_table)
    grad_mixed = jnp.concatenate(
        [
            turned_queries.reshape(seq_count, row_count, query_cols),
            turned_keys.reshape(seq_count, row_count, key_cols),
            value_sums,
        ],
        axis=-1,
    ).astype(jnp.bfloat16)
    grad_normed_one = jnp.einsum(
        "bse,de->bsd", grad_mixed, qkv_back, preferred_element_type=jnp.float32
    )
    back_one, grad_gain_one = norm_back(
        source, inverse_one, gain_ba.astype(jnp.float32), grad_normed_one
    )
    grad_tokens = (grad_hidden + back_one).astype(jnp.bfloat16)
    exchanged = (
        lax.all_to_all(grad_mixed, "ctx", split_axis=2, concat_axis=1, tiled=True),
        lax.all_to_all(grad_branch, "ctx", split_axis=2, concat_axis=1, tiled=True),
        lax.all_to_all(grad_mix, "ctx", split_axis=2, concat_axis=1, tiled=True),
        lax.all_to_all(grad_rows, "ctx", split_axis=2, concat_axis=1, tiled=True),
    )
    initial = (
        jnp.zeros((model_width, exchanged[0].shape[2]), jnp.float32),
        jnp.zeros((context.shape[2], exchanged[1].shape[2]), jnp.float32),
        jnp.zeros((model_width, exchanged[2].shape[2]), jnp.float32),
        jnp.zeros((activation.shape[2], exchanged[3].shape[2]), jnp.float32),
    )
    pieces = (
        lax.all_gather(normed_one, "ctx", axis=1, tiled=True),
        lax.all_gather(context, "ctx", axis=1, tiled=True),
        lax.all_gather(normed_two, "ctx", axis=1, tiled=True),
        lax.all_gather(activation, "ctx", axis=1, tiled=True),
    )
    updated = []
    for total, piece, right in zip(initial, pieces, exchanged):
        updated.append(jnp.einsum("bsr,bsc->rc", piece, right, preferred_element_type=jnp.float32))
    column_grads = tuple(updated)
    gain_whole = lax.psum((grad_gain_one, grad_gain_two), "ctx")
    final_qkv, final_out, final_gate_up, final_down, final_gain_one, final_gain_two = (
        lax.psum_scatter(
            column_grads[0].astype(jnp.bfloat16), "dp", scatter_dimension=0, tiled=True
        ).astype(jnp.float32),
        lax.psum_scatter(
            column_grads[1].astype(jnp.bfloat16), "dp", scatter_dimension=0, tiled=True
        ).astype(jnp.float32),
        lax.psum_scatter(
            column_grads[2].astype(jnp.bfloat16), "dp", scatter_dimension=0, tiled=True
        ).astype(jnp.float32),
        lax.psum_scatter(
            column_grads[3].astype(jnp.bfloat16), "dp", scatter_dimension=0, tiled=True
        ).astype(jnp.float32),
        lax.psum_scatter(
            gain_whole[0].astype(jnp.bfloat16), "dp", scatter_dimension=0, tiled=True
        ).astype(jnp.float32),
        lax.psum_scatter(
            gain_whole[1].astype(jnp.bfloat16), "dp", scatter_dimension=0, tiled=True
        ).astype(jnp.float32),
    )
    return (
        output,
        grad_tokens,
        final_gain_one,
        final_qkv,
        final_out,
        final_gain_two,
        final_gate_up,
        final_down,
    )


def solution(mesh):
    return jax.shard_map(
        on_device,
        mesh=mesh,
        in_specs=(
            P("dp", "ctx", None),
            P("dp"),
            P("dp"),
            P("dp", "ctx"),
            P("dp", "ctx"),
            P("dp"),
            P("dp", "ctx"),
            P("dp", "ctx"),
            P("dp", "ctx", None),
        ),
        out_specs=(
            P("dp", "ctx", None),
            P("dp", "ctx", None),
            P("dp"),
            P("dp", "ctx"),
            P("dp", "ctx"),
            P("dp"),
            P("dp", "ctx"),
            P("dp", "ctx"),
        ),
        check_vma=False,
    )
```

profile of v0, /device:TPU:0, one launch (start us, length us, event | category | flops | bytes accessed | tf_op | source)
XLA Modules:
  0.0 1029.7 jit_solution(3989720615579372317)
XLA Ops:
  7.9 9.2 all-gather
  17.6 1.5 reshape.401
  19.2 9.3 all-gather.1
  28.6 1.1 reshape.403
  29.8 5.7 all-gather.16.cloned.1.call-done
  35.5 9.1 all_gather.68
  44.7 1.5 copy.121
  48.8 22.3 %all-reduce.7 = (bf16[1152]{0:T(1024)(128)(2,1)S(1)}, bf16[1152]{0:T(1024)(128)(2,1)S(1)}) all-reduce(bf16[1152]{0:T(1024)(128)(2,1)S(1)} %dynamic-update-slice, bf16[1152]{0:T(1024)(128)(2,1)S(1)} %dynamic-update-slice.1), channel_id=1, replica_groups=mesh['dp'=8,'ctx'=4] {'dp'}, use_global_device_ids=true, to_apply=%add | all-reduce | flops 2304 | bytes 9216
  73.1 41.5 %all-gather.12.cloned.1.call-done = bf16[1152,1920]{1,0:T(8,128)(2,1)} async-done(((bf16[144,1920]{1,0:T(8,128)(2,1)}), bf16[1152,1920]{1,0:T(8,128)(2,1)}) %all-gather.12.cloned.1.call-update) | async-done | bytes 4423696 | tf_op jit(solution)/shard_map/all_gather | solution.py:74
  114.6 3.1 fusion.45
  119.3 1.5 reshape.381
  123.1 6.4 all_gather.61
  129.7 6.8 all_gather.62
  136.7 33.0 %while.28 = (s32[]{:T(128)}, bf16[12,192,64]{1,2,0:T(8,128)(2,1)S(1)}, f32[12,3,64]{2,1,0:T(4,128)}, s32[12]{0:T(128)S(1)}, bf16[12,192,64]{2,1,0:T(8,128)(2,1)S...) while((s32[]{:T(128)}, ...), condition=%wide.region_4.5_spmd.clone, body=%wide.region_1.4_spmd.clone.sunk | while | flops 13009026 | bytes 915325 | solution.py:127
  170.9 2.5 multiply_reduce_fusion.3
  173.6 192.9 %all-gather.18.cloned.1.call-done = bf16[1152,6144]{1,0:T(8,128)(2,1)} async-done(((bf16[144,6144]{1,0:T(8,128)(2,1)}), bf16[1152,6144]{1,0:T(8,128)(2,1)}) %all-gather.18.cloned.1.call-update) | async-done | bytes 14155792 | tf_op jit(solution)/shard_map/all_gather | solution.py:76
  366.4 8.9 fusion.36
  375.3 100.7 %all-gather.20.cloned.1.call-done = bf16[3072,1152]{1,0:T(8,128)(2,1)} async-done(((bf16[384,1152]{1,0:T(8,128)(2,1)}), bf16[3072,1152]{1,0:T(8,128)(2,1)}) %all-gather.20.cloned.1.call-update) | async-done | bytes 7077904 | tf_op jit(solution)/shard_map/all_gather | solution.py:77
  476.1 7.3 multiply_convert_fusion.2
  483.4 10.4 %multiply_reduce_fusion.1 = (f32[1152]{0:T(1024)S(1)}, f32[2,64]{1,0:T(2,128)S(1)}, f32[2,64,1152]{2,1,0:T(8,128)S(1)}) fusion(f32[2,64,1152]{2,1,0:T(8,128)S(1)} %get-tuple-element.276, f32[2,64]{1,0:T(2,128)S(1)} %get-tuple-element.272, f32[1152]{0:T(1024)S(1)} %convert_element_type.148, bf16[1152,6144]{1,0:T(8,128)(2,1)} %all-gather.18.cloned.1.call-done, ...), kind=kOutput, calls=%fused_computation.113 | convolution fusion | flops 1815968512 | bytes 16918528 | tf_op jit(solution)/shard_map/bsf,df->bsd/dot_general | solution.py:171
  494.6 1.6 fusion.66
  496.2 1.5 reshape.387
  498.6 87.8 %while.29 = (s32[]{:T(128)}, f32[12,192,64]{2,1,0:T(8,128)}, bf16[12,256,64]{1,2,0:T(8,128)(2,1)}, bf16[12,256,64]{1,2,0:T(8,128)(2,1)}, s32[12]{0:T(128)S(1)}, ...) while((s32[]{:T(128)}, f32[12,192,64]{2,1,0:T(8,128)}, ...), condition=%wide.region_9.10_spmd.clone, body=%wide.region_7.9_spmd.clone.sunk | while | flops 32157824 | bytes 2198193 | solution.py:217
  502.4 1.0 multiply_reduce_fusion.5
  517.0 1.0 multiply_reduce_fusion.5
  524.3 1.0 multiply_reduce_fusion.5
  531.5 1.0 multiply_reduce_fusion.5
  560.8 1.0 multiply_reduce_fusion.5
  568.2 1.0 multiply_reduce_fusion.5
  586.4 2.0 copy.124
  594.5 2.0 copy.155
  598.0 1.2 reshape.431
  599.1 3.5 all-to-all-start.1
  602.7 16.7 %all-reduce.10.cloned.1.call-done = bf16[2,256,384]{2,0,1:T(2,128)(2,1)} async-done(((bf16[2,256,384]{2,0,1:T(2,128)(2,1)}), bf16[2,256,384]{2,0,1:T(2,128)(2,1)}) %all-reduce.10.cloned.1.call-update) | async-done | bytes 393232
  621.2 17.3 %all-gather.24.cloned.1.call-done = bf16[2,256,1152]{2,1,0:T(8,128)(2,1)} async-done(((bf16[2,64,1152]{2,1,0:T(8,128)(2,1)}), bf16[2,256,1152]{2,1,0:T(8,128)(2,1)}) %all-gather.24.cloned.1.call-update) | async-done | bytes 1179664 | tf_op jit(solution)/shard_map/all_gather | solution.py:267
  638.5 3.0 fusion.49
  642.4 19.6 %reduce-scatter.8.cloned.1.call-done = bf16[2,64,384]{2,1,0:T(8,128)(2,1)} async-done(((bf16[2,256,384]{2,1,0:T(8,128)(2,1)}), bf16[2,64,384]{2,1,0:T(8,128)(2,1)}) %reduce-scatter.8.cloned.1.call-update) | async-done | bytes 98320 | tf_op jit(solution)/shard_map/reduce_scatter | solution.py:228
  664.4 13.8 %all_to_all.72 = bf16[4,2,30720]{2,1,0:T(2,128)(2,1)} all-to-all(bf16[4,2,30720]{2,1,0:T(2,128)(2,1)S(1)} %reshape.429), channel_id=1, replica_groups=mesh['dp'=8,'ctx'=4] {'ctx'}, dimensions={0} | all-to-all | bytes 983040 | tf_op jit(solution)/shard_map/all_to_all | solution.py:254
  678.2 2.9 reshape.430
  681.8 1.9 all-gather.22.cloned.1.call-done
  683.6 3.2 fusion.48
  688.1 11.4 %all_to_all.73 = bf16[4,2,18432]{2,1,0:T(2,128)(2,1)S(1)} all-to-all(bf16[4,2,18432]{2,1,0:T(2,128)(2,1)S(1)} %reshape.435), channel_id=1, replica_groups=mesh['dp'=8,'ctx'=4] {'ctx'}, dimensions={0} | all-to-all | bytes 589824 | tf_op jit(solution)/shard_map/all_to_all | solution.py:257
  700.3 15.2 %all-gather.28.cloned.1.call-done = bf16[2,256,3072]{2,1,0:T(8,128)(2,1)} async-done(((bf16[2,64,3072]{2,1,0:T(8,128)(2,1)}), bf16[2,256,3072]{2,1,0:T(8,128)(2,1)}) %all-gather.28.cloned.1.call-update) | async-done | bytes 3145744 | tf_op jit(solution)/shard_map/all_gather | solution.py:269
  715.5 4.3 fusion.47
  719.8 4.0 copy.143
  723.9 1.7 pad_maximum_fusion
  725.5 5.2 copy.133
  730.7 4.1 reshape.433
  734.8 23.3 %all_to_all.74 = bf16[4,2,98304]{2,1,0:T(2,128)(2,1)} all-to-all(bf16[4,2,98304]{2,1,0:T(2,128)(2,1)S(1)} %reshape.433), channel_id=1, replica_groups=mesh['dp'=8,'ctx'=4] {'ctx'}, dimensions={0} | all-to-all | bytes 3145728 | tf_op jit(solution)/shard_map/all_to_all | solution.py:256
  758.1 4.9 reshape.434
  763.1 6.9 copy.134
  770.0 5.1 fusion.38
  776.2 5.1 fusion.63
  781.3 1.5 fusion.79
  782.8 10.6 %all-reduce.5 = (bf16[1152]{0:T(1024)(128)(2,1)S(1)}, bf16[1152]{0:T(1024)(128)(2,1)S(1)}) all-reduce(f32[1152]{0:T(1024)S(1)} %get-tuple-element.201, f32[1152]{0:T(1024)S(1)} %get-tuple-element.199), channel_id=1, replica_groups=mesh['dp'=8,'ctx'=4] {'ctx'}, use_global_device_ids=true, to_apply=%region_14.15 | all-reduce | flops 2304 | bytes 13824 | tf_op jit(solution)/shard_map/psum | solution.py:275
  793.4 21.2 %all-reduce.6 = (bf16[1152]{0:T(1024)(128)(2,1)S(1)}, bf16[1152]{0:T(1024)(128)(2,1)S(1)}) all-reduce(bf16[1152]{0:T(1024)(128)(2,1)S(1)} %get-tuple-element.241, bf16[1152]{0:T(1024)(128)(2,1)S(1)} %get-tuple-element.242), channel_id=4, replica_groups=mesh['dp'=8,'ctx'=4] {'dp'}, use_global_device_ids=true, to_apply=%region_15.16.clone | all-reduce | flops 2304 | bytes 9216
  815.3 1.1 fusion.76
  816.4 1.6 convert_element_type.169
  818.0 48.9 %reduce-scatter.10.cloned.1.call-done = bf16[144,480]{1,0:T(8,128)(2,1)} async-done(((bf16[1152,480]{1,0:T(8,128)(2,1)}), bf16[144,480]{1,0:T(8,128)(2,1)}) %reduce-scatter.10.cloned.1.call-update) | async-done | bytes 138256 | tf_op jit(solution)/shard_map/reduce_scatter | solution.py:277
  866.9 1.7 convert_element_type.167
  868.5 70.1 %reduce-scatter.16.cloned.1.call-done = bf16[384,288]{1,0:T(8,128)(2,1)} async-done(((bf16[3072,288]{1,0:T(8,128)(2,1)}), bf16[384,288]{1,0:T(8,128)(2,1)}) %reduce-scatter.16.cloned.1.call-update) | async-done | bytes 221200
  938.7 1.1 copy.144
  940.6 80.1 %reduce-scatter.14.cloned.1.call-done = bf16[144,1536]{1,0:T(8,128)(2,1)} async-done(((bf16[1152,1536]{1,0:T(8,128)(2,1)}), bf16[144,1536]{1,0:T(8,128)(2,1)}) %reduce-scatter.14.cloned.1.call-update) | async-done | bytes 442384 | tf_op jit(solution)/shard_map/reduce_scatter | solution.py:283
  1020.8 2.0 convert_element_type.173
  (484 shorter events, 143.1 us)
Async XLA Ops:
  7.2 28.3 %all-gather.16.cloned.1.call-start = ((), (), s32[]{:S(2)}) async-start(), calls=%async_computation.11 | async-start | bytes 2211840 | tf_op jit(solution)/shard_map/all_gather | solution.py:70
  7.9 106.7 %all-gather.12.cloned.1.call-start = ((), (), s32[]{:S(2)}) async-start(), calls=%async_computation.9 | async-start | bytes 4976640 | tf_op jit(solution)/shard_map/all_gather | solution.py:74
  17.1 2.0 copy-start.20
  19.1 151.8 %all-gather.14.cloned.1.call-start = ((), (), s32[]{:S(2)}) async-start(), calls=%async_computation.10 | async-start | bytes 2985984 | tf_op jit(solution)/shard_map/all_gather | solution.py:75
  28.6 6.9 copy-start.19
  29.7 336.7 %all-gather.18.cloned.1.call-start = ((), (), s32[]{:S(2)}) async-start(), calls=%async_computation.12 | async-start | bytes 15925248 | tf_op jit(solution)/shard_map/all_gather | solution.py:76
  35.4 440.6 %all-gather.20.cloned.1.call-start = ((), (), s32[]{:S(2)}) async-start(), calls=%async_computation.13 | async-start | bytes 7962624 | tf_op jit(solution)/shard_map/all_gather | solution.py:77
  44.6 1.7 copy-start.29
  44.6 2.3 copy-start.26
  44.6 3.6 copy-start.27
  44.6 3.9 copy-start.28
  44.7 26.4 %copy-start.1 = (bf16[2,64,1152]{2,1,0:T(8,128)(2,1)S(1)}, bf16[2,64,1152]{2,1,0:T(8,128)(2,1)}, u32[]{:S(2)}) copy-start(bf16[2,64,1152]{2,1,0:T(8,128)(2,1)} %param.13) | copy-start | bytes 884740
  44.7 27.6 %copy-start.7 = (bf16[2,64,1152]{2,1,0:T(8,128)(2,1)S(1)}, bf16[2,64,1152]{2,1,0:T(8,128)(2,1)}, u32[]{:S(2)}) copy-start(bf16[2,64,1152]{2,1,0:T(8,128)(2,1)} %param.21) | copy-start | bytes 884740
  46.2 573.2 %all-reduce.10.cloned.1.call-start = ((), (), s32[]{:S(2)}) async-start(), calls=%async_computation.23 | async-start | bytes 786432
  71.8 1.3 copy-start.21
  71.9 1.2 copy-start.23
  72.0 45.7 %copy-start.5 = (bf16[2,64,1152]{2,1,0:T(8,128)(2,1)}, bf16[2,64,1152]{2,1,0:T(8,128)(2,1)S(1)}, u32[]{:S(2)}) copy-start(bf16[2,64,1152]{2,1,0:T(8,128)(2,1)S(1)} %fusion.72) | copy-start | bytes 884740
  117.7 3.0 copy-start.4
  121.4 0.9 slice-start.2
  122.7 7.0 copy-start.18
  122.9 13.8 %copy-start.17 = (bf16[12,192,64]{1,2,0:T(8,128)(2,1)S(1)}, bf16[12,192,64]{1,2,0:T(8,128)(2,1)}, u32[]{:S(2)}) copy-start(bf16[12,192,64]{1,2,0:T(8,128)(2,1)} %custom-call.1) | copy-start | bytes 884740
  122.9 13.8 %copy-start.31 = (s32[12]{0:T(128)S(1)}, s32[12]{0:T(128)}, u32[]{:S(2)}) copy-start(s32[12]{0:T(128)} %reshape.380) | copy-start | bytes 148
  169.7 1.1 copy-start.13
  170.8 2.6 copy-start.3
  173.6 201.8 %copy-start.6 = (bf16[2,64,1152]{2,1,0:T(8,128)(2,1)}, bf16[2,64,1152]{2,1,0:T(8,128)(2,1)S(1)}, u32[]{:S(2)}) copy-start(bf16[2,64,1152]{2,1,0:T(8,128)(2,1)S(1)} %multiply_convert_fusion.4) | copy-start | bytes 884740
  173.6 302.5 %copy-start.11 = (bf16[2,64,1152]{2,1,0:T(8,128)(2,1)S(1)}, bf16[2,64,1152]{2,1,0:T(8,128)(2,1)}, u32[]{:S(2)}) copy-start(bf16[2,64,1152]{2,1,0:T(8,128)(2,1)} %broadcast_select_fusion) | copy-start | bytes 884740
  483.4 10.4 %copy-start.14 = (bf16[2,64,3072]{2,1,0:T(8,128)(2,1)}, bf16[2,64,3072]{2,1,0:T(8,128)(2,1)S(1)}, u32[]{:S(2)}) copy-start(bf16[2,64,3072]{2,1,0:T(8,128)(2,1)S(1)} %get-tuple-element.255) | copy-start | bytes 2359300
  483.4 10.4 %copy-start.15 = (bf16[2,64,3072]{2,1,0:T(8,128)(2,1)}, bf16[2,64,3072]{2,1,0:T(8,128)(2,1)S(1)}, u32[]{:S(2)}) copy-start(bf16[2,64,3072]{2,1,0:T(8,128)(2,1)S(1)} %get-tuple-element.256) | copy-start | bytes 2359300
  483.4 10.4 %copy-start.8 = (bf16[2,64,1152]{2,1,0:T(8,128)(2,1)S(1)}, bf16[2,64,1152]{2,1,0:T(8,128)(2,1)}, u32[]{:S(2)}) copy-start(bf16[2,64,1152]{2,1,0:T(8,128)(2,1)} %param.21) | copy-start | bytes 884740
  483.4 10.4 %copy-start.24 = (pred[2,64]{1,0:T(4,128)(4,1)S(1)}, pred[2,64]{1,0:T(4,128)(4,1)}, u32[]{:S(2)}) copy-start(pred[2,64]{1,0:T(4,128)(4,1)} %copy-done.23) | copy-start | bytes 388
  483.4 11.2 %copy-start = (bf16[1152,1152]{1,0:T(8,128)(2,1)S(1)}, bf16[1152,1152]{1,0:T(8,128)(2,1)}, u32[]{:S(2)}) copy-start(bf16[1152,1152]{1,0:T(8,128)(2,1)} %all-gather.14.cloned.1.call-done) | copy-start | bytes 7962628
  493.8 0.8 copy-start.9
  496.2 2.4 copy-start.32
  586.4 3.0 copy-start.16
  588.4 4.1 copy-start.30
  588.4 50.1 %all-gather.24.cloned.1.call-start = ((), (), s32[]{:S(2)}) async-start(), calls=%async_computation.17 | async-start | bytes 1474560 | tf_op jit(solution)/shard_map/all_gather | solution.py:267
  589.2 72.8 %reduce-scatter.8.cloned.1.call-start = ((), (), s32[]{:S(2)}) async-start(), calls=%async_computation.14 | async-start | bytes 491520 | tf_op jit(solution)/shard_map/reduce_scatter | solution.py:228
  590.4 93.2 %all-gather.22.cloned.1.call-start = ((), (), s32[]{:S(2)}) async-start(), calls=%async_computation.15 | async-start | bytes 1474560 | tf_op jit(solution)/shard_map/all_gather | solution.py:266
  591.2 124.4 %all-gather.28.cloned.1.call-start = ((), (), s32[]{:S(2)}) async-start(), calls=%async_computation.21 | async-start | bytes 3932160 | tf_op jit(solution)/shard_map/all_gather | solution.py:269
  591.7 178.2 %all-gather.26.cloned.1.call-start = ((), (), s32[]{:S(2)}) async-start(), calls=%async_computation.19 | async-start | bytes 1474560 | tf_op jit(solution)/shard_map/all_gather | solution.py:268
  599.1 21.2 %all-to-all-start.1 = ((bf16[4,2,18432]{2,1,0:T(2,128)(2,1)}), bf16[4,2,18432]{2,1,0:T(2,128)(2,1)S(1)}, u32[]{:S(2)}, u32[]{:S(2)}) async-start(bf16[4,2,18432]{2,1,0:T(2,128)(2,1)} %reshape.431), calls=%async_computation.3 | async-start | bytes 589824 | tf_op jit(solution)/shard_map/all_to_all | solution.py:255
  602.6 213.8 %reduce-scatter.12.cloned.1.call-start = ((), (), s32[]{:S(2)}) async-start(), calls=%async_computation.18 | async-start | bytes 995328 | tf_op jit(solution)/shard_map/reduce_scatter | solution.py:280
  641.5 225.4 %reduce-scatter.10.cloned.1.call-start = ((), (), s32[]{:S(2)}) async-start(), calls=%async_computation.16 | async-start | bytes 1327104 | tf_op jit(solution)/shard_map/reduce_scatter | solution.py:277
  683.6 3.3 copy-start.12
  686.9 251.8 %reduce-scatter.16.cloned.1.call-start = ((), (), s32[]{:S(2)}) async-start(), calls=%async_computation.22 | async-start | bytes 2654208
  723.8 296.9 %reduce-scatter.14.cloned.1.call-start = ((), (), s32[]{:S(2)}) async-start(), calls=%async_computation.20 | async-start | bytes 3981312 | tf_op jit(solution)/shard_map/reduce_scatter | solution.py:283
  775.0 1.1 copy-start.2
  775.0 6.2 slice-start
  776.2 5.1 slice-start.1
  776.2 5.1 copy-start.22
  781.3 34.0 %copy-start.10 = (f32[2,64,1152]{2,1,0:T(8,128)S(1)}, f32[2,64,1152]{2,1,0:T(8,128)}, u32[]{:S(2)}) copy-start(f32[2,64,1152]{2,1,0:T(8,128)} %copy-done.9) | copy-start | bytes 1769476
  781.3 34.0 %copy-start.25 = (f32[2,64]{1,0:T(2,128)S(1)}, f32[2,64]{1,0:T(2,128)}, u32[]{:S(2)}) copy-start(f32[2,64]{1,0:T(2,128)} %get-tuple-element.266) | copy-start | bytes 1540
Sparse Core Ops, SparseCore 0:
  9.6 25.8 all-gather.15
  37.6 76.9 all-gather.11
  116.8 53.2 all-gather.13
  172.1 194.2 all-gather.17
  369.0 106.9 all-gather.19
  588.5 30.7 all-reduce.9
  621.0 17.4 all-gather.23
  641.1 20.8 reduce-scatter.7
  664.2 19.3 all-gather.21
  685.1 30.3 all-gather.27
  717.2 17.4 all-gather.25
  738.9 61.1 reduce-scatter.11
  803.9 62.9 reduce-scatter.9
  870.6 68.0 reduce-scatter.15
  942.6 78.1 reduce-scatter.13
where the time goes:
time: 1040 us; the launch traced here: 1030 us
  waiting for transfers between devices  614 us (59%)
  blocking collectives  143 us (14%)
  local copies, waits for them, and re-layouts  116 us (11%)
  matrix products  97.4 us (9%)
  other arithmetic  36.5 us (4%)
  between operations  17.2 us (2%)
    all_gather x1, waiting for transfers between devices, on_device(): lax.all_gather(forward_wide[2], 'dp', axis=0, tiled=True)  193 us
    all_gather x1, waiting for transfers between devices, on_device(): lax.all_gather(forward_wide[3], 'dp', axis=0, tiled=True)  101 us
    unnamed x17, waiting for transfers between devices  90.3 us
    reduce_scatter x1, waiting for transfers between devices, on_device(): lax.psum_scatter(column_grads[2].astype(jnp.bfloat16), 'dp', scatter_dime...  80.1 us
    reduce_scatter x1, waiting for transfers between devices, on_device(): lax.psum_scatter(column_grads[0].astype(jnp.bfloat16), 'dp', scatter_dime...  48.9 us
    unnamed x2, blocking collectives  43.5 us
    all_gather x1, waiting for transfers between devices, on_device(): lax.all_gather(forward_wide[0], 'dp', axis=0, tiled=True)  41.5 us
    unnamed x91, local copies, waits for them, and re-layouts  26.5 us
  transfers between devices with their start and end apart: 16, of which 12 were waited for; matrix products, arithmetic and copies ran while one was open for 13% of the time, Pallas kernels for 0%

commit v1 on v0

--- a/solution.py
+++ b/solution.py
@@ -1,8 +1,11 @@
+import functools
 import math
 
 import jax
 import jax.numpy as jnp
 from jax import lax
+from jax.experimental import pallas as pl
+from jax.experimental.pallas import tpu as pltpu
 from jax.sharding import PartitionSpec as P
 
 QH = 18
@@ -305,9 +308,757 @@
     )
 
 
+MESH = pl.DeviceIdType.MESH
+
+
+class Place:
+    def __init__(self):
+        self.dp = lax.axis_index("dp")
+        self.ctx = lax.axis_index("ctx")
+        self.z = lax.div(self.dp, 2)
+        self.y = lax.rem(self.dp, 2)
+        self.x = lax.div(self.ctx, 2)
+        self.c = lax.rem(self.ctx, 2)
+        self.up = (self.dp + 2, self.ctx)
+        self.down = (self.dp - 2, self.ctx)
+        self.across = (self.dp + 1 - 2 * self.y, self.ctx)
+        self.chip = (self.dp, (1 - self.x) * 2 + self.c)
+        self.core = (self.dp, self.x * 2 + 1 - self.c)
+        self.has_up = self.z < 3
+        self.has_down = self.z > 0
+
+
+def greet(place):
+    barrier = pltpu.get_barrier_semaphore()
+
+    def tell(device):
+        pl.semaphore_signal(barrier, inc=1, device_id=device, device_id_type=MESH)
+
+    pl.when(place.has_up)(lambda: tell(place.up))
+    pl.when(place.has_down)(lambda: tell(place.down))
+    tell(place.across)
+    for step in (1, 2, 3):
+        tell((place.dp, lax.rem(place.ctx + step, 4)))
+    ends = place.has_up.astype(jnp.int32) + place.has_down.astype(jnp.int32)
+    pl.semaphore_wait(barrier, 4 + ends)
+
+
+class Wires:
+    def __init__(self, send_sems, recv_sems, names):
+        self.send_sems = send_sems
+        self.recv_sems = recv_sems
+        self.index = names
+        self.count = 0
+        self.pending = []
+
+    def slot(self, name):
+        if name not in self.index:
+            self.index[name] = len(self.index)
+        return self.index[name]
+
+    def send(self, src, dst, name, device, cond=None, extra=None):
+        number = self.count
+        self.count += 1
+        at = self.slot(name)
+        if extra is not None:
+            at = at + extra
+        copy = pltpu.make_async_remote_copy(
+            src_ref=src,
+            dst_ref=dst,
+            send_sem=self.send_sems.at[number],
+            recv_sem=self.recv_sems.at[at],
+            device_id=device,
+            device_id_type=MESH,
+        )
+        if cond is None:
+            copy.start()
+        else:
+            pl.when(cond)(copy.start)
+        self.pending.append((copy, cond))
+
+    def take(self, dst, name, device, extra=None):
+        at = self.slot(name)
+        if extra is not None:
+            at = at + extra
+        pltpu.make_async_remote_copy(
+            src_ref=dst,
+            dst_ref=dst,
+            send_sem=self.send_sems.at[0],
+            recv_sem=self.recv_sems.at[at],
+            device_id=device,
+            device_id_type=MESH,
+        ).wait_recv()
+
+    def drain(self):
+        for copy, cond in self.pending:
+            if cond is None:
+                copy.wait_send()
+            else:
+                pl.when(cond)(copy.wait_send)
+        self.pending = []
+
+
+BELOW, ABOVE = 0, 1
+
+
+def both(first, second):
+    return second if first is None else jnp.logical_and(first, second)
+
+
+def source_valid(place, way, dist):
+    return place.z >= dist if way == BELOW else place.z + dist <= 3
+
+
+def source_pos(place, way, dist):
+    return place.dp - 2 * dist if way == BELOW else place.dp + 2 * dist
+
+
+def flood_start(wires, place, name, own, block, spread):
+    wires.send(own, block(place.dp), (name, BELOW, 1), place.up, place.has_up)
+    wires.send(own, block(place.dp), (name, ABOVE, 1), place.down, place.has_down)
+    wires.send(own, block(place.dp), (name, "y", 0, 0), place.across)
+    spread(own, place.dp, (0, 0, 0), None)
+
+
+def flood_step(wires, place, name, block, spread, way, dist):
+    here = source_valid(place, way, dist)
+    pos = source_pos(place, way, dist)
+    view = block(pos)
+    came_from = place.down if way == BELOW else place.up
+    pl.when(here)(lambda: wires.take(view, (name, way, dist), came_from))
+    if dist < 3:
+        onward = place.up if way == BELOW else place.down
+        more = place.has_up if way == BELOW else place.has_down
+        wires.send(view, view, (name, way, dist + 1), onward, jnp.logical_and(here, more))
+    wires.send(view, view, (name, "y", way, dist), place.across, here)
+    spread(view, pos, (0, way, dist), here)
+
+
+def flood_side(wires, place, name, block, spread, way, dist):
+    if dist == 0:
+        here, pos = None, place.dp
+    else:
+        here, pos = source_valid(place, way, dist), source_pos(place, way, dist)
+    pos = pos + 1 - 2 * place.y
+    view = block(pos)
+    if here is None:
+        wires.take(view, (name, "y", 0, 0), place.across)
+    else:
+        pl.when(here)(lambda: wires.take(view, (name, "y", way, dist), place.across))
+    spread(view, pos, (1, way, dist), here)
+
+
+HOPS = [(way, dist) for dist in (1, 2, 3) for way in (BELOW, ABOVE)]
+
+
+def no_spread(view, pos, key, cond):
+    return None
+
+
+def gather_kernel(
+    names,
+    qkv_ref, out_ref, gu_ref, downt_ref, gain_ref,
+    qkv_all, out_all, gu_all, downt_all, gain_all,
+    send_sems, recv_sems, local_sems,
+):
+    place = Place()
+    wires = Wires(send_sems, recv_sems, names)
+    rows = qkv_ref.shape[0]
+    units = gu_all.shape[2]
+    half = downt_ref.shape[1]
+    strip = downt_ref.shape[0]
+    dp, ctx = place.dp, place.ctx
+    greet(place)
+
+    def row_view(ref, lead, pos):
+        return ref.at[lead, pl.ds(pl.multiple_of(pos * rows, 16), rows)]
+
+    locals_ = []
+
+    def local(src, dst, cond=None):
+        copy = pltpu.make_async_copy(src, dst, local_sems.at[len(locals_)])
+        locals_.append((copy, cond))
+        if cond is None:
+            copy.start()
+        else:
+            pl.when(cond)(copy.start)
+
+    for part in range(2):
+        target = 2 * place.c + part
+        src = gu_ref.at[:, pl.ds(part * units, units)]
+        dst = row_view(gu_all, place.x, dp)
+        away = target != ctx
+        wires.send(src, dst, ("gu_mix", 0), (dp, target), away, extra=place.x)
+        local(src, dst, target == ctx)
+    wires.slot(("gu_mix", 1))
+
+    def attention_spread(name, ref):
+        def spread(view, pos, key, cond):
+            dst = row_view(ref, ctx, pos)
+            wires.send(view, dst, (name, "x") + key, place.chip, cond)
+            wires.send(view, dst, (name, "c") + key, place.core, cond)
+        return spread
+
+    attention = [("qkv", qkv_ref, qkv_all), ("out", out_ref, out_all)]
+    for name, own, ref in attention:
+        block = functools.partial(row_view, ref, ctx)
+        local(own, block(dp))
+        flood_start(wires, place, name, own, block, attention_spread(name, ref))
+    gain_block = lambda pos: gain_all.at[pos]
+    local(gain_ref, gain_block(dp))
+    flood_start(wires, place, "gain", gain_ref, gain_block, no_spread)
+
+    lanes = pl.ds(pl.multiple_of(place.y * half, 128), half)
+    other_lanes = pl.ds(pl.multiple_of((1 - place.y) * half, 128), half)
+    dst = downt_all.at[pl.ds(pl.multiple_of(ctx * strip, 16), strip), lanes]
+    wires.send(downt_ref, dst, ("down_mix", 0), (dp, place.z), ctx != place.z, extra=ctx)
+    for j in range(1, 4):
+        wires.slot(("down_mix", j))
+    local(downt_ref, dst, ctx == place.z)
+
+    def gu_view(part):
+        return functools.partial(row_view, gu_all, part)
+
+    for part in range(2):
+        remote = (part * 2 + place.x) != ctx
+        came_from = (dp, part * 2 + place.x)
+        view = gu_view(part)(dp)
+        pl.when(remote)(lambda: wires.take(view, ("gu_mix", part), came_from))
+    for copy, cond in locals_:
+        if cond is None:
+            copy.wait()
+        else:
+            pl.when(cond)(copy.wait)
+    for part in range(2):
+        flood_start(wires, place, ("gu", part), gu_view(part)(dp), gu_view(part), no_spread)
+
+    at_home = ctx == place.z
+    strips = [downt_all.at[pl.ds(j * strip, strip), lanes] for j in range(4)]
+    other_strips = [downt_all.at[pl.ds(j * strip, strip), other_lanes] for j in range(4)]
+
+    def take_strips():
+        for j in range(4):
+            pl.when(ctx != j)(
+                functools.partial(wires.take, strips[j], ("down_mix", j), (dp, j))
+            )
+
+    pl.when(at_home)(take_strips)
+    for j in range(4):
+        wires.send(strips[j], strips[j], ("down", j, BELOW, 1), place.up, jnp.logical_and(at_home, place.has_up))
+        wires.send(strips[j], strips[j], ("down", j, ABOVE, 1), place.down, jnp.logical_and(at_home, place.has_down))
+        wires.send(strips[j], strips[j], ("down_y", j), place.across, at_home)
+
+    def down_step(way, dist):
+        offset = place.z - ctx if way == BELOW else ctx - place.z
+        here = offset == dist
+        came_from = place.down if way == BELOW else place.up
+        onward = place.up if way == BELOW else place.down
+        more = place.has_up if way == BELOW else place.has_down
+        for j in range(4):
+            pl.when(here)(functools.partial(wires.take, strips[j], ("down", j, way, dist), came_from))
+            if dist < 3:
+                wires.send(strips[j], strips[j], ("down", j, way, dist + 1), onward, jnp.logical_and(here, more))
+            wires.send(strips[j], strips[j], ("down_y", j), place.across, here)
+
+    for way, dist in HOPS:
+        for name, own, ref in attention:
+            flood_step(wires, place, name, functools.partial(row_view, ref, ctx), attention_spread(name, ref), way, dist)
+        flood_step(wires, place, "gain", gain_block, no_spread, way, dist)
+        for part in range(2):
+            flood_step(wires, place, ("gu", part), gu_view(part), no_spread, way, dist)
+        down_step(way, dist)
+    for way, dist in [(0, 0)] + HOPS:
+        for name, own, ref in attention:
+            flood_side(wires, place, name, functools.partial(row_view, ref, ctx), attention_spread(name, ref), way, dist)
+        flood_side(wires, place, "gain", gain_block, no_spread, way, dist)
+
+    def positions():
+        for side in range(2):
+            for way, dist in [(0, 0)] + HOPS:
+                if dist == 0:
+                    here, pos = None, place.dp
+                else:
+                    here, pos = source_valid(place, way, dist), source_pos(place, way, dist)
+                if side == 1:
+                    pos = pos + 1 - 2 * place.y
+                yield (side, way, dist), here, pos
+
+    far = place.chip[1]
+    for name, own, ref in attention:
+        for key, here, pos in positions():
+            view = row_view(ref, far, pos)
+            def arrive():
+                wires.take(view, (name, "x") + key, place.chip)
+            if here is None:
+                arrive()
+            else:
+                pl.when(here)(arrive)
+            wires.send(view, view, (name, "d") + key, place.core, here)
+    for name, own, ref in attention:
+        for key, here, pos in positions():
+            for mark, lead in (("c", place.core[1]), ("d", 3 - ctx)):
+                view = row_view(ref, lead, pos)
+                def arrive():
+                    wires.take(view, (name, mark) + key, place.core)
+                if here is None:
+                    arrive()
+                else:
+                    pl.when(here)(arrive)
+    for part in range(2):
+        for way, dist in [(0, 0)] + HOPS:
+            flood_side(wires, place, ("gu", part), gu_view(part), no_spread, way, dist)
+    for j in range(4):
+        wires.take(other_strips[j], ("down_y", j), place.across)
+    wires.drain()
+
+
+def gather_weights(w_qkv, w_out, w_gate_up, down_t, gains):
+    dtype = w_qkv.dtype
+    rows = w_qkv.shape[0]
+    units = w_gate_up.shape[1] // 2
+    shapes = (
+        jax.ShapeDtypeStruct((4, 8 * rows, w_qkv.shape[1]), dtype),
+        jax.ShapeDtypeStruct((4, 8 * rows, w_out.shape[1]), dtype),
+        jax.ShapeDtypeStruct((2, 8 * rows, units), dtype),
+        jax.ShapeDtypeStruct((4 * down_t.shape[0], 2 * down_t.shape[1]), dtype),
+        jax.ShapeDtypeStruct((8,) + gains.shape, gains.dtype),
+    )
+    anywhere = pl.BlockSpec(memory_space=pltpu.MemorySpace.HBM)
+    return pl.pallas_call(
+        functools.partial(gather_kernel, {}),
+        out_shape=shapes,
+        in_specs=[anywhere] * 5,
+        out_specs=[anywhere] * 5,
+        scratch_shapes=[
+            pltpu.SemaphoreType.DMA((260,)),
+            pltpu.SemaphoreType.DMA((260,)),
+            pltpu.SemaphoreType.DMA((8,)),
+        ],
+        compiler_params=pltpu.CompilerParams(collective_id=0, has_side_effects=True),
+        name="gather_weights",
+    )(w_qkv, w_out, w_gate_up, down_t, gains)
+
+
+def add_rows(dst, srcs, out=None, cast=None, chunk=48):
+    out = dst if out is None else out
+    total_rows = dst.shape[0]
+    assert total_rows % chunk == 0
+
+    def body(i, carry):
+        at = pl.ds(pl.multiple_of(i * chunk, 16), chunk)
+        total = dst[at, :].astype(jnp.float32)
+        for src in srcs:
+            total = total + src[at, :].astype(jnp.float32)
+        out[at, :] = total.astype(out.dtype)
+        return carry
+
+    lax.fori_loop(0, total_rows // chunk, body, 0)
+
+
+def when(cond, action):
+    if cond is None:
+        action()
+    else:
+        pl.when(cond)(action)
+
+
+DRAIN = [(way, dist) for dist in (3, 2, 1, 0) for way in (BELOW, ABOVE)]
+
+
+def sink_step(wires, place, name, block, inbox, way, dist):
+    here = source_valid(place, way, dist)
+    pos = source_pos(place, way, dist)
+    view = block(pos)
+    fed = place.has_up if way == BELOW else place.has_down
+    feeder = place.up if way == BELOW else place.down
+    onward = place.down if way == BELOW else place.up
+    if dist < 3:
+
+        def arrive():
+            wires.take(inbox.at[way, dist], (name, way, dist), feeder)
+            add_rows(view, [inbox.at[way, dist]])
+
+        pl.when(jnp.logical_and(here, fed))(arrive)
+    if dist > 0:
+        wires.send(view, inbox.at[way, dist - 1], (name, way, dist - 1), onward, here)
+
+
+def scatter_kernel(
+    names,
+    qkv_in, out_in, gu_in, downt_in, gain_in,
+    qkv_out, out_out, gu_out, downt_out, gain_out,
+    qkv, out, gu, downt,
+    qkv_core, out_core, qkv_chip, out_chip, qkv_side, out_side, gu_side, down_side,
+    qkv_inbox, out_inbox, gu_inbox, down_inbox, gu_mix, down_mix, gain_box,
+    send_sems, recv_sems, local_sems,
+):
+    place = Place()
+    wires = Wires(send_sems, recv_sems, names)
+    dp, ctx, z, y = place.dp, place.ctx, place.z, place.y
+    rows = qkv_out.shape[0]
+    units = gu.shape[2]
+    strip, half = downt_out.shape
+    loads = []
+    for src, dst in ((gu_in, gu), (downt_in, downt), (out_in, out), (qkv_in, qkv)):
+        copy = pltpu.make_async_copy(src, dst, local_sems.at[len(loads)])
+        copy.start()
+        loads.append(copy)
+    greet(place)
+
+    def row_view(ref, lead, pos):
+        return ref.at[lead, pl.ds(pl.multiple_of(pos * rows, 16), rows)]
+
+    lanes = pl.ds(pl.multiple_of(y * half, 128), half)
+    other_lanes = pl.ds(pl.multiple_of((1 - y) * half, 128), half)
+    strips = [downt.at[pl.ds(j * strip, strip), lanes] for j in range(4)]
+    other_strips = [downt.at[pl.ds(j * strip, strip), other_lanes] for j in range(4)]
+    loads[0].wait()
+    for zs in range(4):
+        for part in range(2):
+            wires.send(row_view(gu, part, 2 * zs + 1 - y), gu_side.at[part, zs], ("gu_y", part, zs), place.across)
+    loads[1].wait()
+    for j in range(4):
+        wires.send(other_strips[j], down_side.at[j], ("down_y", j), place.across)
+    attention = [
+        ("out", out, out_core, out_chip, out_side, out_inbox, out_out),
+        ("qkv", qkv, qkv_core, qkv_chip, qkv_side, qkv_inbox, qkv_out),
+    ]
+    pair = 2 * rows
+
+    def pair_view(ref, lead, zs):
+        return ref.at[lead, pl.ds(zs * pair, pair)]
+
+    for number, (name, ref, core, chip, side, inbox, final) in enumerate(attention):
+        loads[2 + number].wait()
+        for zs in range(4):
+            for xx in range(2):
+                wires.send(
+                    pair_view(ref, 2 * xx + 1 - place.c, zs), pair_view(core, xx, zs),
+                    (name, "c", xx, zs), place.core,
+                )
+    for name, ref, core, chip, side, inbox, final in attention:
+        far = place.chip[1]
+        for zs in range(4):
+            for xx in range(2):
+                wires.take(pair_view(core, xx, zs), (name, "c", xx, zs), place.core)
+                add_rows(pair_view(ref, 2 * xx + place.c, zs), [pair_view(core, xx, zs)])
+            wires.send(pair_view(ref, far, zs), chip.at[pl.ds(zs * pair, pair)], (name, "x", zs), place.chip)
+    for zs in range(4):
+        for part in range(2):
+            wires.take(gu_side.at[part, zs], ("gu_y", part, zs), place.across)
+            add_rows(row_view(gu, part, 2 * zs + y), [gu_side.at[part, zs]])
+    for j in range(4):
+        wires.take(down_side.at[j], ("down_y", j), place.across)
+        add_rows(strips[j], [down_side.at[j]])
+    for name, ref, core, chip, side, inbox, final in attention:
+        for zs in range(4):
+            span = chip.at[pl.ds(zs * pair, pair)]
+            wires.take(span, (name, "x", zs), place.chip)
+            add_rows(pair_view(ref, ctx, zs), [span])
+            wires.send(row_view(ref, ctx, 2 * zs + 1 - y), side.at[zs], (name, "y", zs), place.across)
+
+    def down_step(dist):
+        for way in (BELOW, ABOVE):
+            offset = z - ctx if way == BELOW else ctx - z
+            here = offset == dist
+            fed = place.has_up if way == BELOW else place.has_down
+            feeder = place.up if way == BELOW else place.down
+            onward = place.down if way == BELOW else place.up
+            for j in range(4):
+                def arrive():
+                    wires.take(down_inbox.at[way, j], ("down", j, way), feeder)
+                    add_rows(strips[j], [down_inbox.at[way, j]])
+                pl.when(jnp.logical_and(here, fed))(arrive)
+                if dist > 0:
+                    wires.send(strips[j], down_inbox.at[way, j], ("down", j, way), onward, here)
+
+    for way, dist in DRAIN:
+        for part in range(2):
+            sink_step(wires, place, ("gu", part), functools.partial(row_view, gu, part), gu_inbox.at[part], way, dist)
+        if way == BELOW:
+            down_step(dist)
+    for part in range(2):
+        target = part * 2 + place.x
+        block = row_view(gu, part, dp)
+        wires.send(block, gu_mix.at[place.c], ("gu_mix", 0), (dp, target), target != ctx, extra=place.c)
+
+        def keep():
+            add_rows(block, [], out=gu_mix.at[place.c])
+
+        pl.when(target == ctx)(keep)
+    wires.slot(("gu_mix", 1))
+    for j in range(4):
+        here = ctx == z
+        wires.send(strips[j], down_mix, ("down_mix",), (dp, j), jnp.logical_and(here, ctx != j))
+        pl.when(jnp.logical_and(here, ctx == j))(functools.partial(add_rows, strips[j], [], down_mix))
+    for name, ref, core, chip, side, inbox, final in attention:
+        for zs in range(4):
+            wires.take(side.at[zs], (name, "y", zs), place.across)
+            add_rows(row_view(ref, ctx, 2 * zs + y), [side.at[zs]])
+        for way, dist in DRAIN:
+            sink_step(wires, place, name, functools.partial(row_view, ref, ctx), inbox, way, dist)
+        add_rows(row_view(ref, ctx, dp), [], out=final)
+
+    gain_out[...] = gain_in[...]
+
+    def swap(slot, device, cond=None):
+        wires.send(gain_out, gain_box.at[slot], ("gain", slot), device, cond)
+
+    def add_gain(slot, device):
+        wires.take(gain_box.at[slot], ("gain", slot), device)
+        gain_out[...] = gain_out[...] + gain_box[slot]
+
+    def settle():
+        copy, cond = wires.pending.pop()
+        when(cond, copy.wait_send)
+
+    for slot, device in enumerate((place.core, place.chip, place.across)):
+        swap(slot, device)
+        settle()
+        add_gain(slot, device)
+    low_end, high_end = z == 0, z == 3
+    mid_low, mid_high = z == 1, z == 2
+    swap(3, place.up, low_end)
+    settle()
+    swap(3, place.down, high_end)
+    settle()
+    pl.when(mid_low)(lambda: add_gain(3, place.down))
+    pl.when(mid_high)(lambda: add_gain(3, place.up))
+    swap(4, place.up, mid_low)
+    settle()
+    swap(4, place.down, mid_high)
+    settle()
+    pl.when(mid_low)(lambda: add_gain(4, place.up))
+    pl.when(mid_high)(lambda: add_gain(4, place.down))
+    swap(5, place.down, mid_low)
+    swap(5, place.up, mid_high)
+
+    def last(device):
+        wires.take(gain_box.at[5], ("gain", 5), device)
+        gain_out[...] = gain_box[5]
+
+    pl.when(low_end)(lambda: last(place.up))
+    pl.when(high_end)(lambda: last(place.down))
+
+    for part in range(2):
+        source = 2 * place.c + part
+        pl.when(source != ctx)(
+            lambda: wires.take(gu_mix.at[part], ("gu_mix", part), (dp, source))
+        )
+        add_rows(gu_mix.at[part], [], out=gu_out.at[:, pl.ds(part * units, units)])
+    pl.when(ctx != z)(lambda: wires.take(down_mix, ("down_mix",), (dp, z)))
+    add_rows(down_mix, [], out=downt_out)
+    wires.drain()
+
+
+def scatter_grads(qkv, out, gu, downt, gains):
+    rows = qkv.shape[1] // 8
+    qkv_cols, out_cols, units = qkv.shape[2], out.shape[2], gu.shape[2]
+    strip, half = downt.shape[0] // 4, downt.shape[1] // 2
+    f32, low = jnp.float32, qkv.dtype
+    shapes = (
+        jax.ShapeDtypeStruct((rows, qkv_cols), f32),
+        jax.ShapeDtypeStruct((rows, out_cols), f32),
+        jax.ShapeDtypeStruct((rows, 2 * units), f32),
+        jax.ShapeDtypeStruct((strip, half), f32),
+        jax.ShapeDtypeStruct(gains.shape, f32),
+    )
+    anywhere = pl.BlockSpec(memory_space=pltpu.MemorySpace.HBM)
+    vmem = pl.BlockSpec(memory_space=pltpu.MemorySpace.VMEM)
+
+    def box(*shape, dtype=low):
+        return pltpu.VMEM(shape, dtype)
+
+    scratch = [
+        box(*qkv.shape), box(*out.shape), box(*gu.shape), box(*downt.shape),
+        box(2, 8 * rows, qkv_cols), box(2, 8 * rows, out_cols),
+        box(8 * rows, qkv_cols), box(8 * rows, out_cols),
+        box(4, rows, qkv_cols), box(4, rows, out_cols),
+        box(2, 4, rows, units), box(4, strip, half),
+        box(2, 3, rows, qkv_cols), box(2, 3, rows, out_cols),
+        box(2, 2, 3, rows, units), box(2, 4, strip, half),
+        box(2, rows, units), box(strip, half),
+        box(6, *gains.shape, dtype=f32),
+        pltpu.SemaphoreType.DMA((200,)),
+        pltpu.SemaphoreType.DMA((200,)),
+        pltpu.SemaphoreType.DMA((4,)),
+    ]
+    return pl.pallas_call(
+        functools.partial(scatter_kernel, {}),
+        out_shape=shapes,
+        in_specs=[anywhere] * 4 + [vmem],
+        out_specs=[vmem] * 5,
+        scratch_shapes=scratch,
+        compiler_params=pltpu.CompilerParams(
+            collective_id=1, has_side_effects=True, vmem_limit_bytes=60 * 2**20
+        ),
+        name="scatter_grads",
+    )(qkv, out, gu, downt, gains)
+
+
+def split_columns(values_in, parts):
+    return jnp.concatenate([values_in[j] for j in range(parts)], axis=-1)
+
+
+def on_device_fast(tokens, lengths, gain_one, w_qkv, w_out, gain_two, w_gate_up, w_down, cotangent):
+    seq_count, row_count, width = tokens.shape
+    rows = seq_count * row_count
+    f32, low = jnp.float32, jnp.bfloat16
+    block = gain_one.shape[0]
+    gains = jnp.zeros((8, 256), f32)
+    gains = gains.at[0, :block].set(gain_one.astype(f32)).at[1, :block].set(gain_two.astype(f32))
+    qkv_all, out_all, gu_all, down_t, gain_all = gather_weights(
+        w_qkv, w_out, w_gate_up, w_down.T, gains
+    )
+    gain_a = gain_all[:, 0, :block].reshape(-1)
+    gain_b = gain_all[:, 1, :block].reshape(-1)
+    query_cols, key_cols = QH * HD, KVH * HD
+    group = QH // KVH
+    scale = 1.0 / math.sqrt(HD)
+    position = lax.axis_index("ctx") * row_count + jnp.arange(row_count, dtype=jnp.int32)
+    valid_rows = position[None, :] < lengths[:, None]
+    cosine, sine_table = angles(position, HD)
+    cosine, sine_table = cosine[:, None, :], sine_table[:, None, :]
+    grad_rows = jnp.where(valid_rows[..., None], cotangent, jnp.zeros_like(cotangent))
+    grad_all = lax.all_gather(grad_rows, "ctx").reshape(-1, width)
+    source = tokens.astype(f32).reshape(rows, width)
+    inverse_one = lax.rsqrt(jnp.mean(source * source, axis=-1, keepdims=True) + EPS)
+    normed_one = (source * inverse_one * gain_a).astype(low)
+    projected = split_columns(
+        jnp.einsum("rd,jde->jre", normed_one, qkv_all, preferred_element_type=f32), 4
+    ).reshape(seq_count, row_count, -1)
+    queries = rotate(
+        projected[..., :query_cols].reshape(seq_count, row_count, QH, HD), cosine, sine_table
+    ).astype(low)
+    keys = rotate(
+        projected[..., query_cols : query_cols + key_cols].reshape(seq_count, row_count, KVH, HD),
+        cosine, sine_table,
+    ).astype(low)
+    values = projected[..., query_cols + key_cols :].astype(low).reshape(seq_count, row_count, KVH, HD)
+    both_all = lax.all_gather(jnp.stack([keys, values]), "ctx", axis=2, tiled=True)
+    keys_all = both_all[0].transpose(0, 2, 1, 3)
+    values_all = both_all[1].transpose(0, 2, 1, 3)
+    slots = keys_all.shape[2]
+    query_blocks = (
+        queries.reshape(seq_count, row_count, KVH, group, HD)
+        .transpose(0, 2, 3, 1, 4)
+        .reshape(seq_count, KVH, group * row_count, HD)
+    )
+    keyidx = jnp.arange(slots, dtype=jnp.int32)
+    allowed = (keyidx[None, None, :] <= position[None, :, None]) & (
+        keyidx[None, None, :] < lengths[:, None, None]
+    )
+    allowed = jnp.broadcast_to(
+        allowed[:, None, None], (seq_count, 1, group, row_count, slots)
+    ).reshape(seq_count, 1, group * row_count, slots)
+    scores = jnp.einsum("bksd,bktd->bkst", query_blocks, keys_all, preferred_element_type=f32) * scale
+    scores = jnp.where(allowed, scores, NEGATIVE)
+    row_max = jnp.max(scores, axis=-1, keepdims=True)
+    terms = jnp.exp(scores - row_max)
+    probs = terms / jnp.sum(terms, axis=-1, keepdims=True)
+    probs_low = probs.astype(low)
+    attended = jnp.einsum("bkst,bktd->bksd", probs_low, values_all, preferred_element_type=f32)
+
+    def join(blocks):
+        return (
+            blocks.reshape(seq_count, KVH, group, row_count, HD)
+            .transpose(0, 3, 1, 2, 4)
+            .reshape(rows, query_cols)
+        )
+
+    context = join(attended.astype(low))
+    hidden = source + split_columns(
+        jnp.einsum("re,jed->jrd", context, out_all, preferred_element_type=f32), 4
+    )
+    inverse_two = lax.rsqrt(jnp.mean(hidden * hidden, axis=-1, keepdims=True) + EPS)
+    normed_two = (hidden * inverse_two * gain_b).astype(low)
+    normed_all = lax.all_gather(normed_two, "ctx").reshape(-1, width)
+    gate = jnp.dot(normed_all, gu_all[0], preferred_element_type=f32)
+    up = jnp.dot(normed_all, gu_all[1], preferred_element_type=f32)
+    gate_sig = jax.nn.sigmoid(gate)
+    swish = gate * gate_sig
+    activation = (swish * up).astype(low)
+    partial = jnp.einsum("rf,df->rd", activation, down_t, preferred_element_type=f32)
+    branch = lax.psum_scatter(
+        partial.astype(low).reshape(4, rows, width), "ctx", scatter_dimension=0, tiled=False
+    )
+    result = hidden + branch.astype(f32)
+    output = jnp.where(
+        valid_rows[..., None], result.reshape(seq_count, row_count, width), 0.0
+    ).astype(low)
+    grad_act = jnp.dot(grad_all, down_t, preferred_element_type=f32)
+    grad_gate = (grad_act * up * gate_sig * (1.0 + gate * (1.0 - gate_sig))).astype(low)
+    grad_up = (grad_act * swish).astype(low)
+    grad_normed = jnp.einsum("rf,df->rd", grad_gate, gu_all[0], preferred_element_type=f32)
+    grad_normed = grad_normed + jnp.einsum("rf,df->rd", grad_up, gu_all[1], preferred_element_type=f32)
+    grad_down_t = jnp.einsum("rd,rf->df", grad_all, activation, preferred_element_type=f32).astype(low)
+    grad_gu = jnp.stack(
+        [
+            jnp.einsum("rd,rf->df", normed_all, grad_gate, preferred_element_type=f32),
+            jnp.einsum("rd,rf->df", normed_all, grad_up, preferred_element_type=f32),
+        ]
+    ).astype(low)
+    grad_normed_two = lax.psum_scatter(
+        grad_normed.astype(low).reshape(4, rows, width), "ctx", scatter_dimension=0, tiled=False
+    ).astype(f32)
+    flat_grad = grad_rows.astype(f32).reshape(rows, width)
+
+    def norm_rows(source_in, inverse, gain, grad_in):
+        scaled = grad_in * gain
+        mean_term = jnp.mean(scaled * source_in, axis=-1, keepdims=True)
+        back = inverse * scaled - source_in * (inverse * inverse * inverse) * mean_term
+        return back, jnp.sum(grad_in * source_in * inverse, axis=0)
+
+    back_two, grad_gain_two = norm_rows(hidden, inverse_two, gain_b, grad_normed_two)
+    grad_hidden = flat_grad + back_two
+    grad_branch = grad_hidden.astype(low)
+    wide = grad_branch.reshape(rows, 4, -1)
+    grad_out = jnp.einsum("re,rjd->jed", context, wide, preferred_element_type=f32).astype(low)
+    grad_context = jnp.einsum("rjd,jed->re", wide, out_all, preferred_element_type=f32).astype(low)
+    grad_blocks = (
+        grad_context.reshape(seq_count, row_count, KVH, group, HD)
+        .transpose(0, 2, 3, 1, 4)
+        .reshape(seq_count, KVH, group * row_count, HD)
+    )
+    grad_probs = jnp.einsum("bksd,bktd->bkst", grad_blocks, values_all, preferred_element_type=f32)
+    delta = jnp.sum(probs * grad_probs, axis=-1, keepdims=True)
+    grad_scores = (probs * (grad_probs - delta)).astype(low)
+    grad_values = jnp.einsum("bkst,bksd->bktd", probs_low, grad_blocks, preferred_element_type=f32)
+    grad_keys = jnp.einsum("bkst,bksd->bktd", grad_scores, query_blocks, preferred_element_type=f32) * scale
+    grad_queries = jnp.einsum("bkst,bktd->bksd", grad_scores, keys_all, preferred_element_type=f32) * scale
+    sums = lax.psum_scatter(
+        jnp.stack([grad_keys, grad_values]).astype(low).transpose(3, 0, 1, 2, 4),
+        "ctx", scatter_dimension=0, tiled=True,
+    ).astype(f32)
+    sums = sums.transpose(1, 2, 0, 3, 4)
+    turned_queries = rotate(
+        join(grad_queries).reshape(seq_count, row_count, QH, HD), cosine, -sine_table
+    )
+    turned_keys = rotate(sums[0], cosine, -sine_table)
+    grad_mixed = jnp.concatenate(
+        [
+            turned_queries.reshape(rows, query_cols),
+            turned_keys.reshape(rows, key_cols),
+            sums[1].reshape(rows, key_cols),
+        ],
+        axis=-1,
+    ).astype(low).reshape(rows, 4, -1)
+    grad_qkv = jnp.einsum("rd,rje->jde", normed_one, grad_mixed, preferred_element_type=f32).astype(low)
+    grad_normed_one = jnp.einsum("rje,jde->rd", grad_mixed, qkv_all, preferred_element_type=f32)
+    back_one, grad_gain_one = norm_rows(source, inverse_one, gain_a, grad_normed_one)
+    grad_tokens = (grad_hidden + back_one).astype(low).reshape(tokens.shape)
+    gain_rows = jnp.zeros((8, width), f32).at[0].set(grad_gain_one).at[1].set(grad_gain_two)
+    final_qkv, final_out, final_gu, final_down, gain_sums = scatter_grads(
+        grad_qkv, grad_out, grad_gu, grad_down_t, gain_rows
+    )
+    mine = lax.dynamic_slice(gain_sums, (0, lax.axis_index("dp") * block), (8, block))
+    return (output, grad_tokens, mine[0], final_qkv, final_out, mine[1], final_gu, final_down.T)
+
+
 def solution(mesh):
+    fits = mesh.shape["dp"] == 8 and mesh.shape["ctx"] == 4
     return jax.shard_map(
-        on_device,
+        on_device_fast if fits else on_device,
         mesh=mesh,
         in_specs=(
             P("dp", "ctx", None),

time: 1040 us -> 516 us (0.50)
  waiting for transfers between devices: 614 us -> 38.3 us
  Pallas kernels: 0 us -> 263 us
  blocking collectives: 143 us -> 13.4 us
  matrix products: 97.4 us -> 62.2 us
  local copies, waits for them, and re-layouts: 116 us -> 86.7 us
    all_gather x9 -> x2, waiting for transfers between devices: 375 us -> 24.3 us  [the longest x1 13 us: on_device_fast(): grad_all = lax.all_gather(grad_rows, 'ctx').reshape(-1, width)]
    pallas_call x0 -> x2, Pallas kernels: none -> 263 us  [the longest x1 157 us: scatter_grads(): pl.pallas_call(functools.partial(scatter_kernel, {}), out_shape=shapes, i...]
    reduce_scatter x4 -> x2, waiting for transfers between devices: 149 us -> 0.04 us  [the longest x1 0.02 us: on_device_fast(): lax.psum_scatter(partial.astype(low).reshape(4, rows, width), 'ctx', scat...]
    unnamed x17 -> x6, waiting for transfers between devices: 90.3 us -> 13.9 us
    all_to_all x3 -> x0, blocking collectives: 48.5 us -> none  [the longest x1 23.3 us: on_device(): lax.all_to_all(grad_mix, 'ctx', split_axis=2, concat_axis=1, tiled=True)]
    unnamed x2 -> x0, blocking collectives: 43.5 us -> none
    dot_general x96 -> x20, matrix products: 97.4 us -> 59.3 us  [the longest x1 6.54 us: on_device_fast(): jnp.einsum('bkst,bksd->bktd', probs_low, grad_blocks, preferred_element_t...]
    dynamic_slice x48 -> x0, local copies, waits for them, and re-layouts: 31.6 us -> none  [the longest x36 23.6 us: on_device(): lax.map(forward_block, (query_blocks, key_blocks, value_blocks, pair_leng...]
  transfers between devices with their start and end apart: 16 -> 5, of which waited for: 12 -> 3; matrix products, arithmetic and copies ran while one was open for 13% -> 15% of each run, Pallas kernels for 0% -> 0%
where the time goes in v1:
time: 516 us; the launch traced here: 509 us
  Pallas kernels  263 us (51%)
  local copies, waits for them, and re-layouts  86.7 us (17%)
  matrix products  62.2 us (12%)
  waiting for transfers between devices  38.3 us (7%)
  other arithmetic  29.9 us (6%)
  between operations  15.4 us (3%)
  blocking collectives  13.4 us (3%)
    pallas_call x1, Pallas kernels, scatter_grads(): pl.pallas_call(functools.partial(scatter_kernel, {}), out_shape=shapes, i...  157 us
    pallas_call x1, Pallas kernels, gather_weights(): pl.pallas_call(functools.partial(gather_kernel, {}), out_shape=shapes, in...  106 us
    unnamed x140, local copies, waits for them, and re-layouts  14.9 us
    unnamed x6, waiting for transfers between devices  13.9 us
    all_gather x1, blocking collectives, on_device_fast(): lax.all_gather(jnp.stack([keys, values]), 'ctx', axis=2, tiled=True)  13.4 us
    all_gather x1, waiting for transfers between devices, on_device_fast(): grad_all = lax.all_gather(grad_rows, 'ctx').reshape(-1, width)  13 us
    all_gather x1, waiting for transfers between devices, on_device_fast(): normed_all = lax.all_gather(normed_two, 'ctx').reshape(-1, width)  11.3 us
  transfers between devices with their start and end apart: 5, of which 3 were waited for; matrix products, arithmetic and copies ran while one was open for 15% of the time, Pallas kernels for 0%

profile of v1, /device:TPU:0, one launch (start us, length us, event | category | flops | bytes accessed | tf_op | source)
XLA Modules:
  0.0 509.3 jit_solution(10615560390544239107)
XLA Ops:
  8.2 1.3 multiply_reduce_fusion.5
  11.6 105.7 %gather_weights.1 = (bf16[4,1152,480]{2,1,0:T(8,128)(2,1)}, bf16[4,1152,288]{2,1,0:T(8,128)(2,1)}, bf16[2,1152,768]{2,1,0:T(8,128)(2,1)}, bf16[1152,768]{1,0:T(8,128)(2,1)}, f32[8,8,256]{2,1,0:T(8,128)}) custom-call(bf16[144,480]{1,0:T(8,128)(2,1)} %qkv_ref.1, bf16[144,288]{1,0:T(8,128)(2,1)} %out_ref.1, bf16[144,1536]{1,0:T(8,128)(2,1)} %gu_ref.1, ...), custom_call_target="tpu_custom_call" | custom-call | tf_op jit(solution)/shard_map/gather_weights/pallas_call | solution.py:627
  117.3 1.6 slice_reduce_fusion
  119.9 4.0 convolution_bitcast_fusion.2
  127.1 13.4 %all_gather.13 = bf16[2,2,256,6,64]{4,1,3,0,2:T(2,128)(2,1)S(1)} all-gather(bf16[2,2,64,6,64]{4,1,3,0,2:T(2,128)(2,1)S(1)} %copy.277), channel_id=1, replica_groups=mesh['dp'=8,'ctx'=4] {'ctx'}, dimensions={2}, use_global_device_ids=true | all-gather | bytes 983040 | tf_op jit(solution)/shard_map/all_gather | solution.py:938
  140.4 2.0 fusion.73
  144.2 1.4 subtract_convert_fusion
  148.7 1.8 copy.347
  150.6 2.9 fusion.78
  153.5 6.4 %convolution_convert_fusion.7 = bf16[2,6,192,64]{2,3,1,0:T(8,128)(2,1)} fusion(bf16[1,2,256,6,64]{2,4,3,1,0:T(8,128)(2,1)} %copy.347, f32[2,6,192]{2,1,0:T(8,128)} %get-tuple-element.135, pred[2,192,256]{2,1,0:T(8,128)(4,1)} %bitcast.235, bf16[2,6,192,64]{3,2,1,0:T(8,128)(2,1)} %bitcast.206, bf16[1,2,256,6,64]{2,4,3,1,0:T(8,128)(2,1)} %copy-done.16), kind=kOutput, calls=%fused_computation.51 | convolution fusion | flops 154094080 | bytes 1483776 | tf_op jit(solution)/shard_map/bkst,bktd->bksd/dot_general | solution.py:960
  159.9 2.0 copy.281
  161.9 2.1 copy.282
  164.0 2.1 reshape.678
  166.1 2.1 convolution_bitcast_fusion.3
  168.2 1.3 slice_bitcast_fusion.7
  169.4 1.7 copy.285
  171.2 1.7 copy.286
  172.9 1.7 copy.287
  174.6 1.7 copy.288
  176.3 2.3 concatenate.110
  178.6 1.3 multiply_reduce_fusion.4
  181.9 2.1 copy.289
  184.0 2.2 fusion.28
  186.2 1.8 copy.290
  189.4 2.0 fusion.72
  191.7 11.3 %all-gather.4.cloned.1.call-done = bf16[4,128,1152]{2,1,0:T(8,128)(2,1)} async-done(((bf16[1,128,1152]{2,1,0:T(8,128)(2,1)}), bf16[4,128,1152]{2,1,0:T(8,128)(2,1)}) %all-gather.4.cloned.1.call-update) | async-done | bytes 1179664 | tf_op jit(solution)/shard_map/all_gather | solution.py:975
  203.0 4.3 fusion.7
  207.3 2.3 fusion.11
  209.7 13.0 %all-gather.6.cloned.1.call-done = bf16[8,64,1152]{2,1,0:T(8,128)(2,1)} async-done(((bf16[2,64,1152]{2,1,0:T(8,128)(2,1)}), bf16[8,64,1152]{2,1,0:T(8,128)(2,1)}) %all-gather.6.cloned.1.call-update) | async-done | bytes 1179664 | tf_op jit(solution)/shard_map/all_gather | solution.py:923
  222.6 5.4 %multiply_convert_fusion.1 = (bf16[512,768]{1,0:T(8,128)(2,1)S(1)}, bf16[512,768]{1,0:T(8,128)(2,1)S(1)}, bf16[512,768]{1,0:T(8,128)(2,1)}) fusion(f32[512,768]{1,0:T(8,128)} %fusion.11, f32[512,768]{1,0:T(8,128)} %fusion.7, bf16[512,1152]{1,0:T(8,128)(2,1)} %bitcast.244, bf16[1152,768]{1,0:T(8,128)(2,1)} %get-tuple-element.70), kind=kOutput, calls=%fused_computation.34 | convolution fusion | flops 911867904 | bytes 8454144 | tf_op jit(solution)/shard_map/dot_general | solution.py:989
  229.3 2.2 fusion.3
  231.5 2.4 copy.291
  234.0 2.4 reshape.685
  236.3 1.4 mul.467
  237.7 2.4 reshape.686
  240.1 2.2 copy.295
  242.3 2.3 copy.294
  244.6 2.0 pad_maximum_fusion.3
  246.6 2.2 copy.316
  248.8 2.3 concatenate.121
  251.1 2.1 copy.293
  255.7 2.8 fusion.1
  260.1 2.2 convolution_convert_fusion.5
  262.4 2.4 convolution_convert_fusion.2.downt_in
  264.7 2.2 pad_maximum_fusion.gu_in
  267.2 2.3 fusion.32
  270.1 1.3 div.40
  272.4 3.6 fusion.4
  276.0 1.3 copy.297
  278.1 2.1 multiply_reduce_fusion
  282.1 6.5 %fusion.22 = bf16[1,2,6,256,64]{3,4,2,1,0:T(8,128)(2,1)} fusion(bf16[2,6,192,64]{3,2,1,0:T(8,128)(2,1)} %bitcast.229, f32[2,6,192]{2,1,0:T(8,128)} %get-tuple-element.135, pred[2,192,256]{2,1,0:T(8,128)(4,1)} %bitcast.236, bf16[2,6,192,64]{3,2,1,0:T(8,128)(2,1)} %bitcast.207, bf16[1,2,256,6,64]{2,4,3,1,0:T(8,128)(2,1)S(1)} %copy-done.17), kind=kOutput, calls=%fused_computation.53 | convolution fusion | flops 154143232 | bytes 1483776 | tf_op jit(solution)/shard_map/bkst,bksd->bktd/dot_general | solution.py:1026
  291.7 1.5 fusion.13
  296.0 2.1 add_convert_fusion.1
  298.1 2.1 convert_element_type.173
  300.2 1.9 convolution_convert_fusion.1
  302.1 3.2 copy.319
  305.3 13.8 %reduce-scatter.10.cloned.1.call-done = bf16[64,1536]{1,0:T(8,128)(2,1)} async-done(((bf16[256,1536]{1,0:T(8,128)(2,1)}), bf16[64,1536]{1,0:T(8,128)(2,1)}) %reduce-scatter.10.cloned.1.call-update) | async-done | bytes 196624
  322.0 4.5 multiply_reduce_fusion.1
  326.5 3.4 convolution_convert_fusion
  329.9 6.6 %copy.314 = bf16[4,480,1152]{1,2,0:T(8,128)(2,1)} copy(bf16[4,480,1152]{2,1,0:T(8,128)(2,1)} %convolution_convert_fusion) | data formatting | bytes 8847360 | tf_op jit(solution)/shard_map/convert_element_type | solution.py:1046
  337.3 157.1 %scatter_grads.1 = (f32[144,480]{1,0:T(8,128)}, f32[144,288]{1,0:T(8,128)}, f32[144,1536]{1,0:T(8,128)}, f32[288,384]{1,0:T(8,128)}, f32[8,1152]{1,0:T(8,128)}) custom-call(bf16[4,1152,480]{2,1,0:T(8,128)(2,1)} %bitcast.195, bf16[4,1152,288]{2,1,0:T(8,128)(2,1)} %bitcast.196, bf16[2,1152,768]{2,1,0:T(8,128)(2,1)} %pad_maximum_fusion.gu_in, ...), custom_call_target="tpu_custom_call" | custom-call | tf_op jit(solution)/shard_map/scatter_grads/pallas_call | solution.py:886
  495.9 1.4 fusion.77
  497.3 1.7 copy.382
  499.0 1.6 copy.383
  (226 shorter events, 37.6 us)
Async XLA Ops:
  7.2 195.8 %all-gather.4.cloned.1.call-start = ((), (), s32[]{:S(2)}) async-start(), calls=%async_computation.3 | async-start | bytes 1474560 | tf_op jit(solution)/shard_map/all_gather | solution.py:975
  8.2 115.7 %copy-start.4 = (f32[2,64,1152]{2,1,0:T(8,128)}, f32[2,64,1152]{2,1,0:T(8,128)S(1)}, u32[]{:S(2)}) copy-start(f32[2,64,1152]{2,1,0:T(8,128)S(1)} %convert_element_type.141) | copy-start | bytes 1769476
  119.1 4.8 copy-start.1
  124.8 23.7 %copy-start.54 = (s32[64]{0:T(128)}, s32[64]{0:T(128)S(1)}, u32[]{:S(2)}) copy-start(s32[64]{0:T(128)S(1)} %get-tuple-element.140) | copy-start | bytes 772
  125.9 1.2 copy-start.33
  143.2 7.4 %copy-start.16 = (bf16[1,2,256,6,64]{2,4,3,1,0:T(8,128)(2,1)}, bf16[1,2,256,6,64]{2,4,3,1,0:T(8,128)(2,1)S(1)}, u32[]{:S(2)}) copy-start(bf16[1,2,256,6,64]{2,4,3,1,0:T(8,128)(2,1)S(1)} %copy.346) | copy-start | bytes 1179652
  146.7 2.0 copy-start.61
  146.7 2.1 copy-start.8
  148.5 4.9 copy-start.10
  150.6 2.9 copy-start.35
  153.5 12.6 %copy-start = (bf16[4,1152,288]{2,1,0:T(8,128)(2,1)S(1)}, bf16[4,1152,288]{2,1,0:T(8,128)(2,1)}, u32[]{:S(2)}) copy-start(bf16[4,1152,288]{2,1,0:T(8,128)(2,1)} %get-tuple-element.66) | copy-start | bytes 7962628
  188.0 34.6 %all-gather.6.cloned.1.call-start = ((), (), s32[]{:S(2)}) async-start(), calls=%async_computation.6 | async-start | bytes 1474560 | tf_op jit(solution)/shard_map/all_gather | solution.py:923
  191.4 75.8 %reduce-scatter.8.cloned.1.call-start = ((), (), s32[]{:S(2)}) async-start(), calls=%async_computation.5 | async-start | bytes 1474560 | tf_op jit(solution)/shard_map/reduce_scatter | solution.py:1001
  203.0 4.3 copy-start.55
  203.0 4.3 copy-start.58
  222.6 5.4 %copy-start.56 = (bf16[2,1152,768]{2,1,0:T(8,128)(2,1)S(1)}, bf16[2,1152,768]{2,1,0:T(8,128)(2,1)}, u32[]{:S(2)}) copy-start(bf16[2,1152,768]{2,1,0:T(8,128)(2,1)} %get-tuple-element.69) | copy-start | bytes 10616836
  228.0 1.2 copy-start.64
  228.0 1.2 copy-start.62
  233.9 62.0 %reduce-scatter.6.cloned.1.call-start = ((), (), s32[]{:S(2)}) async-start(), calls=%async_computation.4 | async-start | bytes 1474560 | tf_op jit(solution)/shard_map/reduce_scatter | solution.py:982
  255.7 2.8 copy-start.59
  255.7 2.8 copy-start.63
  258.5 1.5 copy-start.57
  258.5 1.7 copy-start.65
  260.1 2.2 copy-start.60
  266.9 52.2 %reduce-scatter.10.cloned.1.call-start = ((), (), s32[]{:S(2)}) async-start(), calls=%async_computation.7 | async-start | bytes 983040
  275.9 2.1 copy-start.13
  278.1 2.1 copy-start.27
  278.1 2.1 copy-start.14
  278.1 2.1 copy-start.39
  280.2 1.0 copy-start.17
  282.1 6.6 %copy-start.11 = (bf16[2,6,3,64,64]{4,3,2,1,0:T(8,128)(2,1)S(1)}, bf16[2,6,3,64,64]{4,3,2,1,0:T(8,128)(2,1)}, u32[]{:S(2)}) copy-start(bf16[2,6,3,64,64]{4,3,2,1,0:T(8,128)(2,1)} %copy-done.10) | copy-start | bytes 884740
  288.7 1.0 copy-start.30
  290.9 0.8 copy-start.25
  290.9 0.8 copy-start.31
  293.2 1.9 copy-start.36
  293.2 2.5 copy-start.6
  293.7 2.2 copy-start.3
  293.7 2.2 copy-start.5
  293.7 2.2 copy-start.7
  293.7 2.2 copy-start.15
  293.7 2.2 copy-start.41
  293.7 2.2 copy-start.43
  293.8 2.2 copy-start.45
  293.8 2.2 copy-start.50
  293.8 2.2 copy-start.52
  296.0 4.2 copy-start.9
  305.3 15.4 %copy-start.26 = (f32[64,32]{1,0:T(8,128)S(1)}, f32[64,32]{1,0:T(8,128)}, u32[]{:S(2)}) copy-start(f32[64,32]{1,0:T(8,128)} %copy-done.24) | copy-start | bytes 24580
  305.3 15.4 %copy-start.32 = (f32[64,32]{1,0:T(8,128)S(1)}, f32[64,32]{1,0:T(8,128)}, u32[]{:S(2)}) copy-start(f32[64,32]{1,0:T(8,128)} %get-tuple-element.132) | copy-start | bytes 24580
  320.6 1.0 copy-start.22
  320.9 1.1 copy-start.2
  320.9 1.1 copy-start.47
  329.9 6.6 %copy-start.38 = (f32[1,1152]{1,0:T(1,128)S(1)}, f32[1,1152]{1,0:T(1,128)}, u32[]{:S(2)}) copy-start(f32[1,1152]{1,0:T(1,128)} %reshape.694) | copy-start | bytes 13828
  337.3 157.2 %copy-start.12 = (f32[128,1152]{0,1:T(8,128)S(1)}, f32[128,1152]{0,1:T(8,128)}, u32[]{:S(2)}) copy-start(f32[128,1152]{0,1:T(8,128)} %copy.293) | copy-start | bytes 1769476
  337.3 157.2 %copy-start.18 = (f32[128,288]{0,1:T(8,128)S(1)}, f32[128,288]{0,1:T(8,128)}, u32[]{:S(2)}) copy-start(f32[128,288]{0,1:T(8,128)} %get-tuple-element.110) | copy-start | bytes 442372
  337.3 157.2 %copy-start.19 = (f32[128,288]{0,1:T(8,128)S(1)}, f32[128,288]{0,1:T(8,128)}, u32[]{:S(2)}) copy-start(f32[128,288]{0,1:T(8,128)} %get-tuple-element.111) | copy-start | bytes 442372
  337.3 157.2 %copy-start.20 = (f32[128,288]{0,1:T(8,128)S(1)}, f32[128,288]{0,1:T(8,128)}, u32[]{:S(2)}) copy-start(f32[128,288]{0,1:T(8,128)} %get-tuple-element.113) | copy-start | bytes 442372
  337.3 157.2 %copy-start.21 = (f32[128,288]{0,1:T(8,128)S(1)}, f32[128,288]{0,1:T(8,128)}, u32[]{:S(2)}) copy-start(f32[128,288]{0,1:T(8,128)} %get-tuple-element.115) | copy-start | bytes 442372
  337.3 157.2 %copy-start.28 = (f32[128,1152]{0,1:T(8,128)S(1)}, f32[128,1152]{0,1:T(8,128)}, u32[]{:S(2)}) copy-start(f32[128,1152]{0,1:T(8,128)} %get-tuple-element.139) | copy-start | bytes 1769476
  337.3 157.2 %copy-start.40 = (f32[128]{0:T(128)S(1)}, f32[128]{0:T(128)}, u32[]{:S(2)}) copy-start(f32[128]{0:T(128)} %rsqrt.34) | copy-start | bytes 1540
  337.3 157.2 %copy-start.48 = (f32[128]{0:T(128)S(1)}, f32[128]{0:T(128)}, u32[]{:S(2)}) copy-start(f32[128]{0:T(128)} %multiply_multiply_fusion.2) | copy-start | bytes 1540
  337.3 157.2 %copy-start.51 = (f32[128]{0:T(128)S(1)}, f32[128]{0:T(128)}, u32[]{:S(2)}) copy-start(f32[128]{0:T(128)} %broadcast_multiply_fusion.1) | copy-start | bytes 1540
  337.3 157.2 %copy-start.53 = (f32[128]{0:T(128)S(1)}, f32[128]{0:T(128)}, u32[]{:S(2)}) copy-start(f32[128]{0:T(128)} %multiply_multiply_fusion.1) | copy-start | bytes 1540
  494.6 6.1 %copy-start.23 = (f32[144,1536]{1,0:T(8,128)S(1)}, f32[144,1536]{1,0:T(8,128)}, u32[]{:S(2)}) copy-start(f32[144,1536]{1,0:T(8,128)} %get-tuple-element.156) | copy-start | bytes 2654212
  495.0 6.6 %copy-start.29 = (f32[288,384]{1,0:T(8,128)S(1)}, f32[288,384]{1,0:T(8,128)}, u32[]{:S(2)}) copy-start(f32[288,384]{1,0:T(8,128)} %get-tuple-element.75) | copy-start | bytes 1327108
  (7 other events, 4.3 us)
Sparse Core Ops, SparseCore 0:
  188.2 14.7 all-gather.3
  205.1 17.4 all-gather.5
  234.0 25.6 reduce-scatter.7
  267.0 25.8 reduce-scatter.5
  295.9 23.2 reduce-scatter.9

commit v2 on v0

--- a/solution.py
+++ b/solution.py
@@ -1,8 +1,11 @@
+import functools
 import math
 
 import jax
 import jax.numpy as jnp
 from jax import lax
+from jax.experimental import pallas as pl
+from jax.experimental.pallas import tpu as pltpu
 from jax.sharding import PartitionSpec as P
 
 QH = 18
@@ -305,9 +308,967 @@
     )
 
 
+MESH = pl.DeviceIdType.MESH
+
+
+class Place:
+    def __init__(self):
+        self.dp = lax.axis_index("dp")
+        self.ctx = lax.axis_index("ctx")
+        self.z = lax.div(self.dp, 2)
+        self.y = lax.rem(self.dp, 2)
+        self.x = lax.div(self.ctx, 2)
+        self.c = lax.rem(self.ctx, 2)
+        self.up = (self.dp + 2, self.ctx)
+        self.down = (self.dp - 2, self.ctx)
+        self.across = (self.dp + 1 - 2 * self.y, self.ctx)
+        self.chip = (self.dp, (1 - self.x) * 2 + self.c)
+        self.core = (self.dp, self.x * 2 + 1 - self.c)
+        self.has_up = self.z < 3
+        self.has_down = self.z > 0
+
+
+def greet(place):
+    barrier = pltpu.get_barrier_semaphore()
+
+    def tell(device):
+        pl.semaphore_signal(barrier, inc=1, device_id=device, device_id_type=MESH)
+
+    pl.when(place.has_up)(lambda: tell(place.up))
+    pl.when(place.has_down)(lambda: tell(place.down))
+    tell(place.across)
+    for step in (1, 2, 3):
+        tell((place.dp, lax.rem(place.ctx + step, 4)))
+    ends = place.has_up.astype(jnp.int32) + place.has_down.astype(jnp.int32)
+    pl.semaphore_wait(barrier, 4 + ends)
+
+
+class Wires:
+    def __init__(self, send_sems, recv_sems, names):
+        self.send_sems = send_sems
+        self.recv_sems = recv_sems
+        self.index = names
+        self.count = 0
+        self.pending = []
+
+    def slot(self, name):
+        if name not in self.index:
+            self.index[name] = len(self.index)
+        return self.index[name]
+
+    def send(self, src, dst, name, device, cond=None, extra=None):
+        number = self.count
+        self.count += 1
+        at = self.slot(name)
+        if extra is not None:
+            at = at + extra
+        copy = pltpu.make_async_remote_copy(
+            src_ref=src,
+            dst_ref=dst,
+            send_sem=self.send_sems.at[number],
+            recv_sem=self.recv_sems.at[at],
+            device_id=device,
+            device_id_type=MESH,
+        )
+        if cond is None:
+            copy.start()
+        else:
+            pl.when(cond)(copy.start)
+        self.pending.append((copy, cond))
+
+    def take(self, dst, name, device, extra=None):
+        at = self.slot(name)
+        if extra is not None:
+            at = at + extra
+        pltpu.make_async_remote_copy(
+            src_ref=dst,
+            dst_ref=dst,
+            send_sem=self.send_sems.at[0],
+            recv_sem=self.recv_sems.at[at],
+            device_id=device,
+            device_id_type=MESH,
+        ).wait_recv()
+
+    def drain(self, first=None):
+        first = len(self.pending) if first is None else first
+        for copy, cond in self.pending[:first]:
+            when(cond, copy.wait_send)
+        self.pending = self.pending[first:]
+
+
+BELOW, ABOVE = 0, 1
+
+
+def both(first, second):
+    return second if first is None else jnp.logical_and(first, second)
+
+
+def source_valid(place, way, dist):
+    return place.z >= dist if way == BELOW else place.z + dist <= 3
+
+
+def source_pos(place, way, dist):
+    return place.dp - 2 * dist if way == BELOW else place.dp + 2 * dist
+
+
+def flood_start(wires, place, name, own, block, spread):
+    wires.send(own, block(place.dp), (name, BELOW, 1), place.up, place.has_up)
+    wires.send(own, block(place.dp), (name, ABOVE, 1), place.down, place.has_down)
+    wires.send(own, block(place.dp), (name, "y", 0, 0), place.across)
+    spread(own, place.dp, (0, 0, 0), None)
+
+
+def flood_step(wires, place, name, block, spread, way, dist):
+    here = source_valid(place, way, dist)
+    pos = source_pos(place, way, dist)
+    view = block(pos)
+    came_from = place.down if way == BELOW else place.up
+    pl.when(here)(lambda: wires.take(view, (name, way, dist), came_from))
+    if dist < 3:
+        onward = place.up if way == BELOW else place.down
+        more = place.has_up if way == BELOW else place.has_down
+        wires.send(view, view, (name, way, dist + 1), onward, jnp.logical_and(here, more))
+    wires.send(view, view, (name, "y", way, dist), place.across, here)
+    spread(view, pos, (0, way, dist), here)
+
+
+def flood_side(wires, place, name, block, spread, way, dist):
+    if dist == 0:
+        here, pos = None, place.dp
+    else:
+        here, pos = source_valid(place, way, dist), source_pos(place, way, dist)
+    pos = pos + 1 - 2 * place.y
+    view = block(pos)
+    if here is None:
+        wires.take(view, (name, "y", 0, 0), place.across)
+    else:
+        pl.when(here)(lambda: wires.take(view, (name, "y", way, dist), place.across))
+    spread(view, pos, (1, way, dist), here)
+
+
+HOPS = [(way, dist) for dist in (1, 2, 3) for way in (BELOW, ABOVE)]
+
+
+def no_spread(view, pos, key, cond):
+    return None
+
+
+def add_rows(dst, srcs, out=None, cast=None, chunk=48):
+    out = dst if out is None else out
+    total_rows = dst.shape[0]
+    assert total_rows % chunk == 0
+
+    def body(i, carry):
+        at = pl.ds(pl.multiple_of(i * chunk, 16), chunk)
+        total = dst[at, :].astype(jnp.float32)
+        for src in srcs:
+            total = total + src[at, :].astype(jnp.float32)
+        out[at, :] = total.astype(out.dtype)
+        return carry
+
+    lax.fori_loop(0, total_rows // chunk, body, 0)
+
+
+def when(cond, action):
+    if cond is None:
+        action()
+    else:
+        pl.when(cond)(action)
+
+
+DRAIN = [(way, dist) for dist in (3, 2, 1, 0) for way in (BELOW, ABOVE)]
+
+
+def sink_step(wires, place, name, block, inbox, way, dist):
+    here = source_valid(place, way, dist)
+    pos = source_pos(place, way, dist)
+    view = block(pos)
+    fed = place.has_up if way == BELOW else place.has_down
+    feeder = place.up if way == BELOW else place.down
+    onward = place.down if way == BELOW else place.up
+    if dist < 3:
+
+        def arrive():
+            wires.take(inbox.at[way, dist], (name, way, dist), feeder)
+            add_rows(view, [inbox.at[way, dist]])
+
+        pl.when(jnp.logical_and(here, fed))(arrive)
+    if dist > 0:
+        wires.send(view, inbox.at[way, dist - 1], (name, way, dist - 1), onward, here)
+
+
+def nn(a, b):
+    return jnp.dot(a, b, preferred_element_type=jnp.float32)
+
+
+def nt(a, b):
+    return lax.dot_general(a, b, (((1,), (1,)), ((), ())), preferred_element_type=jnp.float32)
+
+
+def tn(a, b):
+    return lax.dot_general(a, b, (((0,), (0,)), ((), ())), preferred_element_type=jnp.float32)
+
+
+def layer_kernel(
+    names,
+    tokens, cot, lengths, qkv_in, out_in, gu_in, dt_in, gain_in, cos, sin,
+    output, grad_tokens, gain_out, qkv_out, out_out, gu_out, dt_out,
+    w_qkv, w_out, w_ff, gain_all, gain_row,
+    n1, n2_all, g_all, context, hidden, grad_hidden, proj, q_st, kv_all, p_st, att, go_st, wide, gm,
+    act, d_gate, d_up, gp, gp_box, op, op_box, dkv, dkv_box,
+    d_gu, d_dt,
+    qkv_core, out_core, qkv_chip, out_chip, qkv_side, out_side, gu_side, down_side,
+    qkv_inbox, out_inbox, gu_inbox, down_inbox, gu_mix, down_mix, gain_box,
+    send_sems, recv_sems, local_sems,
+):
+    f32, low = jnp.float32, jnp.bfloat16
+    place = Place()
+    wires = Wires(send_sems, recv_sems, names)
+    dp, ctx, z, y, x, c = place.dp, place.ctx, place.z, place.y, place.x, place.c
+    rows = qkv_in.shape[0]
+    strip, half = dt_in.shape
+    units = act.shape[1]
+    width = tokens.shape[1]
+    own_rows = tokens.shape[0]
+    slots_here = own_rows // 2
+    qkv_cols, out_cols = qkv_in.shape[1], out_in.shape[1]
+    qkv_wide, out_wide = w_qkv.shape[2], w_out.shape[2]
+    group = QH // KVH
+    slabs = KVH // 2
+    gate_at, up_at, down_at = 0, units, 2 * units
+
+    greet(place)
+
+    def row_view(ref, lead, pos):
+        return ref.at[lead, pl.ds(pl.multiple_of(pos * rows, 16), rows)]
+
+    def ff_view(at, pos):
+        return w_ff.at[pl.ds(pl.multiple_of(pos * rows, 16), rows), pl.ds(at, units)]
+
+    locals_ = []
+
+    def local(src, dst, cond=None):
+        copy = pltpu.make_async_copy(src, dst, local_sems.at[len(locals_)])
+        locals_.append((copy, cond))
+        when(cond, copy.start)
+
+    my_rows = pl.ds(pl.multiple_of(dp * rows, 16), rows)
+    gu_places = ((gate_at, 0), (up_at, 1))
+    for part in range(2):
+        target = 2 * c + part
+        src = gu_in.at[:, pl.ds(part * units, units)]
+        for at, half_x in gu_places:
+            here = x == half_x
+            wires.send(src, ff_view(at, dp), ("gu_mix", half_x), (dp, target), jnp.logical_and(here, target != ctx))
+            local(src, ff_view(at, dp), jnp.logical_and(here, target == ctx))
+
+    def attention_spread(name, ref):
+        def spread(view, pos, key, cond):
+            dst = row_view(ref, ctx, pos)
+            wires.send(view, dst, (name, "x") + key, place.chip, cond)
+            wires.send(view, dst, (name, "c") + key, place.core, cond)
+        return spread
+
+    attention = [("qkv", qkv_in, w_qkv, qkv_cols), ("out", out_in, w_out, out_cols)]
+
+    def attention_start(name, own, ref, cols):
+        ref[ctx, my_rows, :] = jnp.zeros((rows, ref.shape[2]), low)
+        ref[ctx, my_rows, :cols] = own[...]
+        block = functools.partial(row_view, ref, ctx)
+        flood_start(wires, place, name, block(dp), block, attention_spread(name, ref))
+
+    attention_start(*attention[0])
+    gain_block = lambda pos: gain_all.at[pos]
+    gain_all[dp] = gain_in[...]
+    flood_start(wires, place, "gain", gain_block(dp), gain_block, no_spread)
+    attention_start(*attention[1])
+
+    lanes = pl.ds(pl.multiple_of(down_at + y * half, 128), half)
+    other_lanes = pl.ds(pl.multiple_of(down_at + (1 - y) * half, 128), half)
+    dst = w_ff.at[pl.ds(pl.multiple_of(ctx * strip, 16), strip), lanes]
+    wires.send(dt_in, dst, ("down_mix", 0), (dp, z), ctx != z, extra=ctx)
+    for j in range(1, 4):
+        wires.slot(("down_mix", j))
+    local(dt_in, dst, ctx == z)
+
+    row_at = lax.broadcasted_iota(jnp.int32, (own_rows, 1), 0)
+    first_seq = row_at < slots_here
+    position = ctx * slots_here + jnp.where(first_seq, row_at, row_at - slots_here)
+    row_length = jnp.where(first_seq, lengths[0], lengths[1])
+    valid = position < row_length
+
+    def share(name, ref):
+        mine = ref.at[pl.ds(pl.multiple_of(ctx * own_rows, 16), own_rows)]
+        wires.send(mine, mine, (name, "x"), place.chip)
+        wires.send(mine, mine, (name, "c"), place.core)
+
+    def share_on(name, ref):
+        far = ref.at[pl.ds(pl.multiple_of(place.chip[1] * own_rows, 16), own_rows)]
+        wires.take(far, (name, "x"), place.chip)
+        wires.send(far, far, (name, "d"), place.core)
+
+    def share_end(name, ref):
+        for mark, lead in (("c", place.core[1]), ("d", 3 - ctx)):
+            view = ref.at[pl.ds(pl.multiple_of(lead * own_rows, 16), own_rows)]
+            wires.take(view, (name, mark), place.core)
+
+    here_rows = pl.ds(pl.multiple_of(ctx * own_rows, 16), own_rows)
+    g_all[here_rows, :] = jnp.where(valid, cot[...].astype(f32), 0.0).astype(low)
+
+    for part in range(2):
+        remote = (part * 2 + x) != ctx
+        view = ff_view(gu_places[part][0], dp)
+        pl.when(remote)(lambda: wires.take(view, ("gu_mix", part), (dp, part * 2 + x)))
+    for copy, cond in locals_:
+        when(cond, copy.wait)
+    gu_blocks = [functools.partial(ff_view, at) for at, _ in gu_places]
+    for part in range(2):
+        flood_start(wires, place, ("gu", part), gu_blocks[part](dp), gu_blocks[part], no_spread)
+    share("cot", g_all)
+
+    at_home = ctx == z
+    strips = [w_ff.at[pl.ds(j * strip, strip), lanes] for j in range(4)]
+    other_strips = [w_ff.at[pl.ds(j * strip, strip), other_lanes] for j in range(4)]
+
+    def take_strips():
+        for j in range(4):
+            pl.when(ctx != j)(functools.partial(wires.take, strips[j], ("down_mix", j), (dp, j)))
+
+    def down_start():
+        pl.when(at_home)(take_strips)
+        for j in range(4):
+            wires.send(strips[j], strips[j], ("down", j, BELOW, 1), place.up, jnp.logical_and(at_home, place.has_up))
+            wires.send(strips[j], strips[j], ("down", j, ABOVE, 1), place.down, jnp.logical_and(at_home, place.has_down))
+            wires.send(strips[j], strips[j], ("down_y", j), place.across, at_home)
+
+    def down_step(way, dist):
+        offset = z - ctx if way == BELOW else ctx - z
+        here = offset == dist
+        came_from = place.down if way == BELOW else place.up
+        onward = place.up if way == BELOW else place.down
+        more = place.has_up if way == BELOW else place.has_down
+        for j in range(4):
+            pl.when(here)(functools.partial(wires.take, strips[j], ("down", j, way, dist), came_from))
+            if dist < 3:
+                wires.send(strips[j], strips[j], ("down", j, way, dist + 1), onward, jnp.logical_and(here, more))
+            wires.send(strips[j], strips[j], ("down_y", j), place.across, here)
+
+    def attention_step(way, dist):
+        for name, own, ref, cols in attention:
+            flood_step(wires, place, name, functools.partial(row_view, ref, ctx), attention_spread(name, ref), way, dist)
+
+    def gain_step(way, dist):
+        flood_step(wires, place, "gain", gain_block, no_spread, way, dist)
+
+    def gu_step(way, dist):
+        for part in range(2):
+            flood_step(wires, place, ("gu", part), gu_blocks[part], no_spread, way, dist)
+
+    SIDES = [(0, 0)] + HOPS
+
+    def positions():
+        for side in range(2):
+            for way, dist in SIDES:
+                if dist == 0:
+                    here, pos = None, dp
+                else:
+                    here, pos = source_valid(place, way, dist), source_pos(place, way, dist)
+                if side == 1:
+                    pos = pos + 1 - 2 * y
+                yield (side, way, dist), here, pos
+
+    def attention_sides(which):
+        name, own, ref, cols = which
+        for way, dist in SIDES:
+            flood_side(wires, place, name, functools.partial(row_view, ref, ctx), attention_spread(name, ref), way, dist)
+
+    def attention_chip(which):
+        name, own, ref, cols = which
+        for key, here, pos in positions():
+            view = row_view(ref, place.chip[1], pos)
+            when(here, lambda: wires.take(view, (name, "x") + key, place.chip))
+            wires.send(view, view, (name, "d") + key, place.core, here)
+
+    def attention_core(which):
+        name, own, ref, cols = which
+        for key, here, pos in positions():
+            for mark, lead in (("c", place.core[1]), ("d", 3 - ctx)):
+                view = row_view(ref, lead, pos)
+                when(here, lambda: wires.take(view, (name, mark) + key, place.core))
+
+    down_start()
+    for dist in (1, 2, 3):
+        for way in (BELOW, ABOVE):
+            attention_step(way, dist)
+            gain_step(way, dist)
+        for way in (BELOW, ABOVE):
+            gu_step(way, dist)
+            down_step(way, dist)
+    for way, dist in SIDES:
+        flood_side(wires, place, "gain", gain_block, no_spread, way, dist)
+    attention_sides(attention[0])
+    share_on("cot", g_all)
+    attention_chip(attention[0])
+    attention_core(attention[0])
+    attention_sides(attention[1])
+    attention_chip(attention[1])
+
+    gain_row[...] = jnp.zeros(gain_row.shape, f32)
+    for pos in range(8):
+        piece = gain_all[pos]
+        shift = (pos * rows) % 128
+        if shift:
+            piece = pltpu.roll(piece, shift, 1)
+        at = (pos * rows) // 128 * 128
+        gain_row[:, at : at + 256] += piece
+    gain_a = lambda: gain_row[0:1, :width]
+    gain_b = lambda: gain_row[1:2, :width]
+
+    def norm(values):
+        return lax.rsqrt(jnp.mean(values * values, axis=-1, keepdims=True) + EPS)
+
+    source = tokens[...].astype(f32)
+    n1[...] = (source * norm(source) * gain_a()).astype(low)
+    proj[...] = jnp.zeros(proj.shape, f32)
+    for j in range(4):
+        part = nn(n1[...], w_qkv[j])
+        part = jnp.concatenate([part, jnp.zeros((own_rows, 128), f32)], axis=1)
+        at = qkv_cols * j
+        if at % 128:
+            part = pltpu.roll(part, at % 128, 1)
+        proj[:, at // 128 * 128 : at // 128 * 128 + qkv_wide + 128] += part
+
+    lane = lax.broadcasted_iota(jnp.int32, (own_rows, 128), 1)
+    low_half = lax.rem(lane, HD) < HD // 2
+    side_of = lax.div(lane, HD)
+
+    def turn(values, sign):
+        swapped = jnp.where(low_half, pltpu.roll(values, 128 - HD // 2, 1), pltpu.roll(values, HD // 2, 1))
+        return values * cos[...] + swapped * (sin[...] * sign)
+
+    def head_spots():
+        for head in range(QH):
+            kv = head // group
+            yield head // 2, head % 2, kv // 2, kv % 2, (kv % 2 * group + head % group) * slots_here
+
+    def stack_heads(slab_of, dest, scale):
+        for slab, side, key_slab, key_side, at in head_spots():
+            values = slab_of(slab)
+            if side != key_side:
+                values = pltpu.roll(values, HD, 1)
+            values = (jnp.where(side_of == key_side, values, 0.0) * scale).astype(low)
+            for seq in range(2):
+                dest[seq * slabs + key_slab, at : at + slots_here, :] = values[
+                    seq * slots_here : (seq + 1) * slots_here
+                ]
+
+    def unstack_heads(src, slab):
+        total = jnp.zeros((own_rows, 128), f32)
+        for at_slab, side, key_slab, key_side, at in head_spots():
+            if at_slab != slab:
+                continue
+            values = jnp.concatenate(
+                [src[seq * slabs + key_slab, at : at + slots_here, :] for seq in range(2)], axis=0
+            )
+            values = jnp.where(side_of == key_side, values, 0.0)
+            if side != key_side:
+                values = pltpu.roll(values, HD, 1)
+            total = total + values
+        return total
+
+    turned = {}
+
+    def query_slab(slab):
+        if slab not in turned:
+            turned[slab] = turn(proj[:, slab * 128 : slab * 128 + 128], 1.0)
+        return turned[slab]
+
+    score_scale = 1.0 / math.sqrt(HD)
+    stack_heads(query_slab, q_st, score_scale)
+    q_slabs = QH // 2
+    my_slots = pl.ds(pl.multiple_of(ctx * slots_here, 16), slots_here)
+    for slab in range(2 * slabs):
+        at = (q_slabs + slab) * 128
+        values = proj[:, at : at + 128]
+        if slab < slabs:
+            values = turn(values, 1.0)
+        values = values.astype(low)
+        for seq in range(2):
+            kv_all[seq, slab, my_slots, :] = values[seq * slots_here : (seq + 1) * slots_here]
+
+    def slot_view(lead):
+        return kv_all.at[:, :, pl.ds(pl.multiple_of(lead * slots_here, 16), slots_here)]
+
+    for step in (1, 2, 3):
+        wires.send(slot_view(ctx), slot_view(ctx), ("kv", step), (dp, lax.rem(ctx + step, 4)))
+    attention_core(attention[1])
+    for step in (1, 2, 3):
+        peer = lax.rem(ctx + 4 - step, 4)
+        wires.take(slot_view(peer), ("kv", step), (dp, peer))
+
+    stack = q_st.shape[1]
+    slots = kv_all.shape[2]
+
+    def attend(i, carry):
+        seq, slab = lax.div(i, slabs), lax.rem(i, slabs)
+        scores = nt(q_st[i], kv_all[seq, slab])
+        at = ctx * slots_here + lax.rem(lax.broadcasted_iota(jnp.int32, (stack, slots), 0), slots_here)
+        key_at = lax.broadcasted_iota(jnp.int32, (stack, slots), 1)
+        length = jnp.where(seq == 0, lengths[0], lengths[1])
+        allowed = jnp.logical_and(key_at <= at, key_at < length)
+        scores = jnp.where(allowed, scores, NEGATIVE)
+        terms = jnp.exp(scores - jnp.max(scores, axis=-1, keepdims=True))
+        probs = (terms / jnp.sum(terms, axis=-1, keepdims=True)).astype(low)
+        p_st[i] = probs
+        att[i] = nn(probs, kv_all[seq, slabs + slab])
+        return carry
+
+    lax.fori_loop(0, 2 * slabs, attend, 0)
+    for slab in range(q_slabs):
+        context[:, slab * 128 : slab * 128 + 128] = unstack_heads(att, slab).astype(low)
+    hidden[...] = source
+    for j in range(4):
+        part = nn(context[...], w_out[j])
+        at = out_cols * j
+        if at % 128:
+            part = pltpu.roll(part, at % 128, 1)
+        hidden[:, at // 128 * 128 : at // 128 * 128 + out_wide] += part
+    n2_all[here_rows, :] = (hidden[...] * norm(hidden[...]) * gain_b()).astype(low)
+    share("n2", n2_all)
+    share_end("cot", g_all)
+
+    gathered = len(wires.pending)
+
+    for part in range(2):
+        for way, dist in SIDES:
+            flood_side(wires, place, ("gu", part), gu_blocks[part], no_spread, way, dist)
+    for j in range(4):
+        wires.take(other_strips[j], ("down_y", j), place.across)
+    share_on("n2", n2_all)
+    share_end("n2", n2_all)
+
+    tall, tile = 256, 256
+
+    def feed(i, carry):
+        at = pl.ds(pl.multiple_of(lax.div(i, units // tile) * tall, tall), tall)
+        unit = lax.rem(i, units // tile) * tile
+
+        def cols(base):
+            return pl.ds(pl.multiple_of(base + unit, tile), tile)
+
+        gate = nn(n2_all[at, :], w_ff[:, cols(gate_at)])
+        up = nn(n2_all[at, :], w_ff[:, cols(up_at)])
+        back = nn(g_all[at, :], w_ff[:, cols(down_at)])
+        sig = jax.nn.sigmoid(gate)
+        swish = gate * sig
+        act[at, cols(0)] = (swish * up).astype(low)
+        d_gate[at, cols(0)] = (back * up * sig * (1.0 + gate * (1.0 - sig))).astype(low)
+        d_up[at, cols(0)] = (back * swish).astype(low)
+        return carry
+
+    lax.fori_loop(0, (4 * own_rows // tall) * (units // tile), feed, 0)
+
+    across_core = (1 - x) * 2 + 1 - c
+    across_own = (1 - x) * 2 + c
+    beside = x * 2 + 1 - c
+    wide_tile = 384
+
+    def group_blocks(compute, name, ref, box):
+        for mark, lead in (("cx", across_core), ("", across_own), ("cc", beside), ("", ctx)):
+            compute(lead)
+            if mark:
+                wires.send(ref.at[lead], box.at[0 if mark == "cx" else 1], (name, mark), place.core)
+
+    def group_on(name, ref, box):
+        wires.take(box.at[0], (name, "cx"), place.core)
+        add_any(ref.at[across_own], box.at[0])
+        wires.send(ref.at[across_own], box.at[2], (name, "x"), place.chip)
+
+    def group_end(name, ref, box):
+        wires.take(box.at[1], (name, "cc"), place.core)
+        wires.take(box.at[2], (name, "x"), place.chip)
+        return ref[ctx].astype(f32) + box[1].astype(f32) + box[2].astype(f32)
+
+    def add_any(dst, src):
+        dst[...] = (dst[...].astype(f32) + src[...].astype(f32)).astype(low)
+
+    def lead_rows(lead):
+        return pl.ds(pl.multiple_of(lead * own_rows, 16), own_rows)
+
+    def back_block(lead):
+        def body(n, carry):
+            at = pl.ds(pl.multiple_of(n * wide_tile, 128), wide_tile)
+            total = nt(d_gate[lead_rows(lead), :], w_ff[at, pl.ds(gate_at, units)])
+            total = total + nt(d_up[lead_rows(lead), :], w_ff[at, pl.ds(up_at, units)])
+            gp[lead, :, at] = total.astype(low)
+            return carry
+
+        lax.fori_loop(0, width // wide_tile, body, 0)
+
+    def forward_block(lead):
+        def body(n, carry):
+            at = pl.ds(pl.multiple_of(n * wide_tile, 128), wide_tile)
+            op[lead, :, at] = nt(act[lead_rows(lead), :], w_ff[at, pl.ds(down_at, units)]).astype(low)
+            return carry
+
+        lax.fori_loop(0, width // wide_tile, body, 0)
+
+    group_blocks(back_block, "gp", gp, gp_box)
+
+    def grad_ff(m, carry):
+        at = pl.ds(pl.multiple_of(m * 128, 128), 128)
+        left = n2_all[:, at]
+        d_gu[0, at, :] = tn(left, d_gate[...]).astype(low)
+        d_gu[1, at, :] = tn(left, d_up[...]).astype(low)
+        d_dt[at, :] = tn(g_all[:, at], act[...]).astype(low)
+        return carry
+
+    lax.fori_loop(0, width // 128, grad_ff, 0)
+    group_on("gp", gp, gp_box)
+
+    d_lanes = pl.ds(pl.multiple_of(y * half, 128), half)
+    d_other = pl.ds(pl.multiple_of((1 - y) * half, 128), half)
+    d_strips = [d_dt.at[pl.ds(j * strip, strip), d_lanes] for j in range(4)]
+    d_other_strips = [d_dt.at[pl.ds(j * strip, strip), d_other] for j in range(4)]
+    for zs in range(4):
+        for part in range(2):
+            wires.send(row_view(d_gu, part, 2 * zs + 1 - y), gu_side.at[part, zs], ("dgu_y", part, zs), place.across)
+    for j in range(4):
+        wires.send(d_other_strips[j], down_side.at[j], ("ddown_y", j), place.across)
+
+    group_blocks(forward_block, "op", op, op_box)
+    group_on("op", op, op_box)
+
+    def norm_back(values, inverse, gain, grad_in):
+        scaled = grad_in * gain
+        mean_term = jnp.mean(scaled * values, axis=-1, keepdims=True)
+        back = inverse * scaled - values * (inverse * inverse * inverse) * mean_term
+        return back, jnp.sum(grad_in * values * inverse, axis=0, keepdims=True)
+
+    gain_out[...] = jnp.zeros(gain_out.shape, f32)
+    back_two, gain_two_grad = norm_back(hidden[...], norm(hidden[...]), gain_b(), group_end("gp", gp, gp_box))
+    gain_out[1:2, :] = gain_two_grad
+    grad_hidden[...] = g_all[here_rows, :].astype(f32) + back_two
+    out_lane = lax.broadcasted_iota(jnp.int32, (own_rows, out_wide), 1)
+    for j in range(4):
+        at = out_cols * j
+        part = grad_hidden[:, at // 128 * 128 : at // 128 * 128 + out_wide]
+        if at % 128:
+            part = pltpu.roll(part, out_wide - at % 128, 1)
+        wide[j] = jnp.where(out_lane < out_cols, part, 0.0).astype(low)
+
+    def context_back(n, carry):
+        at = pl.ds(pl.multiple_of(n * wide_tile, 128), wide_tile)
+        total = nt(wide[0], w_out[0, at, :])
+        for j in range(1, 4):
+            total = total + nt(wide[j], w_out[j, at, :])
+        proj[:, at] = total
+        return carry
+
+    lax.fori_loop(0, width // wide_tile, context_back, 0)
+    stack_heads(lambda slab: proj[:, slab * 128 : slab * 128 + 128], go_st, 1.0)
+
+    wires.drain(gathered)
+    pair = 2 * rows
+
+    def out_view(lead, at, size):
+        return w_out.at[lead, pl.ds(at, size)]
+
+    def qkv_view(lead, at, size):
+        return w_ff.at[pl.ds(at, size), pl.ds(pl.multiple_of(lead * qkv_wide, 128), qkv_wide)]
+
+    def grad_out(m, carry):
+        at = pl.ds(pl.multiple_of(m * 128, 128), 128)
+        for j in range(4):
+            w_out[j, at, :] = tn(context[:, at], wide[j]).astype(low)
+        return carry
+
+    lax.fori_loop(0, width // 128, grad_out, 0)
+
+    def core_send(name, view, core):
+        for zs in range(4):
+            for xx in range(2):
+                wires.send(
+                    view(2 * xx + 1 - c, zs * pair, pair), core.at[xx, pl.ds(zs * pair, pair)],
+                    (name, "gc", xx, zs), place.core,
+                )
+
+    def core_add(name, view, core, chip):
+        for zs in range(4):
+            for xx in range(2):
+                box = core.at[xx, pl.ds(zs * pair, pair)]
+                wires.take(box, (name, "gc", xx, zs), place.core)
+                add_rows(view(2 * xx + c, zs * pair, pair), [box])
+            wires.send(view(place.chip[1], zs * pair, pair), chip.at[pl.ds(zs * pair, pair)], (name, "gx", zs), place.chip)
+
+    def own_view(view, pos):
+        return view(ctx, pl.multiple_of(pos * rows, 16), rows)
+
+    def chip_add(name, view, chip, side):
+        for zs in range(4):
+            span = chip.at[pl.ds(zs * pair, pair)]
+            wires.take(span, (name, "gx", zs), place.chip)
+            add_rows(view(ctx, zs * pair, pair), [span])
+            wires.send(own_view(view, 2 * zs + 1 - y), side.at[zs], (name, "gy", zs), place.across)
+
+    def side_add(name, view, side):
+        for zs in range(4):
+            wires.take(side.at[zs], (name, "gy", zs), place.across)
+            add_rows(own_view(view, 2 * zs + y), [side.at[zs]])
+
+    def drain_z(name, view, inbox):
+        for way, dist in DRAIN:
+            sink_step(wires, place, (name, "g"), functools.partial(own_view, view), inbox, way, dist)
+
+    core_send("out", out_view, out_core)
+
+    def attend_back(i, carry):
+        seq, slab = lax.div(i, slabs), lax.rem(i, slabs)
+        grad_probs = nt(go_st[i], kv_all[seq, slabs + slab])
+        probs = p_st[i].astype(f32)
+        delta = jnp.sum(probs * grad_probs, axis=-1, keepdims=True)
+        grad_scores = (probs * (grad_probs - delta)).astype(low)
+        att[i] = nn(grad_scores, kv_all[seq, slab]) * score_scale
+        grad_key = tn(grad_scores, q_st[i])
+        grad_value = tn(p_st[i], go_st[i])
+        for j in range(4):
+            part = slice(j * slots_here, (j + 1) * slots_here)
+            dkv[j, seq, slab] = grad_key[part].astype(low)
+            dkv[j, seq, slabs + slab] = grad_value[part].astype(low)
+        return carry
+
+    lax.fori_loop(0, 2 * slabs, attend_back, 0)
+    group_blocks(lambda lead: None, "dkv", dkv, dkv_box)
+    core_add("out", out_view, out_core, out_chip)
+    group_on("dkv", dkv, dkv_box)
+
+    for zs in range(4):
+        for part in range(2):
+            wires.take(gu_side.at[part, zs], ("dgu_y", part, zs), place.across)
+            add_rows(row_view(d_gu, part, 2 * zs + y), [gu_side.at[part, zs]])
+    for j in range(4):
+        wires.take(down_side.at[j], ("ddown_y", j), place.across)
+        add_rows(d_strips[j], [down_side.at[j]])
+
+    sums = group_end("dkv", dkv, dkv_box)
+    proj[...] = jnp.zeros(proj.shape, f32)
+    for slab in range(q_slabs):
+        proj[:, slab * 128 : slab * 128 + 128] = turn(unstack_heads(att, slab), -1.0)
+    for slab in range(2 * slabs):
+        values = jnp.concatenate([sums[0, slab], sums[1, slab]], axis=0)
+        if slab < slabs:
+            values = turn(values, -1.0)
+        at = (q_slabs + slab) * 128
+        proj[:, at : at + 128] = values
+    qkv_lane = lax.broadcasted_iota(jnp.int32, (own_rows, qkv_wide), 1)
+    for j in range(4):
+        at = qkv_cols * j
+        part = proj[:, at // 128 * 128 : at // 128 * 128 + qkv_wide + 128]
+        if at % 128:
+            part = pltpu.roll(part, qkv_wide + 128 - at % 128, 1)
+        gm[j] = jnp.where(qkv_lane < qkv_cols, part[:, :qkv_wide], 0.0).astype(low)
+
+    def grad_qkv(m, carry):
+        at = pl.ds(pl.multiple_of(m * 128, 128), 128)
+        for j in range(4):
+            w_ff[at, pl.ds(j * qkv_wide, qkv_wide)] = tn(n1[:, at], gm[j]).astype(low)
+        return carry
+
+    lax.fori_loop(0, width // 128, grad_qkv, 0)
+    core_send("qkv", qkv_view, qkv_core)
+    chip_add("out", out_view, out_chip, out_side)
+
+    def tokens_back(n, carry):
+        at = pl.ds(pl.multiple_of(n * wide_tile, 128), wide_tile)
+        total = nt(gm[0], w_qkv[0, at, :])
+        for j in range(1, 4):
+            total = total + nt(gm[j], w_qkv[j, at, :])
+        proj[:, at] = total
+        return carry
+
+    lax.fori_loop(0, width // wide_tile, tokens_back, 0)
+    core_add("qkv", qkv_view, qkv_core, qkv_chip)
+    source = tokens[...].astype(f32)
+    back_one, gain_one_grad = norm_back(source, norm(source), gain_a(), proj[:, :width])
+    gain_out[0:1, :] = gain_one_grad
+    grad_tokens[...] = (grad_hidden[...] + back_one).astype(low)
+    result = hidden[...] + group_end("op", op, op_box)
+    output[...] = jnp.where(valid, result, 0.0).astype(low)
+
+    def down_sink(dist):
+        for way in (BELOW, ABOVE):
+            offset = z - ctx if way == BELOW else ctx - z
+            here = offset == dist
+            fed = place.has_up if way == BELOW else place.has_down
+            feeder = place.up if way == BELOW else place.down
+            onward = place.down if way == BELOW else place.up
+            for j in range(4):
+
+                def arrive():
+                    wires.take(down_inbox.at[way, j], ("ddown", j, way), feeder)
+                    add_rows(d_strips[j], [down_inbox.at[way, j]])
+
+                pl.when(jnp.logical_and(here, fed))(arrive)
+                if dist > 0:
+                    wires.send(d_strips[j], down_inbox.at[way, j], ("ddown", j, way), onward, here)
+
+    for way, dist in DRAIN:
+        for part in range(2):
+            sink_step(wires, place, ("dgu", part), functools.partial(row_view, d_gu, part), gu_inbox.at[part], way, dist)
+        if way == BELOW:
+            down_sink(dist)
+    for part in range(2):
+        target = part * 2 + x
+        block = row_view(d_gu, part, dp)
+        wires.send(block, gu_mix.at[c], ("dgu_mix", 0), (dp, target), target != ctx, extra=c)
+        pl.when(target == ctx)(lambda: add_rows(block, [], out=gu_mix.at[c]))
+    wires.slot(("dgu_mix", 1))
+    for j in range(4):
+        wires.send(d_strips[j], down_mix, ("ddown_mix",), (dp, j), jnp.logical_and(at_home, ctx != j))
+        pl.when(jnp.logical_and(at_home, ctx == j))(functools.partial(add_rows, d_strips[j], [], down_mix))
+    chip_add("qkv", qkv_view, qkv_chip, qkv_side)
+    side_add("out", out_view, out_side)
+    drain_z("out", out_view, out_inbox)
+    side_add("qkv", qkv_view, qkv_side)
+    drain_z("qkv", qkv_view, qkv_inbox)
+    out_out[...] = own_view(out_view, dp)[...].astype(f32)[:, :out_cols]
+    qkv_out[...] = own_view(qkv_view, dp)[...].astype(f32)[:, :qkv_cols]
+
+    def swap(slot, device, cond=None):
+        wires.send(gain_out, gain_box.at[slot], ("gain_sum", slot), device, cond)
+
+    def add_gain(slot, device):
+        wires.take(gain_box.at[slot], ("gain_sum", slot), device)
+        gain_out[...] = gain_out[...] + gain_box[slot]
+
+    def settle():
+        copy, cond = wires.pending.pop()
+        when(cond, copy.wait_send)
+
+    for slot, device in enumerate((place.core, place.chip, place.across)):
+        swap(slot, device)
+        settle()
+        add_gain(slot, device)
+    low_end, high_end = z == 0, z == 3
+    mid_low, mid_high = z == 1, z == 2
+    swap(3, place.up, low_end)
+    settle()
+    swap(3, place.down, high_end)
+    settle()
+    pl.when(mid_low)(lambda: add_gain(3, place.down))
+    pl.when(mid_high)(lambda: add_gain(3, place.up))
+    swap(4, place.up, mid_low)
+    settle()
+    swap(4, place.down, mid_high)
+    settle()
+    pl.when(mid_low)(lambda: add_gain(4, place.up))
+    pl.when(mid_high)(lambda: add_gain(4, place.down))
+    swap(5, place.down, mid_low)
+    swap(5, place.up, mid_high)
+
+    def last(device):
+        wires.take(gain_box.at[5], ("gain_sum", 5), device)
+        gain_out[...] = gain_box[5]
+
+    pl.when(low_end)(lambda: last(place.up))
+    pl.when(high_end)(lambda: last(place.down))
+
+    for part in range(2):
+        origin = 2 * c + part
+        pl.when(origin != ctx)(lambda: wires.take(gu_mix.at[part], ("dgu_mix", part), (dp, origin)))
+        add_rows(gu_mix.at[part], [], out=gu_out.at[:, pl.ds(part * units, units)])
+    pl.when(ctx != z)(lambda: wires.take(down_mix, ("ddown_mix",), (dp, z)))
+    add_rows(down_mix, [], out=dt_out)
+    wires.drain()
+
+
+def on_device_fast(tokens, lengths, gain_one, w_qkv, w_out, gain_two, w_gate_up, w_down, cotangent):
+    seq_count, row_count, width = tokens.shape
+    own_rows = seq_count * row_count
+    f32, low = jnp.float32, jnp.bfloat16
+    block = gain_one.shape[0]
+    gains = jnp.stack([gain_one, gain_two]).astype(f32)
+    gains = jnp.pad(gains, ((0, 6), (0, 256 - block)))
+    position = lax.axis_index("ctx") * row_count + jnp.arange(row_count, dtype=jnp.int32)
+    cosine, sine = angles(position, HD)
+    cosine = jnp.tile(cosine, (seq_count, 4))
+    sine = jnp.tile(jnp.concatenate([-sine, sine], axis=1), (seq_count, 2))
+    rows, qkv_cols = w_qkv.shape
+    out_cols = w_out.shape[1]
+    units = w_gate_up.shape[1] // 2
+    half, strip = w_down.shape
+    qkv_wide = -(-qkv_cols // 128) * 128
+    out_wide = -(-out_cols // 128) * 128
+    deep = 8 * rows
+    slots = 4 * row_count
+    slabs = KVH // 2
+    stack = 2 * QH // KVH * row_count
+
+    def box(*shape, dtype=low):
+        return pltpu.VMEM(shape, dtype)
+
+    scratch = [
+        box(4, deep, qkv_wide), box(4, deep, out_wide), box(deep, 3 * units),
+        box(8, 8, 256, dtype=f32), box(8, deep + 128, dtype=f32),
+        box(own_rows, width), box(4 * own_rows, width), box(4 * own_rows, width),
+        box(own_rows, QH * HD), box(own_rows, width, dtype=f32), box(own_rows, width, dtype=f32),
+        box(own_rows, 4 * qkv_wide, dtype=f32),
+        box(seq_count * slabs, stack, 128), box(seq_count, 2 * slabs, slots, 128),
+        box(seq_count * slabs, stack, slots), box(seq_count * slabs, stack, 128, dtype=f32),
+        box(seq_count * slabs, stack, 128), box(4, own_rows, out_wide), box(4, own_rows, qkv_wide),
+        box(4 * own_rows, units), box(4 * own_rows, units), box(4 * own_rows, units),
+        box(4, own_rows, width), box(3, own_rows, width),
+        box(4, own_rows, width), box(3, own_rows, width),
+        box(4, seq_count, 2 * slabs, row_count, 128), box(3, seq_count, 2 * slabs, row_count, 128),
+        box(2, deep, units), box(deep, units),
+        box(2, deep, qkv_wide), box(2, deep, out_wide),
+        box(deep, qkv_wide), box(deep, out_wide),
+        box(4, rows, qkv_wide), box(4, rows, out_wide),
+        box(2, 4, rows, units), box(4, strip, half),
+        box(2, 3, rows, qkv_wide), box(2, 3, rows, out_wide),
+        box(2, 2, 3, rows, units), box(2, 4, strip, half),
+        box(2, rows, units), box(strip, half),
+        box(6, 8, width, dtype=f32),
+        pltpu.SemaphoreType.DMA((480,)),
+        pltpu.SemaphoreType.DMA((480,)),
+        pltpu.SemaphoreType.DMA((8,)),
+    ]
+    vmem = pl.BlockSpec(memory_space=pltpu.MemorySpace.VMEM)
+    smem = pl.BlockSpec(memory_space=pltpu.MemorySpace.SMEM)
+    shapes = (
+        jax.ShapeDtypeStruct((own_rows, width), low),
+        jax.ShapeDtypeStruct((own_rows, width), low),
+        jax.ShapeDtypeStruct((8, width), f32),
+        jax.ShapeDtypeStruct((rows, qkv_cols), f32),
+        jax.ShapeDtypeStruct((rows, out_cols), f32),
+        jax.ShapeDtypeStruct((rows, 2 * units), f32),
+        jax.ShapeDtypeStruct((strip, half), f32),
+    )
+    output, grad_tokens, gain_sums, final_qkv, final_out, final_gu, final_dt = pl.pallas_call(
+        functools.partial(layer_kernel, {}),
+        out_shape=shapes,
+        in_specs=[vmem, vmem, smem] + [vmem] * 7,
+        out_specs=[vmem] * 7,
+        scratch_shapes=scratch,
+        compiler_params=pltpu.CompilerParams(
+            collective_id=0, has_side_effects=True, vmem_limit_bytes=64 * 2**20
+        ),
+        name="layer",
+    )(
+        tokens.reshape(own_rows, width), cotangent.reshape(own_rows, width), lengths,
+        w_qkv, w_out, w_gate_up, w_down.T, gains, cosine, sine,
+    )
+    mine = lax.dynamic_slice(gain_sums, (0, lax.axis_index("dp") * block), (8, block))
+    return (
+        output.reshape(tokens.shape), grad_tokens.reshape(tokens.shape),
+        mine[0], final_qkv, final_out, mine[1], final_gu, final_dt.T,
+    )
+
+
 def solution(mesh):
+    fits = mesh.shape["dp"] == 8 and mesh.shape["ctx"] == 4
     return jax.shard_map(
-        on_device,
+        on_device_fast if fits else on_device,
         mesh=mesh,
         in_specs=(
             P("dp", "ctx", None),

time: 1040 us -> 321 us (0.31)
  waiting for transfers between devices: 614 us -> 0 us
  Pallas kernels: 0 us -> 309 us
  blocking collectives: 143 us -> 0 us
  local copies, waits for them, and re-layouts: 116 us -> 10.8 us
  matrix products: 97.4 us -> 0 us
  other arithmetic: 36.5 us -> 0.77 us
  between operations: 17.2 us -> 0.7 us
    all_gather x9 -> x0, waiting for transfers between devices: 375 us -> none  [the longest x1 193 us: on_device(): lax.all_gather(forward_wide[2], 'dp', axis=0, tiled=True)]
    pallas_call x0 -> x1, Pallas kernels: none -> 309 us  [on_device_fast(): pl.pallas_call(functools.partial(layer_kernel, {}), out_shape=shapes, in_...]
    reduce_scatter x4 -> x0, waiting for transfers between devices: 149 us -> none  [the longest x1 80.1 us: on_device(): lax.psum_scatter(column_grads[2].astype(jnp.bfloat16), 'dp', scatter_dime...]
    dot_general x96 -> x0, matrix products: 97.4 us -> none  [the longest x4 15.5 us: on_device(): jnp.einsum('bsr,bsc->rc', piece, right, preferred_element_type=jnp.float32)]
    unnamed x17 -> x0, waiting for transfers between devices: 90.3 us -> none
    all_to_all x3 -> x0, blocking collectives: 48.5 us -> none  [the longest x1 23.3 us: on_device(): lax.all_to_all(grad_mix, 'ctx', split_axis=2, concat_axis=1, tiled=True)]
    unnamed x2 -> x0, blocking collectives: 43.5 us -> none
    all_gather x5 -> x0, blocking collectives: 40.8 us -> none  [the longest x1 9.28 us: on_device(): lax.all_gather(w_out, 'ctx', axis=1, tiled=True)]
  transfers between devices with their start and end apart: 16 -> 0, of which waited for: 12 -> 0; matrix products, arithmetic and copies ran while one was open for 13% -> 0% of each run, Pallas kernels for 0% -> 0%
where the time goes in v2:
time: 321 us
  Pallas kernels  309 us (96%)
  local copies, waits for them, and re-layouts  10.8 us (3%)
    pallas_call x1, Pallas kernels, on_device_fast(): pl.pallas_call(functools.partial(layer_kernel, {}), out_shape=shapes, in_...  309 us
    unnamed x20, local copies, waits for them, and re-layouts  7.56 us

profile of v2, /device:TPU:0, one launch (start us, length us, event | category | flops | bytes accessed | tf_op | source)
XLA Modules:
  0.0 320.9 jit_solution(8041884071120817793)
XLA Ops:
  0.7 0.0 copy-start.5
  0.7 0.6 copy-done.5
  1.3 0.0 copy-start.6
  1.3 0.6 copy-done.6
  2.0 0.6 fusion.7.gain_in
  2.6 0.1 fusion.5
  2.7 0.1 copy.17
  2.9 0.8 tile.21.sin
  3.7 0.1 tile.9
  3.8 0.7 copy.18.cos
  4.5 308.7 %layer.1 = (bf16[128,1152]{1,0:T(8,128)(2,1)}, bf16[128,1152]{1,0:T(8,128)(2,1)}, f32[8,1152]{1,0:T(8,128)}, f32[144,480]{1,0:T(8,128)}, f32[144,288]{1,0:T(8,12...) custom-call(bf16[128,1152]{1,0:T(8,128)(2,1)} %bitcast.13, bf16[128,1152]{1,0:T(8,128)(2,1)} %bitcast.14, s32[2]{0:T(128)} %lengths.1, ...), custom_call_target="tpu_custom_call" | custom-call | tf_op jit(solution)/shard_map/layer/pallas_call | solution.py:1247
  313.2 1.4 fusion.8
  314.6 0.0 copy-start.3
  314.7 0.0 copy-start.2
  314.7 1.8 copy.25
  316.4 0.0 copy-done.3
  316.4 0.0 copy-start
  316.4 0.7 copy.26
  317.1 0.0 copy-done.2
  317.1 0.0 copy-start.4
  317.1 0.7 copy.27
  317.9 0.3 copy-done.4
  318.2 0.7 copy.28
  318.9 0.0 copy-done
  318.9 0.0 copy-start.1
  318.9 0.9 copy.29
  319.8 0.4 copy-done.1
  320.2 0.8 copy.30
  (7 shorter events, 0.1 us)
Async XLA Ops:
  0.7 0.7 copy-start.5
  1.3 0.7 copy-start.6
  314.6 1.8 copy-start.3
  314.7 2.5 copy-start.2
  316.4 2.5 copy-start
  317.1 1.0 copy-start.4
  318.9 1.3 copy-start.1

commit v3 on v2

--- a/solution.py
+++ b/solution.py
@@ -479,24 +479,6 @@
 DRAIN = [(way, dist) for dist in (3, 2, 1, 0) for way in (BELOW, ABOVE)]
 
 
-def sink_step(wires, place, name, block, inbox, way, dist):
-    here = source_valid(place, way, dist)
-    pos = source_pos(place, way, dist)
-    view = block(pos)
-    fed = place.has_up if way == BELOW else place.has_down
-    feeder = place.up if way == BELOW else place.down
-    onward = place.down if way == BELOW else place.up
-    if dist < 3:
-
-        def arrive():
-            wires.take(inbox.at[way, dist], (name, way, dist), feeder)
-            add_rows(view, [inbox.at[way, dist]])
-
-        pl.when(jnp.logical_and(here, fed))(arrive)
-    if dist > 0:
-        wires.send(view, inbox.at[way, dist - 1], (name, way, dist - 1), onward, here)
-
-
 def nn(a, b):
     return jnp.dot(a, b, preferred_element_type=jnp.float32)
 
@@ -581,7 +563,6 @@
     gain_block = lambda pos: gain_all.at[pos]
     gain_all[dp] = gain_in[...]
     flood_start(wires, place, "gain", gain_block(dp), gain_block, no_spread)
-    attention_start(*attention[1])
 
     lanes = pl.ds(pl.multiple_of(down_at + y * half, 128), half)
     other_lanes = pl.ds(pl.multiple_of(down_at + (1 - y) * half, 128), half)
@@ -624,7 +605,6 @@
     gu_blocks = [functools.partial(ff_view, at) for at, _ in gu_places]
     for part in range(2):
         flood_start(wires, place, ("gu", part), gu_blocks[part](dp), gu_blocks[part], no_spread)
-    share("cot", g_all)
 
     at_home = ctx == z
     strips = [w_ff.at[pl.ds(j * strip, strip), lanes] for j in range(4)]
@@ -639,7 +619,7 @@
         for j in range(4):
             wires.send(strips[j], strips[j], ("down", j, BELOW, 1), place.up, jnp.logical_and(at_home, place.has_up))
             wires.send(strips[j], strips[j], ("down", j, ABOVE, 1), place.down, jnp.logical_and(at_home, place.has_down))
-            wires.send(strips[j], strips[j], ("down_y", j), place.across, at_home)
+            wires.send(strips[j], strips[j], ("down_y", j, 0, 0), place.across, at_home)
 
     def down_step(way, dist):
         offset = z - ctx if way == BELOW else ctx - z
@@ -651,67 +631,96 @@
             pl.when(here)(functools.partial(wires.take, strips[j], ("down", j, way, dist), came_from))
             if dist < 3:
                 wires.send(strips[j], strips[j], ("down", j, way, dist + 1), onward, jnp.logical_and(here, more))
-            wires.send(strips[j], strips[j], ("down_y", j), place.across, here)
-
-    def attention_step(way, dist):
-        for name, own, ref, cols in attention:
+            wires.send(strips[j], strips[j], ("down_y", j, way, dist), place.across, here)
+
+    SIDES = [(0, 0)] + HOPS
+    WAYS = {0: [(0, 0)], 1: HOPS[:2], 2: HOPS[2:4], 3: HOPS[4:]}
+    att_w, out_w = attention
+
+    def hop(which, dist):
+        name, own, ref, cols = which
+        for way, dist in WAYS[dist]:
             flood_step(wires, place, name, functools.partial(row_view, ref, ctx), attention_spread(name, ref), way, dist)
 
-    def gain_step(way, dist):
-        flood_step(wires, place, "gain", gain_block, no_spread, way, dist)
-
-    def gu_step(way, dist):
-        for part in range(2):
-            flood_step(wires, place, ("gu", part), gu_blocks[part], no_spread, way, dist)
-
-    SIDES = [(0, 0)] + HOPS
-
-    def positions():
-        for side in range(2):
-            for way, dist in SIDES:
-                if dist == 0:
-                    here, pos = None, dp
-                else:
-                    here, pos = source_valid(place, way, dist), source_pos(place, way, dist)
-                if side == 1:
-                    pos = pos + 1 - 2 * y
-                yield (side, way, dist), here, pos
-
-    def attention_sides(which):
+    def side(which, dist):
         name, own, ref, cols = which
-        for way, dist in SIDES:
+        for way, dist in WAYS[dist]:
             flood_side(wires, place, name, functools.partial(row_view, ref, ctx), attention_spread(name, ref), way, dist)
 
-    def attention_chip(which):
+    def gain_step(dist):
+        for way, dist in WAYS[dist]:
+            flood_step(wires, place, "gain", gain_block, no_spread, way, dist)
+
+    def ff_step(dist):
+        for way, dist in WAYS[dist]:
+            for part in range(2):
+                flood_step(wires, place, ("gu", part), gu_blocks[part], no_spread, way, dist)
+            down_step(way, dist)
+
+    def spots(column, dist):
+        for way, dist in WAYS[dist]:
+            if dist == 0:
+                here, pos = None, dp
+            else:
+                here, pos = source_valid(place, way, dist), source_pos(place, way, dist)
+            if column == 1:
+                pos = pos + 1 - 2 * y
+            yield (column, way, dist), here, pos
+
+    def chip(which, column, dist):
         name, own, ref, cols = which
-        for key, here, pos in positions():
+        for key, here, pos in spots(column, dist):
             view = row_view(ref, place.chip[1], pos)
             when(here, lambda: wires.take(view, (name, "x") + key, place.chip))
             wires.send(view, view, (name, "d") + key, place.core, here)
 
-    def attention_core(which):
+    def core(which):
         name, own, ref, cols = which
-        for key, here, pos in positions():
-            for mark, lead in (("c", place.core[1]), ("d", 3 - ctx)):
-                view = row_view(ref, lead, pos)
-                when(here, lambda: wires.take(view, (name, mark) + key, place.core))
+        for column in range(2):
+            for dist in range(4):
+                for key, here, pos in spots(column, dist):
+                    for mark, lead in (("c", place.core[1]), ("d", 3 - ctx)):
+                        view = row_view(ref, lead, pos)
+                        when(here, lambda: wires.take(view, (name, mark) + key, place.core))
 
     down_start()
-    for dist in (1, 2, 3):
-        for way in (BELOW, ABOVE):
-            attention_step(way, dist)
-            gain_step(way, dist)
-        for way in (BELOW, ABOVE):
-            gu_step(way, dist)
-            down_step(way, dist)
+    hop(att_w, 1)
+    gain_step(1)
+    side(att_w, 0)
+    attention_start(*out_w)
+    ff_step(1)
+    hop(att_w, 2)
+    gain_step(2)
+    side(att_w, 1)
+    chip(att_w, 0, 0)
+    chip(att_w, 0, 1)
+    hop(out_w, 1)
+    side(out_w, 0)
+    ff_step(2)
+    hop(att_w, 3)
+    gain_step(3)
+    side(att_w, 2)
+    chip(att_w, 1, 0)
+    chip(att_w, 0, 2)
+    hop(out_w, 2)
+    side(out_w, 1)
+    chip(out_w, 0, 0)
+    ff_step(3)
+    side(att_w, 3)
+    chip(att_w, 1, 1)
+    chip(att_w, 0, 3)
+    hop(out_w, 3)
+    side(out_w, 2)
+    chip(out_w, 0, 1)
+    chip(out_w, 1, 0)
     for way, dist in SIDES:
         flood_side(wires, place, "gain", gain_block, no_spread, way, dist)
-    attention_sides(attention[0])
-    share_on("cot", g_all)
-    attention_chip(attention[0])
-    attention_core(attention[0])
-    attention_sides(attention[1])
-    attention_chip(attention[1])
+    chip(att_w, 1, 2)
+    chip(att_w, 1, 3)
+    side(out_w, 3)
+    chip(out_w, 0, 2)
+    chip(out_w, 1, 1)
+    core(att_w)
 
     gain_row[...] = jnp.zeros(gain_row.shape, f32)
     for pos in range(8):
@@ -801,7 +810,10 @@
 
     for step in (1, 2, 3):
         wires.send(slot_view(ctx), slot_view(ctx), ("kv", step), (dp, lax.rem(ctx + step, 4)))
-    attention_core(attention[1])
+    share("cot", g_all)
+    chip(out_w, 0, 3)
+    chip(out_w, 1, 2)
+    chip(out_w, 1, 3)
     for step in (1, 2, 3):
         peer = lax.rem(ctx + 4 - step, 4)
         wires.take(slot_view(peer), ("kv", step), (dp, peer))
@@ -824,6 +836,7 @@
         return carry
 
     lax.fori_loop(0, 2 * slabs, attend, 0)
+    core(out_w)
     for slab in range(q_slabs):
         context[:, slab * 128 : slab * 128 + 128] = unstack_heads(att, slab).astype(low)
     hidden[...] = source
@@ -835,16 +848,23 @@
         hidden[:, at // 128 * 128 : at // 128 * 128 + out_wide] += part
     n2_all[here_rows, :] = (hidden[...] * norm(hidden[...]) * gain_b()).astype(low)
     share("n2", n2_all)
-    share_end("cot", g_all)
+    share_on("cot", g_all)
 
     gathered = len(wires.pending)
 
     for part in range(2):
         for way, dist in SIDES:
             flood_side(wires, place, ("gu", part), gu_blocks[part], no_spread, way, dist)
-    for j in range(4):
-        wires.take(other_strips[j], ("down_y", j), place.across)
+    for way, dist in SIDES:
+        here = at_home if dist == 0 else (z - ctx if way == BELOW else ctx - z) == dist
+
+        def side_strips():
+            for j in range(4):
+                wires.take(other_strips[j], ("down_y", j, way, dist), place.across)
+
+        pl.when(here)(side_strips)
     share_on("n2", n2_all)
+    share_end("cot", g_all)
     share_end("n2", n2_all)
 
     tall, tile = 256, 256
@@ -874,10 +894,10 @@
     wide_tile = 384
 
     def group_blocks(compute, name, ref, box):
-        for mark, lead in (("cx", across_core), ("", across_own), ("cc", beside), ("", ctx)):
-            compute(lead)
-            if mark:
-                wires.send(ref.at[lead], box.at[0 if mark == "cx" else 1], (name, mark), place.core)
+        compute(1 - x)
+        wires.send(ref.at[across_core], box.at[0], (name, "cx"), place.core)
+        compute(x)
+        wires.send(ref.at[beside], box.at[1], (name, "cc"), place.core)
 
     def group_on(name, ref, box):
         wires.take(box.at[0], (name, "cx"), place.core)
@@ -892,28 +912,32 @@
     def add_any(dst, src):
         dst[...] = (dst[...].astype(f32) + src[...].astype(f32)).astype(low)
 
-    def lead_rows(lead):
-        return pl.ds(pl.multiple_of(lead * own_rows, 16), own_rows)
-
-    def back_block(lead):
+    def pair_rows(half_x):
+        return pl.ds(pl.multiple_of(half_x * 2 * own_rows, 16), 2 * own_rows)
+
+    def back_block(half_x):
         def body(n, carry):
             at = pl.ds(pl.multiple_of(n * wide_tile, 128), wide_tile)
-            total = nt(d_gate[lead_rows(lead), :], w_ff[at, pl.ds(gate_at, units)])
-            total = total + nt(d_up[lead_rows(lead), :], w_ff[at, pl.ds(up_at, units)])
-            gp[lead, :, at] = total.astype(low)
+            total = nt(d_gate[pair_rows(half_x), :], w_ff[at, pl.ds(gate_at, units)])
+            total = total + nt(d_up[pair_rows(half_x), :], w_ff[at, pl.ds(up_at, units)])
+            gp[2 * half_x, :, at] = total[:own_rows].astype(low)
+            gp[2 * half_x + 1, :, at] = total[own_rows:].astype(low)
             return carry
 
         lax.fori_loop(0, width // wide_tile, body, 0)
 
-    def forward_block(lead):
+    def forward_block(half_x):
         def body(n, carry):
             at = pl.ds(pl.multiple_of(n * wide_tile, 128), wide_tile)
-            op[lead, :, at] = nt(act[lead_rows(lead), :], w_ff[at, pl.ds(down_at, units)]).astype(low)
+            total = nt(act[pair_rows(half_x), :], w_ff[at, pl.ds(down_at, units)])
+            op[2 * half_x, :, at] = total[:own_rows].astype(low)
+            op[2 * half_x + 1, :, at] = total[own_rows:].astype(low)
             return carry
 
         lax.fori_loop(0, width // wide_tile, body, 0)
 
     group_blocks(back_block, "gp", gp, gp_box)
+    group_on("gp", gp, gp_box)
 
     def grad_ff(m, carry):
         at = pl.ds(pl.multiple_of(m * 128, 128), 128)
@@ -924,17 +948,129 @@
         return carry
 
     lax.fori_loop(0, width // 128, grad_ff, 0)
-    group_on("gp", gp, gp_box)
 
     d_lanes = pl.ds(pl.multiple_of(y * half, 128), half)
     d_other = pl.ds(pl.multiple_of((1 - y) * half, 128), half)
     d_strips = [d_dt.at[pl.ds(j * strip, strip), d_lanes] for j in range(4)]
     d_other_strips = [d_dt.at[pl.ds(j * strip, strip), d_other] for j in range(4)]
-    for zs in range(4):
+    def key_pos(way, dist):
+        if dist == 0:
+            return None, dp
+        return source_valid(place, way, dist), source_pos(place, way, dist)
+
+    KEYS = {3: DRAIN[:2], 2: DRAIN[2:4], 1: DRAIN[4:6], 0: [(BELOW, 0)]}
+    flip = 1 - 2 * y
+
+    def gu_send(dist):
+        for way, dist in KEYS[dist]:
+            here, pos = key_pos(way, dist)
+            for part in range(2):
+                wires.send(
+                    row_view(d_gu, part, pos + flip), gu_side.at[part, way, dist],
+                    (("dgu", part), "y", way, dist), place.across, here,
+                )
+
+    def z_add(name, view, boxes, inbox, way, dist):
+        here, pos = key_pos(way, dist)
+        mine = view(pos)
+        if dist == 0:
+            wires.take(boxes.at[way, dist], (name, "y", way, dist), place.across)
+            add_rows(mine, [boxes.at[way, dist]])
+            for end, fed, feeder in ((BELOW, place.has_up, place.up), (ABOVE, place.has_down, place.down)):
+
+                def own():
+                    wires.take(inbox.at[end, 0], (name, "z", end, 0), feeder)
+                    add_rows(mine, [inbox.at[end, 0]])
+
+                pl.when(fed)(own)
+            return
+        fed = place.has_up if way == BELOW else place.has_down
+        feeder = place.up if way == BELOW else place.down
+        onward = place.down if way == BELOW else place.up
+        side = boxes.at[way, dist]
+
+        def first():
+            wires.take(side, (name, "y", way, dist), place.across)
+            add_rows(mine, [side])
+
+        if dist == 3:
+            pl.when(here)(first)
+        else:
+
+            def more():
+                wires.take(side, (name, "y", way, dist), place.across)
+                wires.take(inbox.at[way, dist], (name, "z", way, dist), feeder)
+                add_rows(mine, [side, inbox.at[way, dist]])
+
+            pl.when(jnp.logical_and(here, jnp.logical_not(fed)))(first)
+            pl.when(jnp.logical_and(here, fed))(more)
+        wires.send(mine, inbox.at[way, dist - 1], (name, "z", way, dist - 1), onward, here)
+
+    def gu_add(dist):
+        for way, dist in KEYS[dist]:
+            for part in range(2):
+                z_add(("dgu", part), functools.partial(row_view, d_gu, part), gu_side.at[part], gu_inbox.at[part], way, dist)
+
+    def down_send():
+        for j in range(4):
+            wires.send(d_other_strips[j], down_side.at[j], ("ddown_y", j), place.across)
+
+    def down_add(dist):
+        away = jnp.abs(z - ctx) == dist
+        if dist == 0:
+            for j in range(4):
+
+                def finish(j=j):
+                    wires.take(down_side.at[j], ("ddown_y", j), place.across)
+                    add_rows(d_strips[j], [down_side.at[j]])
+                    for end, fed, feeder in ((BELOW, place.has_up, place.up), (ABOVE, place.has_down, place.down)):
+
+                        def more():
+                            wires.take(down_inbox.at[end, j], ("ddown", j, end, 0), feeder)
+                            add_rows(d_strips[j], [down_inbox.at[end, j]])
+
+                        pl.when(fed)(more)
+
+                pl.when(away)(finish)
+            return
+        for way in (BELOW, ABOVE):
+            here = (z - ctx if way == BELOW else ctx - z) == dist
+            fed = place.has_up if way == BELOW else place.has_down
+            feeder = place.up if way == BELOW else place.down
+            onward = place.down if way == BELOW else place.up
+            for j in range(4):
+
+                def first():
+                    wires.take(down_side.at[j], ("ddown_y", j), place.across)
+                    add_rows(d_strips[j], [down_side.at[j]])
+
+                def more():
+                    wires.take(down_inbox.at[way, j], ("ddown", j, way, dist), feeder)
+                    add_rows(d_strips[j], [down_inbox.at[way, j]])
+
+                pl.when(here)(first)
+                pl.when(jnp.logical_and(here, fed))(more)
+                wires.send(d_strips[j], down_inbox.at[way, j], ("ddown", j, way, dist - 1), onward, here)
+
+    def ff_add(dist):
+        down_add(dist)
+        gu_add(dist)
+
+    def ff_finish():
         for part in range(2):
-            wires.send(row_view(d_gu, part, 2 * zs + 1 - y), gu_side.at[part, zs], ("dgu_y", part, zs), place.across)
-    for j in range(4):
-        wires.send(d_other_strips[j], down_side.at[j], ("ddown_y", j), place.across)
+            target = part * 2 + x
+            block = row_view(d_gu, part, dp)
+            wires.send(block, gu_mix.at[c], ("dgu_mix", 0), (dp, target), target != ctx, extra=c)
+            pl.when(target == ctx)(lambda: add_rows(block, [], out=gu_mix.at[c]))
+        wires.slot(("dgu_mix", 1))
+        for j in range(4):
+            wires.send(d_strips[j], down_mix, ("ddown_mix",), (dp, j), jnp.logical_and(at_home, ctx != j))
+            pl.when(jnp.logical_and(at_home, ctx == j))(functools.partial(add_rows, d_strips[j], [], down_mix))
+
+    gu_send(3)
+    down_send()
+    for dist in (2, 1, 0):
+        gu_send(dist)
 
     group_blocks(forward_block, "op", op, op_box)
     group_on("op", op, op_box)
@@ -985,40 +1121,50 @@
 
     lax.fori_loop(0, width // 128, grad_out, 0)
 
-    def core_send(name, view, core):
-        for zs in range(4):
-            for xx in range(2):
-                wires.send(
-                    view(2 * xx + 1 - c, zs * pair, pair), core.at[xx, pl.ds(zs * pair, pair)],
-                    (name, "gc", xx, zs), place.core,
-                )
-
-    def core_add(name, view, core, chip):
-        for zs in range(4):
-            for xx in range(2):
-                box = core.at[xx, pl.ds(zs * pair, pair)]
-                wires.take(box, (name, "gc", xx, zs), place.core)
-                add_rows(view(2 * xx + c, zs * pair, pair), [box])
-            wires.send(view(place.chip[1], zs * pair, pair), chip.at[pl.ds(zs * pair, pair)], (name, "gx", zs), place.chip)
+    def core_send(name, view, box):
+        for dist in (3, 2, 1, 0):
+            for way, dist in KEYS[dist]:
+                here, pos = key_pos(way, dist)
+                at = pl.multiple_of((pos - y) * rows, 16)
+                for xx in range(2):
+                    wires.send(
+                        view(2 * xx + 1 - c, at, pair), box.at[xx, pl.ds(at, pair)],
+                        (name, "gc", xx, way, dist), place.core, here,
+                    )
+
+    def core_add(name, view, box, chip_box, dist):
+        for way, dist in KEYS[dist]:
+            here, pos = key_pos(way, dist)
+            at = pl.multiple_of((pos - y) * rows, 16)
+
+            def add():
+                for xx in range(2):
+                    part = box.at[xx, pl.ds(at, pair)]
+                    wires.take(part, (name, "gc", xx, way, dist), place.core)
+                    add_rows(view(2 * xx + c, at, pair), [part])
+
+            when(here, add)
+            wires.send(view(place.chip[1], at, pair), chip_box.at[pl.ds(at, pair)], (name, "gx", way, dist), place.chip, here)
+
+    def chip_add(name, view, chip_box, side_box, dist):
+        for way, dist in KEYS[dist]:
+            here, pos = key_pos(way, dist)
+            at = pl.multiple_of((pos - y) * rows, 16)
+
+            def add():
+                span = chip_box.at[pl.ds(at, pair)]
+                wires.take(span, (name, "gx", way, dist), place.chip)
+                add_rows(view(ctx, at, pair), [span])
+
+            when(here, add)
+            wires.send(own_view(view, pos + flip), side_box.at[way, dist], ((name, "g"), "y", way, dist), place.across, here)
 
     def own_view(view, pos):
         return view(ctx, pl.multiple_of(pos * rows, 16), rows)
 
-    def chip_add(name, view, chip, side):
-        for zs in range(4):
-            span = chip.at[pl.ds(zs * pair, pair)]
-            wires.take(span, (name, "gx", zs), place.chip)
-            add_rows(view(ctx, zs * pair, pair), [span])
-            wires.send(own_view(view, 2 * zs + 1 - y), side.at[zs], (name, "gy", zs), place.across)
-
-    def side_add(name, view, side):
-        for zs in range(4):
-            wires.take(side.at[zs], (name, "gy", zs), place.across)
-            add_rows(own_view(view, 2 * zs + y), [side.at[zs]])
-
-    def drain_z(name, view, inbox):
-        for way, dist in DRAIN:
-            sink_step(wires, place, (name, "g"), functools.partial(own_view, view), inbox, way, dist)
+    def side_add(name, view, side_box, inbox, dist):
+        for way, dist in KEYS[dist]:
+            z_add((name, "g"), functools.partial(own_view, view), side_box, inbox, way, dist)
 
     core_send("out", out_view, out_core)
 
@@ -1039,17 +1185,12 @@
 
     lax.fori_loop(0, 2 * slabs, attend_back, 0)
     group_blocks(lambda lead: None, "dkv", dkv, dkv_box)
-    core_add("out", out_view, out_core, out_chip)
+    for dist in (3, 2, 1, 0):
+        core_add("out", out_view, out_core, out_chip, dist)
     group_on("dkv", dkv, dkv_box)
-
-    for zs in range(4):
-        for part in range(2):
-            wires.take(gu_side.at[part, zs], ("dgu_y", part, zs), place.across)
-            add_rows(row_view(d_gu, part, 2 * zs + y), [gu_side.at[part, zs]])
-    for j in range(4):
-        wires.take(down_side.at[j], ("ddown_y", j), place.across)
-        add_rows(d_strips[j], [down_side.at[j]])
-
+    ff_add(3)
+    for dist in (3, 2):
+        chip_add("out", out_view, out_chip, out_side, dist)
     sums = group_end("dkv", dkv, dkv_box)
     proj[...] = jnp.zeros(proj.shape, f32)
     for slab in range(q_slabs):
@@ -1076,7 +1217,11 @@
 
     lax.fori_loop(0, width // 128, grad_qkv, 0)
     core_send("qkv", qkv_view, qkv_core)
-    chip_add("out", out_view, out_chip, out_side)
+    ff_add(2)
+    for dist in (1, 0):
+        chip_add("out", out_view, out_chip, out_side, dist)
+    for dist in (3, 2, 1, 0):
+        core_add("qkv", qkv_view, qkv_core, qkv_chip, dist)
 
     def tokens_back(n, carry):
         at = pl.ds(pl.multiple_of(n * wide_tile, 128), wide_tile)
@@ -1087,7 +1232,6 @@
         return carry
 
     lax.fori_loop(0, width // wide_tile, tokens_back, 0)
-    core_add("qkv", qkv_view, qkv_core, qkv_chip)
     source = tokens[...].astype(f32)
     back_one, gain_one_grad = norm_back(source, norm(source), gain_a(), proj[:, :width])
     gain_out[0:1, :] = gain_one_grad
@@ -1095,45 +1239,6 @@
     result = hidden[...] + group_end("op", op, op_box)
     output[...] = jnp.where(valid, result, 0.0).astype(low)
 
-    def down_sink(dist):
-        for way in (BELOW, ABOVE):
-            offset = z - ctx if way == BELOW else ctx - z
-            here = offset == dist
-            fed = place.has_up if way == BELOW else place.has_down
-            feeder = place.up if way == BELOW else place.down
-            onward = place.down if way == BELOW else place.up
-            for j in range(4):
-
-                def arrive():
-                    wires.take(down_inbox.at[way, j], ("ddown", j, way), feeder)
-                    add_rows(d_strips[j], [down_inbox.at[way, j]])
-
-                pl.when(jnp.logical_and(here, fed))(arrive)
-                if dist > 0:
-                    wires.send(d_strips[j], down_inbox.at[way, j], ("ddown", j, way), onward, here)
-
-    for way, dist in DRAIN:
-        for part in range(2):
-            sink_step(wires, place, ("dgu", part), functools.partial(row_view, d_gu, part), gu_inbox.at[part], way, dist)
-        if way == BELOW:
-            down_sink(dist)
-    for part in range(2):
-        target = part * 2 + x
-        block = row_view(d_gu, part, dp)
-        wires.send(block, gu_mix.at[c], ("dgu_mix", 0), (dp, target), target != ctx, extra=c)
-        pl.when(target == ctx)(lambda: add_rows(block, [], out=gu_mix.at[c]))
-    wires.slot(("dgu_mix", 1))
-    for j in range(4):
-        wires.send(d_strips[j], down_mix, ("ddown_mix",), (dp, j), jnp.logical_and(at_home, ctx != j))
-        pl.when(jnp.logical_and(at_home, ctx == j))(functools.partial(add_rows, d_strips[j], [], down_mix))
-    chip_add("qkv", qkv_view, qkv_chip, qkv_side)
-    side_add("out", out_view, out_side)
-    drain_z("out", out_view, out_inbox)
-    side_add("qkv", qkv_view, qkv_side)
-    drain_z("qkv", qkv_view, qkv_inbox)
-    out_out[...] = own_view(out_view, dp)[...].astype(f32)[:, :out_cols]
-    qkv_out[...] = own_view(qkv_view, dp)[...].astype(f32)[:, :qkv_cols]
-
     def swap(slot, device, cond=None):
         wires.send(gain_out, gain_box.at[slot], ("gain_sum", slot), device, cond)
 
@@ -1145,40 +1250,67 @@
         copy, cond = wires.pending.pop()
         when(cond, copy.wait_send)
 
-    for slot, device in enumerate((place.core, place.chip, place.across)):
+    def gain_hop(slot):
+        device = (place.core, place.chip, place.across)[slot]
         swap(slot, device)
         settle()
         add_gain(slot, device)
+
     low_end, high_end = z == 0, z == 3
     mid_low, mid_high = z == 1, z == 2
-    swap(3, place.up, low_end)
-    settle()
-    swap(3, place.down, high_end)
-    settle()
-    pl.when(mid_low)(lambda: add_gain(3, place.down))
-    pl.when(mid_high)(lambda: add_gain(3, place.up))
-    swap(4, place.up, mid_low)
-    settle()
-    swap(4, place.down, mid_high)
-    settle()
-    pl.when(mid_low)(lambda: add_gain(4, place.up))
-    pl.when(mid_high)(lambda: add_gain(4, place.down))
-    swap(5, place.down, mid_low)
-    swap(5, place.up, mid_high)
+
+    def gain_hop_3():
+        swap(3, place.up, low_end)
+        settle()
+        swap(3, place.down, high_end)
+        settle()
+        pl.when(mid_low)(lambda: add_gain(3, place.down))
+        pl.when(mid_high)(lambda: add_gain(3, place.up))
+
+    def gain_hop_4():
+        swap(4, place.up, mid_low)
+        settle()
+        swap(4, place.down, mid_high)
+        settle()
+        pl.when(mid_low)(lambda: add_gain(4, place.up))
+        pl.when(mid_high)(lambda: add_gain(4, place.down))
+        swap(5, place.down, mid_low)
+        swap(5, place.up, mid_high)
 
     def last(device):
         wires.take(gain_box.at[5], ("gain_sum", 5), device)
         gain_out[...] = gain_box[5]
 
-    pl.when(low_end)(lambda: last(place.up))
-    pl.when(high_end)(lambda: last(place.down))
-
+    ff_add(1)
+    gain_hop(0)
+    chip_add("qkv", qkv_view, qkv_chip, qkv_side, 3)
+    side_add("out", out_view, out_side, out_inbox, 3)
+    gain_hop(1)
+    ff_add(0)
+    ff_finish()
+    chip_add("qkv", qkv_view, qkv_chip, qkv_side, 2)
+    side_add("out", out_view, out_side, out_inbox, 2)
+    gain_hop(2)
+    side_add("qkv", qkv_view, qkv_side, qkv_inbox, 3)
+    chip_add("qkv", qkv_view, qkv_chip, qkv_side, 1)
+    side_add("out", out_view, out_side, out_inbox, 1)
+    gain_hop_3()
+    side_add("qkv", qkv_view, qkv_side, qkv_inbox, 2)
+    chip_add("qkv", qkv_view, qkv_chip, qkv_side, 0)
+    side_add("out", out_view, out_side, out_inbox, 0)
+    out_out[...] = own_view(out_view, dp)[...].astype(f32)[:, :out_cols]
+    gain_hop_4()
     for part in range(2):
         origin = 2 * c + part
         pl.when(origin != ctx)(lambda: wires.take(gu_mix.at[part], ("dgu_mix", part), (dp, origin)))
         add_rows(gu_mix.at[part], [], out=gu_out.at[:, pl.ds(part * units, units)])
     pl.when(ctx != z)(lambda: wires.take(down_mix, ("ddown_mix",), (dp, z)))
     add_rows(down_mix, [], out=dt_out)
+    pl.when(low_end)(lambda: last(place.up))
+    pl.when(high_end)(lambda: last(place.down))
+    side_add("qkv", qkv_view, qkv_side, qkv_inbox, 1)
+    side_add("qkv", qkv_view, qkv_side, qkv_inbox, 0)
+    qkv_out[...] = own_view(qkv_view, dp)[...].astype(f32)[:, :qkv_cols]
     wires.drain()
 
 
@@ -1223,8 +1355,8 @@
         box(2, deep, units), box(deep, units),
         box(2, deep, qkv_wide), box(2, deep, out_wide),
         box(deep, qkv_wide), box(deep, out_wide),
-        box(4, rows, qkv_wide), box(4, rows, out_wide),
-        box(2, 4, rows, units), box(4, strip, half),
+        box(2, 4, rows, qkv_wide), box(2, 4, rows, out_wide),
+        box(2, 2, 4, rows, units), box(4, strip, half),
         box(2, 3, rows, qkv_wide), box(2, 3, rows, out_wide),
         box(2, 2, 3, rows, units), box(2, 4, strip, half),
         box(2, rows, units), box(strip, half),

time: 321 us -> 254 us (0.79)
  Pallas kernels: 309 us -> 239 us
    pallas_call x1, Pallas kernels: 309 us -> 239 us  [on_device_fast(): pl.pallas_call(functools.partial(layer_kernel, {}), out_shape=shapes, in_...]
where the time goes in v3:
time: 254 us; the launch traced here: 251 us
  Pallas kernels  239 us (94%)
  local copies, waits for them, and re-layouts  10.8 us (4%)
    pallas_call x1, Pallas kernels, on_device_fast(): pl.pallas_call(functools.partial(layer_kernel, {}), out_shape=shapes, in_...  239 us
    unnamed x20, local copies, waits for them, and re-layouts  7.56 us

profile of v3, /device:TPU:0, one launch (start us, length us, event | category | flops | bytes accessed | tf_op | source)
XLA Modules:
  0.0 250.9 jit_solution(5388136174817944949)
XLA Ops:
  0.7 0.0 copy-start.5
  0.7 0.6 copy-done.5
  1.3 0.0 copy-start.6
  1.3 0.6 copy-done.6
  2.0 0.6 fusion.7.gain_in
  2.6 0.1 fusion.5
  2.7 0.1 copy.17
  2.9 0.8 tile.21.sin
  3.7 0.1 tile.9
  3.8 0.7 copy.18.cos
  4.5 238.7 %layer.1 = (bf16[128,1152]{1,0:T(8,128)(2,1)}, bf16[128,1152]{1,0:T(8,128)(2,1)}, f32[8,1152]{1,0:T(8,128)}, f32[144,480]{1,0:T(8,128)}, f32[144,288]{1,0:T(8,12...) custom-call(bf16[128,1152]{1,0:T(8,128)(2,1)} %bitcast.13, bf16[128,1152]{1,0:T(8,128)(2,1)} %bitcast.14, s32[2]{0:T(128)} %lengths.1, ...), custom_call_target="tpu_custom_call" | custom-call | tf_op jit(solution)/shard_map/layer/pallas_call | solution.py:1379
  243.2 1.4 fusion.8
  244.7 0.0 copy-start.3
  244.7 0.0 copy-start.2
  244.7 1.8 copy.25
  246.4 0.0 copy-done.3
  246.4 0.0 copy-start
  246.4 0.7 copy.26
  247.2 0.0 copy-done.2
  247.2 0.0 copy-start.4
  247.2 0.7 copy.27
  247.9 0.3 copy-done.4
  248.2 0.7 copy.28
  248.9 0.0 copy-done
  248.9 0.0 copy-start.1
  248.9 0.9 copy.29
  249.8 0.4 copy-done.1
  250.2 0.8 copy.30
  (7 shorter events, 0.1 us)
Async XLA Ops:
  0.7 0.7 copy-start.5
  1.3 0.7 copy-start.6
  244.7 1.8 copy-start.3
  244.7 2.5 copy-start.2
  246.4 2.5 copy-start
  247.2 1.0 copy-start.4
  248.9 1.3 copy-start.1

commit v4 on v0

--- a/solution.py
+++ b/solution.py
@@ -1,8 +1,11 @@
+import functools
 import math
 
 import jax
 import jax.numpy as jnp
 from jax import lax
+from jax.experimental import pallas as pl
+from jax.experimental.pallas import tpu as pltpu
 from jax.sharding import PartitionSpec as P
 
 QH = 18
@@ -305,9 +308,1284 @@
     )
 
 
+MESH = pl.DeviceIdType.MESH
+
+
+class Place:
+    def __init__(self):
+        self.dp = lax.axis_index("dp")
+        self.ctx = lax.axis_index("ctx")
+        self.z = lax.div(self.dp, 2)
+        self.y = lax.rem(self.dp, 2)
+        self.x = lax.div(self.ctx, 2)
+        self.c = lax.rem(self.ctx, 2)
+        self.up = (self.dp + 2, self.ctx)
+        self.down = (self.dp - 2, self.ctx)
+        self.across = (self.dp + 1 - 2 * self.y, self.ctx)
+        self.chip = (self.dp, (1 - self.x) * 2 + self.c)
+        self.core = (self.dp, self.x * 2 + 1 - self.c)
+        self.has_up = self.z < 3
+        self.has_down = self.z > 0
+
+
+def greet(place):
+    barrier = pltpu.get_barrier_semaphore()
+
+    def tell(device):
+        pl.semaphore_signal(barrier, inc=1, device_id=device, device_id_type=MESH)
+
+    pl.when(place.has_up)(lambda: tell(place.up))
+    pl.when(place.has_down)(lambda: tell(place.down))
+    tell(place.across)
+    for step in (1, 2, 3):
+        tell((place.dp, lax.rem(place.ctx + step, 4)))
+    ends = place.has_up.astype(jnp.int32) + place.has_down.astype(jnp.int32)
+    pl.semaphore_wait(barrier, 4 + ends)
+
+
+class Wires:
+    def __init__(self, send_sems, recv_sems, names):
+        self.send_sems = send_sems
+        self.recv_sems = recv_sems
+        self.index = names
+        self.count = 0
+        self.pending = []
+
+    def slot(self, name):
+        if name not in self.index:
+            self.index[name] = len(self.index)
+        return self.index[name]
+
+    def send(self, src, dst, name, device, cond=None, extra=None):
+        number = self.count
+        self.count += 1
+        at = self.slot(name)
+        if extra is not None:
+            at = at + extra
+        copy = pltpu.make_async_remote_copy(
+            src_ref=src,
+            dst_ref=dst,
+            send_sem=self.send_sems.at[number],
+            recv_sem=self.recv_sems.at[at],
+            device_id=device,
+            device_id_type=MESH,
+        )
+        if cond is None:
+            copy.start()
+        else:
+            pl.when(cond)(copy.start)
+        self.pending.append((copy, cond, name))
+
+    def take(self, dst, name, device, extra=None):
+        at = self.slot(name)
+        if extra is not None:
+            at = at + extra
+        pltpu.make_async_remote_copy(
+            src_ref=dst,
+            dst_ref=dst,
+            send_sem=self.send_sems.at[0],
+            recv_sem=self.recv_sems.at[at],
+            device_id=device,
+            device_id_type=MESH,
+        ).wait_recv()
+
+    def drain(self):
+        for copy, cond, name in self.pending:
+            when(cond, copy.wait_send)
+        self.pending = []
+
+    def drain_named(self, first):
+        for copy, cond, name in self.pending:
+            if name[0] == first:
+                when(cond, copy.wait_send)
+        self.pending = [entry for entry in self.pending if entry[2][0] != first]
+
+
+BELOW, ABOVE = 0, 1
+
+
+def both(first, second):
+    return second if first is None else jnp.logical_and(first, second)
+
+
+def source_valid(place, way, dist):
+    return place.z >= dist if way == BELOW else place.z + dist <= 3
+
+
+def source_pos(place, way, dist):
+    return place.dp - 2 * dist if way == BELOW else place.dp + 2 * dist
+
+
+def flood_start(wires, place, name, own, block, spread):
+    wires.send(own, block(place.dp), (name, BELOW, 1), place.up, place.has_up)
+    wires.send(own, block(place.dp), (name, ABOVE, 1), place.down, place.has_down)
+    wires.send(own, block(place.dp), (name, "y", 0, 0), place.across)
+    spread(own, place.dp, (0, 0, 0), None)
+
+
+def flood_step(wires, place, name, block, spread, way, dist):
+    here = source_valid(place, way, dist)
+    pos = source_pos(place, way, dist)
+    view = block(pos)
+    came_from = place.down if way == BELOW else place.up
+    pl.when(here)(lambda: wires.take(view, (name, way, dist), came_from))
+    if dist < 3:
+        onward = place.up if way == BELOW else place.down
+        more = place.has_up if way == BELOW else place.has_down
+        wires.send(view, view, (name, way, dist + 1), onward, jnp.logical_and(here, more))
+    wires.send(view, view, (name, "y", way, dist), place.across, here)
+    spread(view, pos, (0, way, dist), here)
+
+
+def flood_side(wires, place, name, block, spread, way, dist):
+    if dist == 0:
+        here, pos = None, place.dp
+    else:
+        here, pos = source_valid(place, way, dist), source_pos(place, way, dist)
+    pos = pos + 1 - 2 * place.y
+    view = block(pos)
+    if here is None:
+        wires.take(view, (name, "y", 0, 0), place.across)
+    else:
+        pl.when(here)(lambda: wires.take(view, (name, "y", way, dist), place.across))
+    spread(view, pos, (1, way, dist), here)
+
+
+HOPS = [(way, dist) for dist in (1, 2, 3) for way in (BELOW, ABOVE)]
+
+
+def no_spread(view, pos, key, cond):
+    return None
+
+
+def add_rows(dst, srcs, out=None, cast=None, chunk=48):
+    out = dst if out is None else out
+    total_rows = dst.shape[0]
+    assert total_rows % chunk == 0
+
+    def body(i, carry):
+        at = pl.ds(pl.multiple_of(i * chunk, 16), chunk)
+        total = dst[at, :].astype(jnp.float32)
+        for src in srcs:
+            total = total + src[at, :].astype(jnp.float32)
+        out[at, :] = total.astype(out.dtype)
+        return carry
+
+    lax.fori_loop(0, total_rows // chunk, body, 0)
+
+
+def when(cond, action):
+    if cond is None:
+        action()
+    else:
+        pl.when(cond)(action)
+
+
+DRAIN = [(way, dist) for dist in (3, 2, 1, 0) for way in (BELOW, ABOVE)]
+
+
+def nn(a, b):
+    return jnp.dot(a, b, preferred_element_type=jnp.float32)
+
+
+def nt(a, b):
+    return lax.dot_general(a, b, (((1,), (1,)), ((), ())), preferred_element_type=jnp.float32)
+
+
+def tn(a, b):
+    return lax.dot_general(a, b, (((0,), (0,)), ((), ())), preferred_element_type=jnp.float32)
+
+
+def layer_kernel(
+    names,
+    tokens, cot, lengths, qkv_in, out_in, gu_in, dt_in, gain_in, cos, sin,
+    output, grad_tokens, gain_out, qkv_out, out_out, gu_out, dt_out,
+    w_qkv, w_out, w_ff, d_qkv, d_out, d_ff, gain_all, gain_row,
+    tok_all, n1_all, n2_all, g_all, ctx_all, hidden, grad_hidden, proj, q_st, kv_all, p_st, att, go_st,
+    wide, gm, pq, pq_in, gb_all, gm_all, act, d_gu, gp, gp_box, op, op_box, dkv, dkv_box,
+    qkv_side, out_side, gu_side_a, gu_side_b, down_side, qkv_inbox, out_inbox, gu_inbox_a, gu_inbox_b, down_inbox,
+    up_inbox, up_side, gu_mix, down_mix, gain_box, gain_acc,
+    send_sems, recv_sems, local_sems,
+):
+    f32, low = jnp.float32, jnp.bfloat16
+    place = Place()
+    wires = Wires(send_sems, recv_sems, names)
+    dp, ctx, z, y, x, c = place.dp, place.ctx, place.z, place.y, place.x, place.c
+    rows = qkv_in.shape[0]
+    strip, half = dt_in.shape
+    width = tokens.shape[1]
+    own_rows = tokens.shape[0]
+    slots_here = own_rows // 2
+    qkv_cols, out_cols = qkv_in.shape[1], out_in.shape[1]
+    qkv_wide, out_wide = w_qkv.shape[1], w_out.shape[2]
+    group = QH // KVH
+    slabs = KVH // 2
+    q_slabs = QH // 2
+    span = 3 * half
+    deep = w_ff.shape[0]
+    score_scale = 1.0 / math.sqrt(HD)
+    TILES = range(2)
+
+    greet(place)
+
+    def block_rows(pos):
+        return pl.ds(pl.multiple_of(pos * rows, 16), rows)
+
+    def lead_rows(lead):
+        return pl.ds(pl.multiple_of(lead * own_rows, 16), own_rows)
+
+    here_rows = lead_rows(ctx)
+    my_rows = block_rows(dp)
+
+    def share(name, ref):
+        mine = ref.at[here_rows]
+        wires.send(mine, mine, (name, "x"), place.chip)
+        wires.send(mine, mine, (name, "c"), place.core)
+
+    def share_on(name, ref):
+        far = ref.at[lead_rows(place.chip[1])]
+        wires.take(far, (name, "x"), place.chip)
+        wires.send(far, far, (name, "d"), place.core)
+
+    def share_end(name, ref):
+        for mark, lead in (("c", place.core[1]), ("d", 3 - ctx)):
+            wires.take(ref.at[lead_rows(lead)], (name, mark), place.core)
+
+    def swap_start(name, src, dst):
+        for step in (1, 2, 3):
+            peer = lax.rem(ctx + step, 4)
+            wires.send(src(peer), dst(ctx), (name, step), (dp, peer))
+
+    def swap_end(name, dst):
+        for step in (1, 2, 3):
+            peer = lax.rem(ctx + 4 - step, 4)
+            wires.take(dst(peer), (name, step), (dp, peer))
+
+    locals_ = []
+
+    def local(src, dst, cond=None):
+        copy = pltpu.make_async_copy(src, dst, local_sems.at[len(locals_)])
+        locals_.append((copy, cond))
+        when(cond, copy.start)
+
+    SIDES = [(0, 0)] + HOPS
+    WAYS = {0: [(0, 0)], 1: HOPS[:2], 2: HOPS[2:4], 3: HOPS[4:]}
+
+    class Flood:
+        def __init__(self, name, block, spread=no_spread):
+            self.name, self.block, self.spread = name, block, spread
+
+        def start(self):
+            flood_start(wires, place, self.name, self.block(dp), self.block, self.spread)
+
+        def hop(self, dist):
+            for way, dist in WAYS[dist]:
+                flood_step(wires, place, self.name, self.block, self.spread, way, dist)
+
+        def side(self, dist):
+            for way, dist in WAYS[dist]:
+                flood_side(wires, place, self.name, self.block, self.spread, way, dist)
+
+    class PairFlood:
+        def __init__(self, name, ref, cols):
+            self.name, self.ref, self.cols = name, ref, cols
+
+        def pair(self, plane):
+            return self.ref.at[pl.ds(pl.multiple_of(2 * rows * plane, 16), 2 * rows), self.cols]
+
+        def one(self, pos):
+            return self.ref.at[block_rows(pos), self.cols]
+
+        def start(self):
+            wires.send(self.one(dp), self.one(dp), (self.name, "y"), place.across)
+
+        def side(self):
+            wires.take(self.one(place.across[0]), (self.name, "y"), place.across)
+            view = self.pair(z)
+            wires.send(view, view, (self.name, BELOW, 1), place.up, place.has_up)
+            wires.send(view, view, (self.name, ABOVE, 1), place.down, place.has_down)
+
+        def hop(self, dist):
+            for way, dist in WAYS[dist]:
+                here = source_valid(place, way, dist)
+                view = self.pair(z - dist if way == BELOW else z + dist)
+                came_from = place.down if way == BELOW else place.up
+                pl.when(here)(lambda: wires.take(view, (self.name, way, dist), came_from))
+                if dist < 3:
+                    onward = place.up if way == BELOW else place.down
+                    more = place.has_up if way == BELOW else place.has_down
+                    wires.send(view, view, (self.name, way, dist + 1), onward, jnp.logical_and(here, more))
+
+    def out_block(lead, pos):
+        return w_out.at[lead, block_rows(pos)]
+
+    def out_spread(view, pos, key, cond):
+        wires.send(view, out_block(ctx, pos), ("out", "x") + key, place.chip, cond)
+        wires.send(view, out_block(ctx, pos), ("out", "c") + key, place.core, cond)
+
+    qkv_flood = Flood("qkv", lambda pos: w_qkv.at[block_rows(pos)])
+    gain_flood = Flood("gain", lambda pos: gain_all.at[pos])
+    out_flood = Flood("out", functools.partial(out_block, ctx), out_spread)
+
+    GU_WIDTH = (2 * half, half)
+    up_cols = pl.ds(span + half, half)
+
+    def gu_view(ref, tile, pos):
+        return ref.at[block_rows(pos), pl.ds(tile * span, GU_WIDTH[tile])]
+
+    gu_floods = [Flood(("gu", tile), functools.partial(gu_view, w_ff, tile)) for tile in TILES]
+    up_flood = PairFlood("up", w_ff, up_cols)
+
+    def spots(column, dist):
+        for way, dist in WAYS[dist]:
+            if dist == 0:
+                here, pos = None, dp
+            else:
+                here, pos = source_valid(place, way, dist), source_pos(place, way, dist)
+            if column == 1:
+                pos = pos + 1 - 2 * y
+            yield (column, way, dist), here, pos
+
+    def out_chip(column, dist):
+        for key, here, pos in spots(column, dist):
+            view = out_block(place.chip[1], pos)
+            when(here, lambda: wires.take(view, ("out", "x") + key, place.chip))
+            wires.send(view, view, ("out", "d") + key, place.core, here)
+
+    def out_core():
+        for column in range(2):
+            for dist in range(4):
+                for key, here, pos in spots(column, dist):
+                    for mark, lead in (("c", place.core[1]), ("d", 3 - ctx)):
+                        view = out_block(lead, pos)
+                        when(here, lambda: wires.take(view, ("out", mark) + key, place.core))
+
+    def mix_start(tile):
+        for part in range(2):
+            target = 2 * c + part
+            src = gu_in.at[:, pl.ds((2 * part + tile) * half, half)]
+            dst = w_ff.at[my_rows, pl.ds(pl.multiple_of(tile * span + x * half, 128), half)]
+            wires.send(src, dst, ("gu_mix", tile, 0), (dp, target), target != ctx, extra=x)
+            local(src, dst, target == ctx)
+        wires.slot(("gu_mix", tile, 1))
+
+    def mix_end(tile):
+        for part in range(2):
+            origin = part * 2 + x
+            view = w_ff.at[my_rows, pl.ds(tile * span + part * half, half)]
+            pl.when(origin != ctx)(lambda: wires.take(view, ("gu_mix", tile, part), (dp, origin)))
+
+    lanes = pl.ds(pl.multiple_of(y * span + 2 * half, 128), half)
+    other_lanes = pl.ds(pl.multiple_of((1 - y) * span + 2 * half, 128), half)
+    at_home = ctx == z
+
+    def strips_of(ref, at):
+        return [ref.at[pl.ds(j * strip, strip), at] for j in range(4)]
+
+    strips, other_strips = strips_of(w_ff, lanes), strips_of(w_ff, other_lanes)
+
+    def down_mix_start():
+        dst = w_ff.at[pl.ds(pl.multiple_of(ctx * strip, 16), strip), lanes]
+        wires.send(dt_in, dst, ("down_mix", 0), (dp, z), ctx != z, extra=ctx)
+        for j in range(1, 4):
+            wires.slot(("down_mix", j))
+        local(dt_in, dst, ctx == z)
+
+    def down_start():
+        def take_strips():
+            for j in range(4):
+                pl.when(ctx != j)(functools.partial(wires.take, strips[j], ("down_mix", j), (dp, j)))
+
+        pl.when(at_home)(take_strips)
+        for j in range(4):
+            wires.send(strips[j], strips[j], ("down", j, BELOW, 1), place.up, jnp.logical_and(at_home, place.has_up))
+            wires.send(strips[j], strips[j], ("down", j, ABOVE, 1), place.down, jnp.logical_and(at_home, place.has_down))
+            wires.send(strips[j], strips[j], ("down_y", j, 0, 0), place.across, at_home)
+
+    def down_hop(dist):
+        for way in (BELOW, ABOVE):
+            here = (z - ctx if way == BELOW else ctx - z) == dist
+            came_from = place.down if way == BELOW else place.up
+            onward = place.up if way == BELOW else place.down
+            more = place.has_up if way == BELOW else place.has_down
+            for j in range(4):
+                pl.when(here)(functools.partial(wires.take, strips[j], ("down", j, way, dist), came_from))
+                if dist < 3:
+                    wires.send(strips[j], strips[j], ("down", j, way, dist + 1), onward, jnp.logical_and(here, more))
+                wires.send(strips[j], strips[j], ("down_y", j, way, dist), place.across, here)
+
+    def down_side_end():
+        for way, dist in SIDES:
+            here = at_home if dist == 0 else (z - ctx if way == BELOW else ctx - z) == dist
+
+            def take():
+                for j in range(4):
+                    wires.take(other_strips[j], ("down_y", j, way, dist), place.across)
+
+            pl.when(here)(take)
+
+    row_at = lax.broadcasted_iota(jnp.int32, (own_rows, 1), 0)
+    first_seq = row_at < slots_here
+    position = ctx * slots_here + jnp.where(first_seq, row_at, row_at - slots_here)
+    valid = position < jnp.where(first_seq, lengths[0], lengths[1])
+    def tokens_start():
+        tok_all[here_rows, :] = tokens[...]
+        share("tok", tok_all)
+
+    def qkv_start():
+        w_qkv[my_rows, :] = jnp.zeros((rows, qkv_wide), low)
+        w_qkv[my_rows, :qkv_cols] = qkv_in[...]
+        qkv_flood.start()
+
+    def gain_start():
+        gain_all[dp] = gain_in[...]
+        gain_flood.start()
+
+    def out_start():
+        w_out[ctx, my_rows, :] = jnp.zeros((rows, out_wide), low)
+        w_out[ctx, my_rows, :out_cols] = out_in[...]
+        out_flood.start()
+
+    def cot_start():
+        g_all[here_rows, :] = jnp.where(valid, cot[...].astype(f32), 0.0).astype(low)
+        share("cot", g_all)
+
+    def gain_sides():
+        for dist in range(4):
+            gain_flood.side(dist)
+
+    gain_a = lambda: gain_row[0:1, :width]
+    gain_b = lambda: gain_row[1:2, :width]
+
+    def norm(values):
+        return lax.rsqrt(jnp.mean(values * values, axis=-1, keepdims=True) + EPS)
+
+    lane = lax.broadcasted_iota(jnp.int32, (own_rows, 128), 1)
+    low_half = lax.rem(lane, HD) < HD // 2
+    side_of = lax.div(lane, HD)
+
+    def turn(values, sign):
+        swapped = jnp.where(low_half, pltpu.roll(values, 128 - HD // 2, 1), pltpu.roll(values, HD // 2, 1))
+        return values * cos[...] + swapped * (sin[...] * sign)
+
+    def head_spots():
+        for head in range(QH):
+            kv = head // group
+            yield head // 2, head % 2, kv // 2, kv % 2, (kv % 2 * group + head % group) * slots_here
+
+    def stack_heads(slab_of, dest, scale):
+        for slab, side, key_slab, key_side, at in head_spots():
+            values = slab_of(slab)
+            if side != key_side:
+                values = pltpu.roll(values, HD, 1)
+            values = (jnp.where(side_of == key_side, values, 0.0) * scale).astype(low)
+            for seq in range(2):
+                dest[seq * slabs + key_slab, at : at + slots_here, :] = values[
+                    seq * slots_here : (seq + 1) * slots_here
+                ]
+
+    def unstack_heads(src, slab):
+        total = jnp.zeros((own_rows, 128), f32)
+        for at_slab, side, key_slab, key_side, at in head_spots():
+            if at_slab != slab:
+                continue
+            values = jnp.concatenate(
+                [src[seq * slabs + key_slab, at : at + slots_here, :] for seq in range(2)], axis=0
+            )
+            values = jnp.where(side_of == key_side, values, 0.0)
+            if side != key_side:
+                values = pltpu.roll(values, HD, 1)
+            total = total + values
+        return total
+
+    def project():
+        gain_row[...] = jnp.zeros(gain_row.shape, f32)
+        for pos in range(8):
+            piece = gain_all[pos]
+            shift = (pos * rows) % 128
+            if shift:
+                piece = pltpu.roll(piece, shift, 1)
+            at = (pos * rows) // 128 * 128
+            gain_row[:, at : at + 256] += piece
+
+        def body(i, carry):
+            at = lead_rows(i)
+            source = tok_all[at, :].astype(f32)
+            n1_all[at, :] = (source * norm(source) * gain_a()).astype(low)
+            pq[i] = nn(n1_all[at, :], w_qkv[...])
+            return carry
+
+        lax.fori_loop(0, 4, body, 0)
+        pq_in[ctx] = pq[ctx]
+        swap_start("pq", lambda peer: pq.at[peer], lambda sender: pq_in.at[sender])
+
+    def pq_end():
+        swap_end("pq", lambda sender: pq_in.at[sender])
+        proj[...] = jnp.zeros(proj.shape, f32)
+        for j in range(4):
+            part = jnp.concatenate([pq_in[j], jnp.zeros((own_rows, 128), f32)], axis=1)
+            at = qkv_cols * j
+            if at % 128:
+                part = pltpu.roll(part, at % 128, 1)
+            proj[:, at // 128 * 128 : at // 128 * 128 + qkv_wide + 128] += part
+
+    turned = {}
+
+    def query_slab(slab):
+        if slab not in turned:
+            turned[slab] = turn(proj[:, slab * 128 : slab * 128 + 128], 1.0)
+        return turned[slab]
+
+    def slot_view(lead):
+        return kv_all.at[:, :, pl.ds(pl.multiple_of(lead * slots_here, 16), slots_here)]
+
+    def kv_start():
+        my_slots = pl.ds(pl.multiple_of(ctx * slots_here, 16), slots_here)
+        for slab in range(2 * slabs):
+            at = (q_slabs + slab) * 128
+            values = proj[:, at : at + 128]
+            if slab < slabs:
+                values = turn(values, 1.0)
+            values = values.astype(low)
+            for seq in range(2):
+                kv_all[seq, slab, my_slots, :] = values[seq * slots_here : (seq + 1) * slots_here]
+
+        swap_start("kv", lambda peer: slot_view(ctx), slot_view)
+
+    def queries():
+        stack_heads(query_slab, q_st, score_scale)
+
+    def kv_end():
+        swap_end("kv", slot_view)
+
+    stack = q_st.shape[1]
+    slots = kv_all.shape[2]
+
+    def attend(i, carry):
+        seq, slab = lax.div(i, slabs), lax.rem(i, slabs)
+        scores = nt(q_st[i], kv_all[seq, slab])
+        at = ctx * slots_here + lax.rem(lax.broadcasted_iota(jnp.int32, (stack, slots), 0), slots_here)
+        key_at = lax.broadcasted_iota(jnp.int32, (stack, slots), 1)
+        length = jnp.where(seq == 0, lengths[0], lengths[1])
+        allowed = jnp.logical_and(key_at <= at, key_at < length)
+        scores = jnp.where(allowed, scores, NEGATIVE)
+        terms = jnp.exp(scores - jnp.max(scores, axis=-1, keepdims=True))
+        probs = (terms / jnp.sum(terms, axis=-1, keepdims=True)).astype(low)
+        p_st[i] = probs
+        att[i] = nn(probs, kv_all[seq, slabs + slab])
+        return carry
+
+    def attention():
+        lax.fori_loop(0, 2 * slabs, attend, 0)
+        for slab in range(q_slabs):
+            ctx_all[here_rows, slab * 128 : slab * 128 + 128] = unstack_heads(att, slab).astype(low)
+        share("ctx", ctx_all)
+
+    def out_project():
+        hidden[...] = tokens[...].astype(f32)
+        for j in range(4):
+            part = nn(ctx_all[here_rows, :], w_out[j])
+            at = out_cols * j
+            if at % 128:
+                part = pltpu.roll(part, at % 128, 1)
+            hidden[:, at // 128 * 128 : at // 128 * 128 + out_wide] += part
+        n2_all[here_rows, :] = (hidden[...] * norm(hidden[...]) * gain_b()).astype(low)
+        share("n2", n2_all)
+
+    tall = 2 * own_rows
+
+    def feed(tile):
+        def body(i, carry):
+            at = pl.ds(pl.multiple_of(i * tall, tall), tall)
+            gate = nn(n2_all[at, :], w_ff[:, tile * span : tile * span + half])
+            up = nn(n2_all[at, :], w_ff[:, tile * span + half : tile * span + 2 * half])
+            back = nn(g_all[at, :], w_ff[:, tile * span + 2 * half : (tile + 1) * span])
+            sig = jax.nn.sigmoid(gate)
+            swish = gate * sig
+            act[tile, at, :] = (swish * up).astype(low)
+            d_gu[tile, at, :half] = (back * up * sig * (1.0 + gate * (1.0 - sig))).astype(low)
+            d_gu[tile, at, half:] = (back * swish).astype(low)
+            return carry
+
+        lax.fori_loop(0, 4 * own_rows // tall, body, 0)
+
+    def grad_ff(tile):
+        def body(m, carry):
+            at = pl.ds(pl.multiple_of(m * 128, 128), 128)
+            d_ff[at, tile * span : tile * span + 2 * half] = tn(n2_all[:, at], d_gu[tile]).astype(low)
+            d_ff[at, tile * span + 2 * half : (tile + 1) * span] = tn(g_all[:, at], act[tile]).astype(low)
+            return carry
+
+        lax.fori_loop(0, width // 128, body, 0)
+
+    across_core = (1 - x) * 2 + 1 - c
+    across_own = (1 - x) * 2 + c
+    beside = x * 2 + 1 - c
+    wide_tile = 384
+
+    def group_send(name, ref, box, which):
+        lead, mark = ((across_core, "cx"), (beside, "cc"))[which]
+        wires.send(ref.at[lead], box.at[which], (name, mark), place.core)
+
+    def group_on(name, ref, box):
+        wires.take(box.at[0], (name, "cx"), place.core)
+        mine = ref.at[across_own]
+        mine[...] = (mine[...].astype(f32) + box[0].astype(f32)).astype(low)
+        wires.send(mine, box.at[2], (name, "x"), place.chip)
+
+    def group_end(name, ref, box):
+        wires.take(box.at[1], (name, "cc"), place.core)
+        wires.take(box.at[2], (name, "x"), place.chip)
+        return ref[ctx].astype(f32) + box[1].astype(f32) + box[2].astype(f32)
+
+    def pair_rows(half_x):
+        return pl.ds(pl.multiple_of(half_x * tall, 16), tall)
+
+    def group_product(ref, terms):
+        def compute(half_x):
+            def body(n, carry):
+                at = pl.ds(pl.multiple_of(n * wide_tile, 128), wide_tile)
+                total = None
+                for left, right in terms:
+                    term = nt(left(pair_rows(half_x)), right(at))
+                    total = term if total is None else total + term
+                ref[2 * half_x, :, at] = total[:own_rows].astype(low)
+                ref[2 * half_x + 1, :, at] = total[own_rows:].astype(low)
+                return carry
+
+            lax.fori_loop(0, width // wide_tile, body, 0)
+
+        return compute
+
+    back_terms = [
+        (lambda at, tile=tile: d_gu[tile, at, :], lambda at, tile=tile: w_ff[at, tile * span : tile * span + 2 * half])
+        for tile in TILES
+    ]
+    forward_terms = [
+        (lambda at, tile=tile: act[tile, at, :], lambda at, tile=tile: w_ff[at, tile * span + 2 * half : (tile + 1) * span])
+        for tile in TILES
+    ]
+
+    def key_pos(way, dist):
+        if dist == 0:
+            return None, dp
+        return source_valid(place, way, dist), source_pos(place, way, dist)
+
+    KEYS = {3: DRAIN[:2], 2: DRAIN[2:4], 1: DRAIN[4:6], 0: [(BELOW, 0)]}
+    flip = 1 - 2 * y
+
+    def z_add(name, view, boxes, inbox, way, dist):
+        here, pos = key_pos(way, dist)
+        mine = view(pos)
+        if dist == 0:
+            wires.take(boxes.at[way, dist], (name, "y", way, dist), place.across)
+            add_rows(mine, [boxes.at[way, dist]])
+            for end, fed, feeder in ((BELOW, place.has_up, place.up), (ABOVE, place.has_down, place.down)):
+
+                def own():
+                    wires.take(inbox.at[end, 0], (name, "z", end, 0), feeder)
+                    add_rows(mine, [inbox.at[end, 0]])
+
+                pl.when(fed)(own)
+            return
+        fed = place.has_up if way == BELOW else place.has_down
+        feeder = place.up if way == BELOW else place.down
+        onward = place.down if way == BELOW else place.up
+        side = boxes.at[way, dist]
+
+        def first():
+            wires.take(side, (name, "y", way, dist), place.across)
+            add_rows(mine, [side])
+
+        if dist == 3:
+            pl.when(here)(first)
+        else:
+
+            def more():
+                wires.take(side, (name, "y", way, dist), place.across)
+                wires.take(inbox.at[way, dist], (name, "z", way, dist), feeder)
+                add_rows(mine, [side, inbox.at[way, dist]])
+
+            pl.when(jnp.logical_and(here, jnp.logical_not(fed)))(first)
+            pl.when(jnp.logical_and(here, fed))(more)
+        wires.send(mine, inbox.at[way, dist - 1], (name, "z", way, dist - 1), onward, here)
+
+    class Sink:
+        def __init__(self, name, view, side, inbox):
+            self.name, self.view, self.side, self.inbox = name, view, side, inbox
+
+        def send(self, dist):
+            for way, dist in KEYS[dist]:
+                here, pos = key_pos(way, dist)
+                wires.send(
+                    self.view(pos + flip), self.side.at[way, dist],
+                    (self.name, "y", way, dist), place.across, here,
+                )
+
+        def send_all(self):
+            for dist in (3, 2, 1, 0):
+                self.send(dist)
+
+        def add(self, dist):
+            for way, dist in KEYS[dist]:
+                z_add(self.name, self.view, self.side, self.inbox, way, dist)
+
+    gu_sides, gu_inboxes = (gu_side_a, gu_side_b), (gu_inbox_a, gu_inbox_b)
+    gu_sinks = [
+        Sink(("dgu", tile), functools.partial(gu_view, d_ff, tile), gu_sides[tile], gu_inboxes[tile])
+        for tile in TILES
+    ]
+    out_sink = Sink("dout", lambda pos: d_out.at[block_rows(pos)], out_side, out_inbox)
+    qkv_sink = Sink("dqkv", lambda pos: d_qkv.at[block_rows(pos)], qkv_side, qkv_inbox)
+    d_strips, d_other_strips = strips_of(d_ff, lanes), strips_of(d_ff, other_lanes)
+
+    def down_send(tile):
+        for j in range(4):
+            wires.send(d_other_strips[j], down_side.at[j], ("ddown_y", j), place.across, (1 - y) == tile)
+
+    def down_add(dist):
+        if dist == 0:
+            for j in range(4):
+
+                def finish():
+                    wires.take(down_side.at[j], ("ddown_y", j), place.across)
+                    add_rows(d_strips[j], [down_side.at[j]])
+                    for end, fed, feeder in ((BELOW, place.has_up, place.up), (ABOVE, place.has_down, place.down)):
+
+                        def more():
+                            wires.take(down_inbox.at[end, j], ("ddown", j, end, 0), feeder)
+                            add_rows(d_strips[j], [down_inbox.at[end, j]])
+
+                        pl.when(fed)(more)
+
+                pl.when(at_home)(finish)
+            return
+        for way in (BELOW, ABOVE):
+            here = (z - ctx if way == BELOW else ctx - z) == dist
+            fed = place.has_up if way == BELOW else place.has_down
+            feeder = place.up if way == BELOW else place.down
+            onward = place.down if way == BELOW else place.up
+            for j in range(4):
+
+                def first():
+                    wires.take(down_side.at[j], ("ddown_y", j), place.across)
+                    add_rows(d_strips[j], [down_side.at[j]])
+
+                def more():
+                    wires.take(down_side.at[j], ("ddown_y", j), place.across)
+                    wires.take(down_inbox.at[way, j], ("ddown", j, way, dist), feeder)
+                    add_rows(d_strips[j], [down_side.at[j], down_inbox.at[way, j]])
+
+                pl.when(jnp.logical_and(here, jnp.logical_not(fed)))(first)
+                pl.when(jnp.logical_and(here, fed))(more)
+                wires.send(d_strips[j], down_inbox.at[way, j], ("ddown", j, way, dist - 1), onward, here)
+
+    class PairSink:
+        def __init__(self, name, ref, cols, inbox, side):
+            self.name, self.ref, self.cols, self.inbox, self.side = name, ref, cols, inbox, side
+
+        def pair(self, plane):
+            return self.ref.at[pl.ds(pl.multiple_of(2 * rows * plane, 16), 2 * rows), self.cols]
+
+        def one(self, pos):
+            return self.ref.at[block_rows(pos), self.cols]
+
+        def add(self, dist):
+            if dist == 0:
+                mine = self.pair(z)
+                for end, fed, feeder in ((BELOW, place.has_up, place.up), (ABOVE, place.has_down, place.down)):
+
+                    def more():
+                        wires.take(self.inbox.at[end, 0], (self.name, "z", end, 0), feeder)
+                        add_rows(mine, [self.inbox.at[end, 0]])
+
+                    pl.when(fed)(more)
+                wires.send(self.one(place.across[0]), self.side, (self.name, "y"), place.across)
+                return
+            for way, dist in KEYS[dist]:
+                here = source_valid(place, way, dist)
+                mine = self.pair(z - dist if way == BELOW else z + dist)
+                fed = place.has_up if way == BELOW else place.has_down
+                feeder = place.up if way == BELOW else place.down
+                onward = place.down if way == BELOW else place.up
+                if dist < 3:
+
+                    def more():
+                        wires.take(self.inbox.at[way, dist], (self.name, "z", way, dist), feeder)
+                        add_rows(mine, [self.inbox.at[way, dist]])
+
+                    pl.when(jnp.logical_and(here, fed))(more)
+                wires.send(mine, self.inbox.at[way, dist - 1], (self.name, "z", way, dist - 1), onward, here)
+
+        def end(self):
+            wires.take(self.side, (self.name, "y"), place.across)
+            add_rows(self.one(dp), [self.side])
+
+    up_sink = PairSink("dup", d_ff, up_cols, up_inbox, up_side)
+
+    def gu_finish(tile):
+        for part in range(2):
+            target = part * 2 + x
+            block = d_ff.at[my_rows, pl.ds(tile * span + part * half, half)]
+            wires.send(block, gu_mix.at[c, tile], ("dgu_mix", tile, 0), (dp, target), target != ctx, extra=c)
+            pl.when(target == ctx)(lambda: add_rows(block, [], out=gu_mix.at[c, tile]))
+        wires.slot(("dgu_mix", tile, 1))
+
+    def gu_end(tile):
+        for part in range(2):
+            origin = 2 * c + part
+            box = gu_mix.at[part, tile]
+            pl.when(origin != ctx)(lambda: wires.take(box, ("dgu_mix", tile, part), (dp, origin)))
+            add_rows(box, [], out=gu_out.at[:, pl.ds((2 * part + tile) * half, half)])
+
+    def down_finish():
+        for j in range(4):
+            wires.send(d_strips[j], down_mix, ("ddown_mix",), (dp, j), jnp.logical_and(at_home, ctx != j))
+            pl.when(jnp.logical_and(at_home, ctx == j))(functools.partial(add_rows, d_strips[j], [], down_mix))
+
+    def down_end():
+        pl.when(ctx != z)(lambda: wires.take(down_mix, ("ddown_mix",), (dp, z)))
+        add_rows(down_mix, [], out=dt_out)
+
+    def norm_back(values, inverse, gain, grad_in):
+        scaled = grad_in * gain
+        mean_term = jnp.mean(scaled * values, axis=-1, keepdims=True)
+        back = inverse * scaled - values * (inverse * inverse * inverse) * mean_term
+        return back, jnp.sum(grad_in * values * inverse, axis=0, keepdims=True)
+
+    def gp_block(which):
+        half_x = 1 - x if which == 0 else x
+        group_product(gp, back_terms)(half_x)
+        group_send("gp", gp, gp_box, which)
+
+    def op_block(which):
+        half_x = 1 - x if which == 0 else x
+        group_product(op, forward_terms)(half_x)
+        group_send("op", op, op_box, which)
+
+    def hidden_back():
+        gain_acc[0] = jnp.zeros(gain_out.shape, f32)
+        back_two, gain_two_grad = norm_back(hidden[...], norm(hidden[...]), gain_b(), group_end("gp", gp, gp_box))
+        gain_acc[0, 1:2, :] = gain_two_grad
+        grad_hidden[...] = g_all[here_rows, :].astype(f32) + back_two
+        out_lane = lax.broadcasted_iota(jnp.int32, (own_rows, out_wide), 1)
+        for j in range(4):
+            at = out_cols * j
+            part = grad_hidden[:, at // 128 * 128 : at // 128 * 128 + out_wide]
+            if at % 128:
+                part = pltpu.roll(part, out_wide - at % 128, 1)
+            wide[j] = jnp.where(out_lane < out_cols, part, 0.0).astype(low)
+        gb_all[here_rows, :] = wide[ctx]
+        swap_start("gb", lambda peer: wide.at[peer], lambda sender: gb_all.at[lead_rows(sender)])
+
+    def context_back(n, carry):
+        at = pl.ds(pl.multiple_of(n * wide_tile, 128), wide_tile)
+        total = nt(wide[0], w_out[0, at, :])
+        for j in range(1, 4):
+            total = total + nt(wide[j], w_out[j, at, :])
+        proj[:, at] = total
+        return carry
+
+    def grad_context():
+        lax.fori_loop(0, width // wide_tile, context_back, 0)
+        stack_heads(lambda slab: proj[:, slab * 128 : slab * 128 + 128], go_st, 1.0)
+
+    def attend_back(i, carry):
+        seq, slab = lax.div(i, slabs), lax.rem(i, slabs)
+        grad_probs = nt(go_st[i], kv_all[seq, slabs + slab])
+        probs = p_st[i].astype(f32)
+        delta = jnp.sum(probs * grad_probs, axis=-1, keepdims=True)
+        grad_scores = (probs * (grad_probs - delta)).astype(low)
+        att[i] = nn(grad_scores, kv_all[seq, slab]) * score_scale
+        grad_key = tn(grad_scores, q_st[i])
+        grad_value = tn(p_st[i], go_st[i])
+        for j in range(4):
+            part = slice(j * slots_here, (j + 1) * slots_here)
+            dkv[j, seq, slab] = grad_key[part].astype(low)
+            dkv[j, seq, slabs + slab] = grad_value[part].astype(low)
+        return carry
+
+    def attention_back():
+        lax.fori_loop(0, 2 * slabs, attend_back, 0)
+        group_send("dkv", dkv, dkv_box, 0)
+        group_send("dkv", dkv, dkv_box, 1)
+
+    def gb_end():
+        swap_end("gb", lambda sender: gb_all.at[lead_rows(sender)])
+
+    def grad_out(m, carry):
+        at = pl.ds(pl.multiple_of(m * 128, 128), 128)
+        d_out[at, :] = tn(ctx_all[:, at], gb_all[...]).astype(low)
+        return carry
+
+    def grad_out_all():
+        lax.fori_loop(0, width // 128, grad_out, 0)
+
+    def grad_mixed():
+        sums = group_end("dkv", dkv, dkv_box)
+        proj[...] = jnp.zeros(proj.shape, f32)
+        for slab in range(q_slabs):
+            proj[:, slab * 128 : slab * 128 + 128] = turn(unstack_heads(att, slab), -1.0)
+        for slab in range(2 * slabs):
+            values = jnp.concatenate([sums[0, slab], sums[1, slab]], axis=0)
+            if slab < slabs:
+                values = turn(values, -1.0)
+            at = (q_slabs + slab) * 128
+            proj[:, at : at + 128] = values
+        qkv_lane = lax.broadcasted_iota(jnp.int32, (own_rows, qkv_wide), 1)
+        for j in range(4):
+            at = qkv_cols * j
+            part = proj[:, at // 128 * 128 : at // 128 * 128 + qkv_wide + 128]
+            if at % 128:
+                part = pltpu.roll(part, qkv_wide + 128 - at % 128, 1)
+            gm[j] = jnp.where(qkv_lane < qkv_cols, part[:, :qkv_wide], 0.0).astype(low)
+        gm_all[here_rows, :] = gm[ctx]
+        swap_start("gm", lambda peer: gm.at[peer], lambda sender: gm_all.at[lead_rows(sender)])
+
+    def gm_end():
+        swap_end("gm", lambda sender: gm_all.at[lead_rows(sender)])
+
+    def grad_qkv(m, carry):
+        at = pl.ds(pl.multiple_of(m * 128, 128), 128)
+        d_qkv[at, :] = tn(n1_all[:, at], gm_all[...]).astype(low)
+        return carry
+
+    def grad_qkv_all():
+        lax.fori_loop(0, width // 128, grad_qkv, 0)
+
+    tokens_terms = [(lambda at: gm_all[at, :], lambda at: w_qkv[at, :])]
+
+    def gt_block(which):
+        if which == 0:
+            wires.drain_named("gp")
+        half_x = 1 - x if which == 0 else x
+        group_product(gp, tokens_terms)(half_x)
+        group_send("gt", gp, gp_box, which)
+
+    def output_end():
+        result = hidden[...] + group_end("op", op, op_box)
+        output[...] = jnp.where(valid, result, 0.0).astype(low)
+
+    def tokens_end():
+        source = tokens[...].astype(f32)
+        back_one, gain_one_grad = norm_back(source, norm(source), gain_a(), group_end("gt", gp, gp_box))
+        gain_acc[0, 0:1, :] = gain_one_grad
+        grad_tokens[...] = (grad_hidden[...] + back_one).astype(low)
+
+    low_end, high_end = z == 0, z == 3
+    mid_low, mid_high = z == 1, z == 2
+
+    def gain_send(hop):
+        def go(device, cond=None):
+            wires.send(gain_acc.at[hop], gain_box.at[hop], ("gain_sum", hop), device, cond)
+
+        if hop < 3:
+            go((place.core, place.chip, place.across)[hop])
+        elif hop == 3:
+            go(place.up, low_end)
+            go(place.down, high_end)
+        elif hop == 4:
+            go(place.up, mid_low)
+            go(place.down, mid_high)
+        else:
+            go(place.down, mid_low)
+            go(place.up, mid_high)
+
+    def gain_take(hop):
+        def add(device):
+            wires.take(gain_box.at[hop], ("gain_sum", hop), device)
+            gain_acc[hop + 1] = gain_acc[hop] + gain_box[hop]
+
+        def last(device):
+            wires.take(gain_box.at[hop], ("gain_sum", hop), device)
+            gain_out[...] = gain_box[hop]
+
+        def done():
+            gain_out[...] = gain_acc[hop]
+
+        if hop < 3:
+            add((place.core, place.chip, place.across)[hop])
+        elif hop == 3:
+            pl.when(mid_low)(lambda: add(place.down))
+            pl.when(mid_high)(lambda: add(place.up))
+        elif hop == 4:
+            pl.when(mid_low)(lambda: add(place.up))
+            pl.when(mid_high)(lambda: add(place.down))
+        else:
+            pl.when(low_end)(lambda: last(place.up))
+            pl.when(high_end)(lambda: last(place.down))
+            pl.when(mid_low)(done)
+            pl.when(mid_high)(done)
+
+    def out_end():
+        out_out[...] = d_out[my_rows, :].astype(f32)[:, :out_cols]
+
+    def qkv_end():
+        qkv_out[...] = d_qkv[my_rows, :].astype(f32)[:, :qkv_cols]
+
+    def locals_end():
+        for copy, cond in locals_:
+            when(cond, copy.wait)
+
+    mix_start(0)
+    qkv_start()
+    mix_start(1)
+    gain_start()
+    down_mix_start()
+    locals_end()
+    tokens_start()
+    qkv_flood.hop(1)
+    qkv_flood.hop(2)
+    qkv_flood.hop(3)
+    mix_end(1)
+    qkv_flood.side(0)
+    out_start()
+    gain_flood.hop(1)
+    cot_start()
+    gain_flood.hop(2)
+    mix_end(0)
+    gu_floods[0].start()
+    qkv_flood.side(3)
+    gain_flood.hop(3)
+    out_flood.hop(1)
+    qkv_flood.side(2)
+    share_on("tok", tok_all)
+    share_end("tok", tok_all)
+    down_start()
+    gain_sides()
+    gu_floods[1].start()
+    qkv_flood.side(1)
+    project()
+    up_flood.start()
+    share_on("cot", g_all)
+    out_flood.hop(2)
+    out_flood.hop(3)
+    out_flood.side(0)
+    down_hop(1)
+    up_flood.side()
+    gu_floods[1].side(0)
+    gu_floods[1].hop(1)
+    out_chip(0, 0)
+    down_hop(2)
+    gu_floods[0].hop(1)
+    pq_end()
+    kv_start()
+    out_chip(1, 0)
+    queries()
+    share_end("cot", g_all)
+    out_flood.side(2)
+    out_flood.side(3)
+    gu_floods[1].hop(2)
+    out_flood.side(1)
+    down_hop(3)
+    out_chip(0, 2)
+    gu_floods[0].hop(2)
+    kv_end()
+    attention()
+    out_chip(1, 3)
+    out_chip(0, 3)
+    out_chip(0, 1)
+    out_chip(1, 2)
+    out_chip(1, 1)
+    out_core()
+    out_project()
+    gu_floods[0].hop(3)
+    down_side_end()
+    gu_floods[0].side(1)
+    gu_floods[0].side(0)
+    up_flood.hop(1)
+    up_flood.hop(2)
+    gu_floods[1].hop(3)
+    share_on("n2", n2_all)
+    share_end("n2", n2_all)
+    gu_floods[1].side(2)
+    gu_floods[0].side(3)
+    gu_floods[0].side(2)
+    feed(0)
+    grad_ff(0)
+    gu_floods[1].side(3)
+    gu_sinks[0].send(3)
+    gu_sinks[0].send(2)
+    up_flood.hop(3)
+    gu_floods[1].side(1)
+    feed(1)
+    grad_ff(1)
+    up_sink.add(3)
+    down_send(0)
+    down_send(1)
+    share_on("ctx", ctx_all)
+    gp_block(0)
+    group_on("gp", gp, gp_box)
+    gu_sinks[0].add(3)
+    share_end("ctx", ctx_all)
+    op_block(0)
+    gp_block(1)
+    up_sink.add(2)
+    gu_sinks[1].send(3)
+    down_add(3)
+    hidden_back()
+    grad_context()
+    gu_sinks[0].send(1)
+    gu_sinks[0].add(2)
+    attention_back()
+    group_on("dkv", dkv, dkv_box)
+    up_sink.add(1)
+    gu_sinks[1].send(2)
+    gb_end()
+    grad_out_all()
+    out_sink.send(2)
+    out_sink.send(3)
+    grad_mixed()
+    gu_sinks[1].add(3)
+    down_add(2)
+    gu_sinks[1].send(1)
+    gu_sinks[0].add(1)
+    group_on("op", op, op_box)
+    out_sink.send(1)
+    gm_end()
+    grad_qkv_all()
+    gu_sinks[1].add(2)
+    gt_block(0)
+    gu_sinks[1].send(0)
+    group_on("gt", gp, gp_box)
+    out_sink.add(3)
+    gt_block(1)
+    down_add(1)
+    out_sink.send(0)
+    gu_sinks[0].send(0)
+    tokens_end()
+    gain_send(0)
+    gain_take(0)
+    gain_send(1)
+    gain_take(1)
+    gain_send(2)
+    qkv_sink.send(3)
+    op_block(1)
+    qkv_sink.send(2)
+    out_sink.add(2)
+    up_sink.add(0)
+    gu_sinks[0].add(0)
+    gu_finish(0)
+    gain_take(2)
+    gain_send(3)
+    gu_sinks[1].add(1)
+    gain_take(3)
+    gain_send(4)
+    down_add(0)
+    down_finish()
+    qkv_sink.send(1)
+    qkv_sink.add(3)
+    qkv_sink.add(2)
+    up_sink.end()
+    out_sink.add(1)
+    gu_sinks[1].add(0)
+    gu_finish(1)
+    output_end()
+    qkv_sink.send(0)
+    gain_take(4)
+    gain_send(5)
+    down_end()
+    qkv_sink.add(1)
+    out_sink.add(0)
+    out_end()
+    gain_take(5)
+    gu_end(0)
+    gu_end(1)
+    qkv_sink.add(0)
+    qkv_end()
+    wires.drain()
+
+
+def on_device_fast(tokens, lengths, gain_one, w_qkv, w_out, gain_two, w_gate_up, w_down, cotangent):
+    seq_count, row_count, width = tokens.shape
+    own_rows = seq_count * row_count
+    f32, low = jnp.float32, jnp.bfloat16
+    block = gain_one.shape[0]
+    gains = jnp.stack([gain_one, gain_two]).astype(f32)
+    gains = jnp.pad(gains, ((0, 6), (0, 256 - block)))
+    position = lax.axis_index("ctx") * row_count + jnp.arange(row_count, dtype=jnp.int32)
+    cosine, sine = angles(position, HD)
+    cosine = jnp.tile(cosine, (seq_count, 4))
+    sine = jnp.tile(jnp.concatenate([-sine, sine], axis=1), (seq_count, 2))
+    rows, qkv_cols = w_qkv.shape
+    out_cols = w_out.shape[1]
+    units = w_gate_up.shape[1] // 2
+    half, strip = w_down.shape
+    qkv_wide = -(-qkv_cols // 128) * 128
+    out_wide = -(-out_cols // 128) * 128
+    deep = 8 * rows
+    slots = 4 * row_count
+    slabs = KVH // 2
+    stack = 2 * QH // KVH * row_count
+
+    def box(*shape, dtype=low):
+        return pltpu.VMEM(shape, dtype)
+
+    scratch = [
+        box(deep, qkv_wide), box(4, deep, out_wide), box(deep, 3 * units),
+        box(deep, qkv_wide), box(deep, out_wide), box(deep, 3 * units),
+        box(8, 8, 256, dtype=f32), box(8, deep + 128, dtype=f32),
+        box(4 * own_rows, width), box(4 * own_rows, width), box(4 * own_rows, width),
+        box(4 * own_rows, width), box(4 * own_rows, QH * HD),
+        box(own_rows, width, dtype=f32), box(own_rows, width, dtype=f32),
+        box(own_rows, 4 * qkv_wide, dtype=f32),
+        box(seq_count * slabs, stack, 128), box(seq_count, 2 * slabs, slots, 128),
+        box(seq_count * slabs, stack, slots), box(seq_count * slabs, stack, 128, dtype=f32),
+        box(seq_count * slabs, stack, 128),
+        box(4, own_rows, out_wide), box(4, own_rows, qkv_wide),
+        box(4, own_rows, qkv_wide, dtype=f32), box(4, own_rows, qkv_wide, dtype=f32),
+        box(4 * own_rows, out_wide), box(4 * own_rows, qkv_wide),
+        box(2, 4 * own_rows, half), box(2, 4 * own_rows, 2 * half),
+        box(4, own_rows, width), box(3, own_rows, width),
+        box(4, own_rows, width), box(3, own_rows, width),
+        box(4, seq_count, 2 * slabs, row_count, 128), box(3, seq_count, 2 * slabs, row_count, 128),
+        box(2, 4, rows, qkv_wide), box(2, 4, rows, out_wide),
+        box(2, 4, rows, 2 * half), box(2, 4, rows, half), box(4, strip, half),
+        box(2, 3, rows, qkv_wide), box(2, 3, rows, out_wide),
+        box(2, 3, rows, 2 * half), box(2, 3, rows, half), box(2, 4, strip, half),
+        box(2, 3, 2 * rows, half), box(rows, half),
+        box(2, 2, rows, half), box(strip, half),
+        box(6, 8, width, dtype=f32), box(6, 8, width, dtype=f32),
+        pltpu.SemaphoreType.DMA((400,)),
+        pltpu.SemaphoreType.DMA((400,)),
+        pltpu.SemaphoreType.DMA((8,)),
+    ]
+    vmem = pl.BlockSpec(memory_space=pltpu.MemorySpace.VMEM)
+    smem = pl.BlockSpec(memory_space=pltpu.MemorySpace.SMEM)
+    shapes = (
+        jax.ShapeDtypeStruct((own_rows, width), low),
+        jax.ShapeDtypeStruct((own_rows, width), low),
+        jax.ShapeDtypeStruct((8, width), f32),
+        jax.ShapeDtypeStruct((rows, qkv_cols), f32),
+        jax.ShapeDtypeStruct((rows, out_cols), f32),
+        jax.ShapeDtypeStruct((rows, 2 * units), f32),
+        jax.ShapeDtypeStruct((strip, half), f32),
+    )
+    output, grad_tokens, gain_sums, final_qkv, final_out, final_gu, final_dt = pl.pallas_call(
+        functools.partial(layer_kernel, {}),
+        out_shape=shapes,
+        in_specs=[vmem, vmem, smem] + [vmem] * 7,
+        out_specs=[vmem] * 7,
+        scratch_shapes=scratch,
+        compiler_params=pltpu.CompilerParams(
+            collective_id=0, has_side_effects=True, vmem_limit_bytes=64 * 2**20
+        ),
+        name="layer",
+    )(
+        tokens.reshape(own_rows, width), cotangent.reshape(own_rows, width), lengths,
+        w_qkv, w_out, w_gate_up, w_down.T, gains, cosine, sine,
+    )
+    mine = lax.dynamic_slice(gain_sums, (0, lax.axis_index("dp") * block), (8, block))
+    return (
+        output.reshape(tokens.shape), grad_tokens.reshape(tokens.shape),
+        mine[0], final_qkv, final_out, mine[1], final_gu, final_dt.T,
+    )
+
+
 def solution(mesh):
+    fits = mesh.shape["dp"] == 8 and mesh.shape["ctx"] == 4
     return jax.shard_map(
-        on_device,
+        on_device_fast if fits else on_device,
         mesh=mesh,
         in_specs=(
             P("dp", "ctx", None),

time: 1040 us -> 201 us (0.19)
  waiting for transfers between devices: 614 us -> 0 us
  Pallas kernels: 0 us -> 188 us
  blocking collectives: 143 us -> 0 us
  local copies, waits for them, and re-layouts: 116 us -> 10.8 us
  matrix products: 97.4 us -> 0 us
  other arithmetic: 36.5 us -> 0.77 us
  between operations: 17.2 us -> 0.7 us
    all_gather x9 -> x0, waiting for transfers between devices: 375 us -> none  [the longest x1 193 us: on_device(): lax.all_gather(forward_wide[2], 'dp', axis=0, tiled=True)]
    pallas_call x0 -> x1, Pallas kernels: none -> 188 us  [on_device_fast(): pl.pallas_call(functools.partial(layer_kernel, {}), out_shape=shapes, in_...]
    reduce_scatter x4 -> x0, waiting for transfers between devices: 149 us -> none  [the longest x1 80.1 us: on_device(): lax.psum_scatter(column_grads[2].astype(jnp.bfloat16), 'dp', scatter_dime...]
    dot_general x96 -> x0, matrix products: 97.4 us -> none  [the longest x4 15.5 us: on_device(): jnp.einsum('bsr,bsc->rc', piece, right, preferred_element_type=jnp.float32)]
    unnamed x17 -> x0, waiting for transfers between devices: 90.3 us -> none
    all_to_all x3 -> x0, blocking collectives: 48.5 us -> none  [the longest x1 23.3 us: on_device(): lax.all_to_all(grad_mix, 'ctx', split_axis=2, concat_axis=1, tiled=True)]
    unnamed x2 -> x0, blocking collectives: 43.5 us -> none
    all_gather x5 -> x0, blocking collectives: 40.8 us -> none  [the longest x1 9.28 us: on_device(): lax.all_gather(w_out, 'ctx', axis=1, tiled=True)]
  transfers between devices with their start and end apart: 16 -> 0, of which waited for: 12 -> 0; matrix products, arithmetic and copies ran while one was open for 13% -> 0% of each run, Pallas kernels for 0% -> 0%
where the time goes in v4:
time: 201 us
  Pallas kernels  188 us (94%)
  local copies, waits for them, and re-layouts  10.8 us (5%)
    pallas_call x1, Pallas kernels, on_device_fast(): pl.pallas_call(functools.partial(layer_kernel, {}), out_shape=shapes, in_...  188 us
    unnamed x20, local copies, waits for them, and re-layouts  7.56 us

profile of v4, /device:TPU:0, one launch (start us, length us, event | category | flops | bytes accessed | tf_op | source)
XLA Modules:
  0.0 200.6 jit_solution(2050638368351759512)
XLA Ops:
  0.7 0.0 copy-start.5
  0.7 0.6 copy-done.5
  1.3 0.0 copy-start.6
  1.3 0.6 copy-done.6
  2.0 0.6 fusion.7.gain_in
  2.6 0.1 fusion.5
  2.7 0.1 copy.17
  2.9 0.8 tile.21.sin
  3.7 0.1 tile.9
  3.8 0.7 copy.18.cos
  4.5 188.3 %layer.1 = (bf16[128,1152]{1,0:T(8,128)(2,1)}, bf16[128,1152]{1,0:T(8,128)(2,1)}, f32[8,1152]{1,0:T(8,128)}, f32[144,480]{1,0:T(8,128)}, f32[144,288]{1,0:T(8,12...) custom-call(bf16[128,1152]{1,0:T(8,128)(2,1)} %bitcast.13, bf16[128,1152]{1,0:T(8,128)(2,1)} %bitcast.14, s32[2]{0:T(128)} %lengths.1, ...), custom_call_target="tpu_custom_call" | custom-call | tf_op jit(solution)/shard_map/layer/pallas_call | solution.py:1564
  192.9 1.4 fusion.8
  194.3 0.0 copy-start.3
  194.3 0.0 copy-start.2
  194.3 1.8 copy.25
  196.1 0.0 copy-done.3
  196.1 0.0 copy-start
  196.1 0.7 copy.26
  196.8 0.0 copy-done.2
  196.8 0.0 copy-start.4
  196.8 0.7 copy.27
  197.5 0.3 copy-done.4
  197.8 0.7 copy.28
  198.5 0.0 copy-done
  198.5 0.0 copy-start.1
  198.5 0.9 copy.29
  199.4 0.4 copy-done.1
  199.8 0.8 copy.30
  (7 shorter events, 0.1 us)
Async XLA Ops:
  0.7 0.7 copy-start.5
  1.3 0.7 copy-start.6
  194.3 1.8 copy-start.3
  194.3 2.5 %copy-start.2 = (f32[144,480]{1,0:T(8,128)S(1)}, f32[144,480]{1,0:T(8,128)}, u32[]{:S(2)}) copy-start(f32[144,480]{1,0:T(8,128)} %get-tuple-element.38) | copy-start | bytes 829444
  196.1 2.5 %copy-start = (f32[144,1536]{1,0:T(8,128)S(1)}, f32[144,1536]{1,0:T(8,128)}, u32[]{:S(2)}) copy-start(f32[144,1536]{1,0:T(8,128)} %get-tuple-element.41) | copy-start | bytes 2654212
  196.8 1.0 copy-start.4
  198.5 1.3 copy-start.1

commit v5 on v4

--- a/solution.py
+++ b/solution.py
@@ -3,6 +3,7 @@
 
 import jax
 import jax.numpy as jnp
+import numpy as np
 from jax import lax
 from jax.experimental import pallas as pl
 from jax.experimental.pallas import tpu as pltpu
@@ -498,9 +499,9 @@
 
 def layer_kernel(
     names,
-    tokens, cot, lengths, qkv_in, out_in, gu_in, dt_in, gain_in, cos, sin,
+    tokens, cot, lengths, qkv_in, out_in, gu_in, dt_in, gain_one, gain_two, cos_table, sin_table,
     output, grad_tokens, gain_out, qkv_out, out_out, gu_out, dt_out,
-    w_qkv, w_out, w_ff, d_qkv, d_out, d_ff, gain_all, gain_row,
+    w_qkv, w_out, w_ff, d_qkv, d_out, d_ff, gain_all, gain_row, cos, sin,
     tok_all, n1_all, n2_all, g_all, ctx_all, hidden, grad_hidden, proj, q_st, kv_all, p_st, att, go_st,
     wide, gm, pq, pq_in, gb_all, gm_all, act, d_gu, gp, gp_box, op, op_box, dkv, dkv_box,
     qkv_side, out_side, gu_side_a, gu_side_b, down_side, qkv_inbox, out_inbox, gu_inbox_a, gu_inbox_b, down_inbox,
@@ -691,6 +692,12 @@
             wires.slot(("down_mix", j))
         local(dt_in, dst, ctx == z)
 
+    def tables():
+        for table, ref in ((cos_table, cos), (sin_table, sin)):
+            mine = table[pl.ds(pl.multiple_of(ctx * slots_here, 16), slots_here), :]
+            ref[:slots_here, :] = mine
+            ref[slots_here:, :] = mine
+
     def down_start():
         def take_strips():
             for j in range(4):
@@ -738,7 +745,9 @@
         qkv_flood.start()
 
     def gain_start():
-        gain_all[dp] = gain_in[...]
+        gain_all[dp] = jnp.zeros(gain_all.shape[1:], f32)
+        gain_all[dp, 0:1, :rows] = gain_one[...].reshape(1, rows).astype(f32)
+        gain_all[dp, 1:2, :rows] = gain_two[...].reshape(1, rows).astype(f32)
         gain_flood.start()
 
     def out_start():
@@ -1318,10 +1327,10 @@
             pl.when(mid_high)(done)
 
     def out_end():
-        out_out[...] = d_out[my_rows, :].astype(f32)[:, :out_cols]
+        out_out[...] = d_out[my_rows, :]
 
     def qkv_end():
-        qkv_out[...] = d_qkv[my_rows, :].astype(f32)[:, :qkv_cols]
+        qkv_out[...] = d_qkv[my_rows, :]
 
     def locals_end():
         for copy, cond in locals_:
@@ -1329,171 +1338,191 @@
 
     mix_start(0)
     qkv_start()
+    out_start()
+    tokens_start()
+    out_chip(0, 0)
+    qkv_flood.hop(1)
+    down_mix_start()
     mix_start(1)
-    gain_start()
-    down_mix_start()
+    tables()
     locals_end()
-    tokens_start()
-    qkv_flood.hop(1)
-    qkv_flood.hop(2)
-    qkv_flood.hop(3)
-    mix_end(1)
-    qkv_flood.side(0)
-    out_start()
-    gain_flood.hop(1)
-    cot_start()
-    gain_flood.hop(2)
     mix_end(0)
     gu_floods[0].start()
+    cot_start()
+    gain_start()
+    gain_flood.hop(1)
+    out_flood.hop(1)
+    gain_flood.hop(2)
+    gain_flood.hop(3)
+    qkv_flood.hop(2)
+    qkv_flood.side(1)
+    qkv_flood.hop(3)
+    share_on("tok", tok_all)
+    out_flood.side(0)
+    down_start()
+    out_flood.hop(2)
     qkv_flood.side(3)
-    gain_flood.hop(3)
-    out_flood.hop(1)
+    gain_sides()
+    mix_end(1)
+    up_flood.start()
+    gu_floods[1].start()
+    qkv_flood.side(0)
     qkv_flood.side(2)
-    share_on("tok", tok_all)
     share_end("tok", tok_all)
-    down_start()
-    gain_sides()
-    gu_floods[1].start()
-    qkv_flood.side(1)
     project()
-    up_flood.start()
+    gu_floods[0].side(0)
+    out_flood.hop(3)
+    down_hop(1)
     share_on("cot", g_all)
-    out_flood.hop(2)
-    out_flood.hop(3)
-    out_flood.side(0)
-    down_hop(1)
-    up_flood.side()
-    gu_floods[1].side(0)
     gu_floods[1].hop(1)
-    out_chip(0, 0)
-    down_hop(2)
+    share_end("cot", g_all)
     gu_floods[0].hop(1)
+    out_chip(0, 2)
+    out_chip(0, 1)
     pq_end()
     kv_start()
+    out_flood.side(1)
+    down_hop(2)
+    out_flood.side(3)
+    queries()
+    down_hop(3)
+    out_flood.side(2)
+    kv_end()
+    up_flood.side()
+    attention()
+    gu_floods[1].side(1)
+    out_chip(1, 2)
+    gu_floods[0].hop(2)
     out_chip(1, 0)
-    queries()
-    share_end("cot", g_all)
-    out_flood.side(2)
-    out_flood.side(3)
-    gu_floods[1].hop(2)
-    out_flood.side(1)
-    down_hop(3)
-    out_chip(0, 2)
-    gu_floods[0].hop(2)
-    kv_end()
-    attention()
+    out_chip(0, 3)
+    out_chip(1, 1)
     out_chip(1, 3)
-    out_chip(0, 3)
-    out_chip(0, 1)
-    out_chip(1, 2)
-    out_chip(1, 1)
     out_core()
     out_project()
+    up_flood.hop(1)
+    gu_floods[0].side(1)
     gu_floods[0].hop(3)
     down_side_end()
-    gu_floods[0].side(1)
-    gu_floods[0].side(0)
-    up_flood.hop(1)
+    gu_floods[1].hop(2)
+    share_on("n2", n2_all)
     up_flood.hop(2)
+    gu_floods[1].side(0)
+    gu_floods[0].side(2)
+    gu_floods[0].side(3)
+    share_end("n2", n2_all)
+    feed(0)
     gu_floods[1].hop(3)
-    share_on("n2", n2_all)
-    share_end("n2", n2_all)
-    gu_floods[1].side(2)
-    gu_floods[0].side(3)
-    gu_floods[0].side(2)
-    feed(0)
     grad_ff(0)
-    gu_floods[1].side(3)
     gu_sinks[0].send(3)
     gu_sinks[0].send(2)
+    gu_floods[1].side(3)
+    gu_floods[1].side(2)
     up_flood.hop(3)
-    gu_floods[1].side(1)
     feed(1)
     grad_ff(1)
     up_sink.add(3)
+    gu_sinks[1].send(3)
+    down_send(1)
     down_send(0)
-    down_send(1)
+    gu_sinks[0].send(1)
+    gu_sinks[1].send(2)
+    gu_sinks[0].add(3)
+    gu_sinks[1].send(0)
+    gp_block(0)
     share_on("ctx", ctx_all)
-    gp_block(0)
     group_on("gp", gp, gp_box)
-    gu_sinks[0].add(3)
-    share_end("ctx", ctx_all)
+    gu_sinks[0].send(0)
+    op_block(1)
     op_block(0)
+    up_sink.add(2)
     gp_block(1)
-    up_sink.add(2)
-    gu_sinks[1].send(3)
-    down_add(3)
+    gu_sinks[1].add(3)
+    gu_sinks[0].add(2)
     hidden_back()
     grad_context()
-    gu_sinks[0].send(1)
-    gu_sinks[0].add(2)
     attention_back()
+    up_sink.add(1)
     group_on("dkv", dkv, dkv_box)
-    up_sink.add(1)
-    gu_sinks[1].send(2)
     gb_end()
+    share_end("ctx", ctx_all)
     grad_out_all()
+    gu_sinks[1].send(1)
+    out_sink.send(3)
+    down_add(3)
+    grad_mixed()
+    gu_sinks[0].add(1)
+    down_add(2)
+    out_sink.send(1)
+    group_on("op", op, op_box)
+    gu_sinks[1].add(2)
+    gm_end()
+    gt_block(0)
+    gt_block(1)
+    up_sink.add(0)
+    grad_qkv_all()
+    qkv_sink.send(3)
     out_sink.send(2)
-    out_sink.send(3)
-    grad_mixed()
-    gu_sinks[1].add(3)
-    down_add(2)
-    gu_sinks[1].send(1)
-    gu_sinks[0].add(1)
-    group_on("op", op, op_box)
-    out_sink.send(1)
-    gm_end()
-    grad_qkv_all()
-    gu_sinks[1].add(2)
-    gt_block(0)
-    gu_sinks[1].send(0)
     group_on("gt", gp, gp_box)
-    out_sink.add(3)
-    gt_block(1)
+    qkv_sink.send(2)
     down_add(1)
-    out_sink.send(0)
-    gu_sinks[0].send(0)
+    gu_sinks[0].add(0)
+    gu_finish(0)
     tokens_end()
     gain_send(0)
     gain_take(0)
+    gu_sinks[1].add(1)
     gain_send(1)
     gain_take(1)
+    out_sink.add(3)
     gain_send(2)
-    qkv_sink.send(3)
-    op_block(1)
-    qkv_sink.send(2)
+    qkv_sink.send(1)
+    qkv_sink.add(3)
     out_sink.add(2)
-    up_sink.add(0)
-    gu_sinks[0].add(0)
-    gu_finish(0)
-    gain_take(2)
-    gain_send(3)
-    gu_sinks[1].add(1)
-    gain_take(3)
-    gain_send(4)
+    qkv_sink.add(2)
     down_add(0)
     down_finish()
-    qkv_sink.send(1)
-    qkv_sink.add(3)
-    qkv_sink.add(2)
+    gain_take(2)
+    gu_sinks[1].add(0)
+    out_sink.send(0)
+    qkv_sink.send(0)
+    output_end()
     up_sink.end()
+    gain_send(3)
     out_sink.add(1)
-    gu_sinks[1].add(0)
+    gain_take(3)
     gu_finish(1)
-    output_end()
-    qkv_sink.send(0)
+    gain_send(4)
+    qkv_sink.add(1)
+    out_sink.add(0)
     gain_take(4)
     gain_send(5)
+    out_end()
+    gu_end(0)
     down_end()
-    qkv_sink.add(1)
-    out_sink.add(0)
-    out_end()
-    gain_take(5)
-    gu_end(0)
     gu_end(1)
     qkv_sink.add(0)
     qkv_end()
+    gain_take(5)
     wires.drain()
+
+
+def finish_kernel(
+    output, grad_tokens, gains, qkv, out, gu, down_t,
+    output_end, grad_tokens_end, qkv_end, out_end, gu_end, down_end, one_end, two_end,
+):
+    f32 = jnp.float32
+    output_end[...] = output[...]
+    grad_tokens_end[...] = grad_tokens[...]
+    qkv_end[...] = qkv[:, : qkv_end.shape[1]].astype(f32)
+    out_end[...] = out[:, : out_end.shape[1]].astype(f32)
+    gu_end[...] = gu[...].astype(f32)
+    down_end[...] = down_t[...].astype(f32)
+    block = one_end.shape[0]
+    width = gains.shape[1]
+    start = lax.axis_index("dp") * block
+    mine = pltpu.roll(gains[...], lax.rem(width - start, width), 1)
+    one_end[...] = mine[0, :block]
+    two_end[...] = mine[1, :block]
 
 
 def on_device_fast(tokens, lengths, gain_one, w_qkv, w_out, gain_two, w_gate_up, w_down, cotangent):
@@ -1501,12 +1530,12 @@
     own_rows = seq_count * row_count
     f32, low = jnp.float32, jnp.bfloat16
     block = gain_one.shape[0]
-    gains = jnp.stack([gain_one, gain_two]).astype(f32)
-    gains = jnp.pad(gains, ((0, 6), (0, 256 - block)))
-    position = lax.axis_index("ctx") * row_count + jnp.arange(row_count, dtype=jnp.int32)
-    cosine, sine = angles(position, HD)
-    cosine = jnp.tile(cosine, (seq_count, 4))
-    sine = jnp.tile(jnp.concatenate([-sine, sine], axis=1), (seq_count, 2))
+    slots = 4 * row_count
+    place_of = np.arange(slots, dtype=np.float32)
+    frequency = np.float32(10000.0) ** (-np.arange(HD // 2, dtype=np.float32) * np.float32(2.0 / HD))
+    angle = place_of[:, None] * frequency[None, :]
+    cosine = np.tile(np.cos(angle), (1, 4))
+    sine = np.tile(np.concatenate([-np.sin(angle), np.sin(angle)], axis=1), (1, 2))
     rows, qkv_cols = w_qkv.shape
     out_cols = w_out.shape[1]
     units = w_gate_up.shape[1] // 2
@@ -1514,7 +1543,6 @@
     qkv_wide = -(-qkv_cols // 128) * 128
     out_wide = -(-out_cols // 128) * 128
     deep = 8 * rows
-    slots = 4 * row_count
     slabs = KVH // 2
     stack = 2 * QH // KVH * row_count
 
@@ -1525,6 +1553,7 @@
         box(deep, qkv_wide), box(4, deep, out_wide), box(deep, 3 * units),
         box(deep, qkv_wide), box(deep, out_wide), box(deep, 3 * units),
         box(8, 8, 256, dtype=f32), box(8, deep + 128, dtype=f32),
+        box(own_rows, 128, dtype=f32), box(own_rows, 128, dtype=f32),
         box(4 * own_rows, width), box(4 * own_rows, width), box(4 * own_rows, width),
         box(4 * own_rows, width), box(4 * own_rows, QH * HD),
         box(own_rows, width, dtype=f32), box(own_rows, width, dtype=f32),
@@ -1556,15 +1585,15 @@
         jax.ShapeDtypeStruct((own_rows, width), low),
         jax.ShapeDtypeStruct((own_rows, width), low),
         jax.ShapeDtypeStruct((8, width), f32),
-        jax.ShapeDtypeStruct((rows, qkv_cols), f32),
-        jax.ShapeDtypeStruct((rows, out_cols), f32),
-        jax.ShapeDtypeStruct((rows, 2 * units), f32),
-        jax.ShapeDtypeStruct((strip, half), f32),
-    )
-    output, grad_tokens, gain_sums, final_qkv, final_out, final_gu, final_dt = pl.pallas_call(
+        jax.ShapeDtypeStruct((rows, qkv_wide), low),
+        jax.ShapeDtypeStruct((rows, out_wide), low),
+        jax.ShapeDtypeStruct((rows, 2 * units), low),
+        jax.ShapeDtypeStruct((strip, half), low),
+    )
+    results = pl.pallas_call(
         functools.partial(layer_kernel, {}),
         out_shape=shapes,
-        in_specs=[vmem, vmem, smem] + [vmem] * 7,
+        in_specs=[vmem, vmem, smem] + [vmem] * 8,
         out_specs=[vmem] * 7,
         scratch_shapes=scratch,
         compiler_params=pltpu.CompilerParams(
@@ -1573,12 +1602,28 @@
         name="layer",
     )(
         tokens.reshape(own_rows, width), cotangent.reshape(own_rows, width), lengths,
-        w_qkv, w_out, w_gate_up, w_down.T, gains, cosine, sine,
-    )
-    mine = lax.dynamic_slice(gain_sums, (0, lax.axis_index("dp") * block), (8, block))
+        w_qkv, w_out, w_gate_up, w_down.T, gain_one, gain_two,
+        cosine, sine,
+    )
+    output, grad_tokens, final_qkv, final_out, final_gu, final_dt, one, two = pl.pallas_call(
+        finish_kernel,
+        out_shape=(
+            jax.ShapeDtypeStruct((own_rows, width), low),
+            jax.ShapeDtypeStruct((own_rows, width), low),
+            jax.ShapeDtypeStruct((rows, qkv_cols), f32),
+            jax.ShapeDtypeStruct((rows, out_cols), f32),
+            jax.ShapeDtypeStruct((rows, 2 * units), f32),
+            jax.ShapeDtypeStruct((strip, half), f32),
+            jax.ShapeDtypeStruct((block,), f32),
+            jax.ShapeDtypeStruct((block,), f32),
+        ),
+        in_specs=[vmem] * 7,
+        out_specs=[vmem] * 8,
+        name="finish",
+    )(*results)
     return (
         output.reshape(tokens.shape), grad_tokens.reshape(tokens.shape),
-        mine[0], final_qkv, final_out, mine[1], final_gu, final_dt.T,
+        one, final_qkv, final_out, two, final_gu, final_dt.T,
     )
 
 

time: 201 us -> 182 us (0.905)
  local copies, waits for them, and re-layouts: 10.8 us -> 0 us
  Pallas kernels: 188 us -> 181 us
    pallas_call x1, Pallas kernels: 188 us -> 178 us  [on_device_fast(): pl.pallas_call(functools.partial(layer_kernel, {}), out_shape=shapes, in_...]
    unnamed x20 -> x0, local copies, waits for them, and re-layouts: 7.56 us -> none
    pallas_call x0 -> x1, Pallas kernels: none -> 2.83 us  [on_device_fast(): pl.pallas_call(finish_kernel, out_shape=(jax.ShapeDtypeStruct((own_rows,...]
where the time goes in v5:
time: 182 us
  Pallas kernels  181 us (99%)
    pallas_call x1, Pallas kernels, on_device_fast(): pl.pallas_call(functools.partial(layer_kernel, {}), out_shape=shapes, in_...  178 us

profile of v5, /device:TPU:0, one launch (start us, length us, event | category | flops | bytes accessed | tf_op | source)
XLA Modules:
  0.0 181.8 jit_solution(567847061618085562)
XLA Ops:
  0.6 178.4 %layer.1 = (bf16[128,1152]{1,0:T(8,128)(2,1)}, bf16[128,1152]{1,0:T(8,128)(2,1)}, f32[8,1152]{1,0:T(8,128)}, bf16[144,512]{1,0:T(8,128)(2,1)}, bf16[144,384]{1,0...) custom-call(bf16[128,1152]{1,0:T(8,128)(2,1)} %bitcast.6, bf16[128,1152]{1,0:T(8,128)(2,1)} %bitcast.7, ...), custom_call_target="tpu_custom_call" | custom-call | tf_op jit(solution)/shard_map/layer/pallas_call | solution.py:1593
  179.0 2.8 %finish.1 = (bf16[128,1152]{1,0:T(8,128)(2,1)}, bf16[128,1152]{1,0:T(8,128)(2,1)}, f32[144,480]{1,0:T(8,128)}, f32[144,288]{1,0:T(8,128)}, f32[144,1536]{1,0:T(8...) custom-call(bf16[128,1152]{1,0:T(8,128)(2,1)} %get-tuple-element.23.output, ...), custom_call_target="tpu_custom_call" | custom-call | tf_op jit(solution)/shard_map/finish/pallas_call | solution.py:1608

commit v6 on v5

--- a/solution.py
+++ b/solution.py
@@ -1,3 +1,4 @@
+import enum
 import functools
 import math
 
@@ -344,41 +345,66 @@
     pl.semaphore_wait(barrier, 4 + ends)
 
 
+class Way(enum.IntEnum):
+    BELOW = 0
+    ABOVE = 1
+
+
+BELOW, ABOVE = Way.BELOW, Way.ABOVE
+SENDS = 80
+
+
 class Wires:
     def __init__(self, send_sems, recv_sems, names):
         self.send_sems = send_sems
         self.recv_sems = recv_sems
         self.index = names
+        self.total = sum(names.values()) if names else 0
+        self.base = {}
         self.count = 0
-        self.pending = []
-
-    def slot(self, name):
-        if name not in self.index:
-            self.index[name] = len(self.index)
-        return self.index[name]
+        self.live = {}
+
+    def slot(self, name, size=1):
+        if name not in self.base:
+            self.base[name] = self.total
+            self.total += size
+        return self.base[name]
+
+    def spot(self, name, plane):
+        if name[0] in ("down", "down_y"):
+            return self.slot(name[:2])
+        if name[0] == "ddown":
+            return self.slot(name[:3])
+        if name[:2] in GROUPED or name[0] in SWAPS:
+            return self.slot(name[:2] if name[:2] in GROUPED else name[:1])
+        if len(name) > 2 and isinstance(name[-2], Way):
+            way, dist = name[-2:]
+            source = plane - dist if way == BELOW else plane + dist
+            if name[-3] == "z":
+                return self.slot(name[:-2], 5) + source + int(way)
+            return self.slot(name[:-2], 4) + source
+        return self.slot(name)
 
     def send(self, src, dst, name, device, cond=None, extra=None):
         number = self.count
         self.count += 1
-        at = self.slot(name)
+        self.settle(number - SENDS)
+        at = self.spot(name, lax.div(device[0], 2))
         if extra is not None:
             at = at + extra
         copy = pltpu.make_async_remote_copy(
             src_ref=src,
             dst_ref=dst,
-            send_sem=self.send_sems.at[number],
+            send_sem=self.send_sems.at[number % SENDS],
             recv_sem=self.recv_sems.at[at],
             device_id=device,
             device_id_type=MESH,
         )
-        if cond is None:
-            copy.start()
-        else:
-            pl.when(cond)(copy.start)
-        self.pending.append((copy, cond, name))
+        when(cond, copy.start)
+        self.live[number] = (copy, cond, name)
 
     def take(self, dst, name, device, extra=None):
-        at = self.slot(name)
+        at = self.spot(name, lax.div(lax.axis_index("dp"), 2))
         if extra is not None:
             at = at + extra
         pltpu.make_async_remote_copy(
@@ -390,19 +416,23 @@
             device_id_type=MESH,
         ).wait_recv()
 
+    def settle(self, number):
+        if number in self.live:
+            copy, cond, name = self.live.pop(number)
+            when(cond, copy.wait_send)
+
     def drain(self):
-        for copy, cond, name in self.pending:
-            when(cond, copy.wait_send)
-        self.pending = []
+        for number in list(self.live):
+            self.settle(number)
 
     def drain_named(self, first):
-        for copy, cond, name in self.pending:
-            if name[0] == first:
-                when(cond, copy.wait_send)
-        self.pending = [entry for entry in self.pending if entry[2][0] != first]
-
-
-BELOW, ABOVE = 0, 1
+        for number in list(self.live):
+            if self.live[number][2][0] == first:
+                self.settle(number)
+
+
+GROUPED = (("out", "c"), ("out", "d"), ("gain", "y")) + tuple((("gu", n), "y") for n in range(3))
+SWAPS = ("pq", "kv", "gb", "gm")
 
 
 def both(first, second):
@@ -504,7 +534,7 @@
     w_qkv, w_out, w_ff, d_qkv, d_out, d_ff, gain_all, gain_row, cos, sin,
     tok_all, n1_all, n2_all, g_all, ctx_all, hidden, grad_hidden, proj, q_st, kv_all, p_st, att, go_st,
     wide, gm, pq, pq_in, gb_all, gm_all, act, d_gu, gp, gp_box, op, op_box, dkv, dkv_box,
-    qkv_side, out_side, gu_side_a, gu_side_b, down_side, qkv_inbox, out_inbox, gu_inbox_a, gu_inbox_b, down_inbox,
+    qkv_side, out_side, gu_side, down_side, qkv_inbox, out_inbox, gu_inbox, down_inbox,
     up_inbox, up_side, gu_mix, down_mix, gain_box, gain_acc,
     send_sems, recv_sems, local_sems,
 ):
@@ -557,10 +587,8 @@
             peer = lax.rem(ctx + step, 4)
             wires.send(src(peer), dst(ctx), (name, step), (dp, peer))
 
-    def swap_end(name, dst):
-        for step in (1, 2, 3):
-            peer = lax.rem(ctx + 4 - step, 4)
-            wires.take(dst(peer), (name, step), (dp, peer))
+    def swap_end(name, three):
+        wires.take(three, (name, 1), place.core)
 
     locals_ = []
 
@@ -579,13 +607,13 @@
         def start(self):
             flood_start(wires, place, self.name, self.block(dp), self.block, self.spread)
 
-        def hop(self, dist):
-            for way, dist in WAYS[dist]:
-                flood_step(wires, place, self.name, self.block, self.spread, way, dist)
-
-        def side(self, dist):
-            for way, dist in WAYS[dist]:
-                flood_side(wires, place, self.name, self.block, self.spread, way, dist)
+        def hop(self, dist, way):
+            way = Way(way)
+            flood_step(wires, place, self.name, self.block, self.spread, way, dist)
+
+        def side(self, dist, way):
+            way = Way(way) if dist else way
+            flood_side(wires, place, self.name, self.block, self.spread, way, dist)
 
     class PairFlood:
         def __init__(self, name, ref, cols):
@@ -606,16 +634,16 @@
             wires.send(view, view, (self.name, BELOW, 1), place.up, place.has_up)
             wires.send(view, view, (self.name, ABOVE, 1), place.down, place.has_down)
 
-        def hop(self, dist):
-            for way, dist in WAYS[dist]:
-                here = source_valid(place, way, dist)
-                view = self.pair(z - dist if way == BELOW else z + dist)
-                came_from = place.down if way == BELOW else place.up
-                pl.when(here)(lambda: wires.take(view, (self.name, way, dist), came_from))
-                if dist < 3:
-                    onward = place.up if way == BELOW else place.down
-                    more = place.has_up if way == BELOW else place.has_down
-                    wires.send(view, view, (self.name, way, dist + 1), onward, jnp.logical_and(here, more))
+        def hop(self, dist, way):
+            way = Way(way)
+            here = source_valid(place, way, dist)
+            view = self.pair(z - dist if way == BELOW else z + dist)
+            came_from = place.down if way == BELOW else place.up
+            pl.when(here)(lambda: wires.take(view, (self.name, way, dist), came_from))
+            if dist < 3:
+                onward = place.up if way == BELOW else place.down
+                more = place.has_up if way == BELOW else place.has_down
+                wires.send(view, view, (self.name, way, dist + 1), onward, jnp.logical_and(here, more))
 
     def out_block(lead, pos):
         return w_out.at[lead, block_rows(pos)]
@@ -628,17 +656,20 @@
     gain_flood = Flood("gain", lambda pos: gain_all.at[pos])
     out_flood = Flood("out", functools.partial(out_block, ctx), out_spread)
 
-    GU_WIDTH = (2 * half, half)
-    up_cols = pl.ds(span + half, half)
-
-    def gu_view(ref, tile, pos):
-        return ref.at[block_rows(pos), pl.ds(tile * span, GU_WIDTH[tile])]
-
-    gu_floods = [Flood(("gu", tile), functools.partial(gu_view, w_ff, tile)) for tile in TILES]
-    up_flood = PairFlood("up", w_ff, up_cols)
-
-    def spots(column, dist):
-        for way, dist in WAYS[dist]:
+    PARTS = [(tile, part) for tile in TILES for part in range(2)]
+
+    def part_cols(number):
+        tile, part = PARTS[number]
+        return pl.ds(tile * span + part * half, half)
+
+    def gu_view(ref, number, pos):
+        return ref.at[block_rows(pos), part_cols(number)]
+
+    gu_floods = [Flood(("gu", number), functools.partial(gu_view, w_ff, number)) for number in range(3)]
+    up_flood = PairFlood("up", w_ff, part_cols(3))
+
+    def spots(column, dist, way=None):
+        for way, dist in WAYS[dist] if way is None else [(way, dist)]:
             if dist == 0:
                 here, pos = None, dp
             else:
@@ -647,34 +678,34 @@
                 pos = pos + 1 - 2 * y
             yield (column, way, dist), here, pos
 
-    def out_chip(column, dist):
-        for key, here, pos in spots(column, dist):
+    def out_chip(column, dist, way):
+        way = Way(way) if dist else way
+        for key, here, pos in spots(column, dist, way):
             view = out_block(place.chip[1], pos)
             when(here, lambda: wires.take(view, ("out", "x") + key, place.chip))
             wires.send(view, view, ("out", "d") + key, place.core, here)
 
     def out_core():
-        for column in range(2):
-            for dist in range(4):
-                for key, here, pos in spots(column, dist):
-                    for mark, lead in (("c", place.core[1]), ("d", 3 - ctx)):
-                        view = out_block(lead, pos)
-                        when(here, lambda: wires.take(view, ("out", mark) + key, place.core))
+        for mark, lead in (("c", place.core[1]), ("d", 3 - ctx)):
+            wires.take(w_out.at[lead], ("out", mark), place.core)
+
+    def gu_sides(number):
+        wires.take(w_ff.at[pl.ds(0, 4 * rows), part_cols(number)], (("gu", number), "y"), place.across)
 
     def mix_start(tile):
         for part in range(2):
             target = 2 * c + part
             src = gu_in.at[:, pl.ds((2 * part + tile) * half, half)]
             dst = w_ff.at[my_rows, pl.ds(pl.multiple_of(tile * span + x * half, 128), half)]
-            wires.send(src, dst, ("gu_mix", tile, 0), (dp, target), target != ctx, extra=x)
+            wires.slot(("gu_mix", tile), 2)
+            wires.send(src, dst, ("gu_mix", tile), (dp, target), target != ctx, extra=x)
             local(src, dst, target == ctx)
-        wires.slot(("gu_mix", tile, 1))
-
-    def mix_end(tile):
-        for part in range(2):
-            origin = part * 2 + x
-            view = w_ff.at[my_rows, pl.ds(tile * span + part * half, half)]
-            pl.when(origin != ctx)(lambda: wires.take(view, ("gu_mix", tile, part), (dp, origin)))
+
+    def mix_end(number):
+        tile, part = PARTS[number]
+        origin = part * 2 + x
+        view = gu_view(w_ff, number, dp)
+        pl.when(origin != ctx)(lambda: wires.take(view, ("gu_mix", tile), (dp, origin), extra=part))
 
     lanes = pl.ds(pl.multiple_of(y * span + 2 * half, 128), half)
     other_lanes = pl.ds(pl.multiple_of((1 - y) * span + 2 * half, 128), half)
@@ -687,9 +718,8 @@
 
     def down_mix_start():
         dst = w_ff.at[pl.ds(pl.multiple_of(ctx * strip, 16), strip), lanes]
-        wires.send(dt_in, dst, ("down_mix", 0), (dp, z), ctx != z, extra=ctx)
-        for j in range(1, 4):
-            wires.slot(("down_mix", j))
+        wires.slot(("down_mix",), 4)
+        wires.send(dt_in, dst, ("down_mix",), (dp, z), ctx != z, extra=ctx)
         local(dt_in, dst, ctx == z)
 
     def tables():
@@ -698,28 +728,22 @@
             ref[:slots_here, :] = mine
             ref[slots_here:, :] = mine
 
-    def down_start():
-        def take_strips():
-            for j in range(4):
-                pl.when(ctx != j)(functools.partial(wires.take, strips[j], ("down_mix", j), (dp, j)))
-
-        pl.when(at_home)(take_strips)
-        for j in range(4):
-            wires.send(strips[j], strips[j], ("down", j, BELOW, 1), place.up, jnp.logical_and(at_home, place.has_up))
-            wires.send(strips[j], strips[j], ("down", j, ABOVE, 1), place.down, jnp.logical_and(at_home, place.has_down))
-            wires.send(strips[j], strips[j], ("down_y", j, 0, 0), place.across, at_home)
-
-    def down_hop(dist):
+    def down_start(j):
+        pl.when(jnp.logical_and(at_home, ctx != j))(lambda: wires.take(strips[j], ("down_mix",), (dp, j), extra=j))
+        wires.send(strips[j], strips[j], ("down", j, BELOW, 1), place.up, jnp.logical_and(at_home, place.has_up))
+        wires.send(strips[j], strips[j], ("down", j, ABOVE, 1), place.down, jnp.logical_and(at_home, place.has_down))
+        wires.send(strips[j], strips[j], ("down_y", j, 0, 0), place.across, at_home)
+
+    def down_hop(dist, j):
         for way in (BELOW, ABOVE):
             here = (z - ctx if way == BELOW else ctx - z) == dist
             came_from = place.down if way == BELOW else place.up
             onward = place.up if way == BELOW else place.down
             more = place.has_up if way == BELOW else place.has_down
-            for j in range(4):
-                pl.when(here)(functools.partial(wires.take, strips[j], ("down", j, way, dist), came_from))
-                if dist < 3:
-                    wires.send(strips[j], strips[j], ("down", j, way, dist + 1), onward, jnp.logical_and(here, more))
-                wires.send(strips[j], strips[j], ("down_y", j, way, dist), place.across, here)
+            pl.when(here)(lambda: wires.take(strips[j], ("down", j, way, dist), came_from))
+            if dist < 3:
+                wires.send(strips[j], strips[j], ("down", j, way, dist + 1), onward, jnp.logical_and(here, more))
+            wires.send(strips[j], strips[j], ("down_y", j, way, dist), place.across, here)
 
     def down_side_end():
         for way, dist in SIDES:
@@ -760,8 +784,7 @@
         share("cot", g_all)
 
     def gain_sides():
-        for dist in range(4):
-            gain_flood.side(dist)
+        wires.take(gain_all.at[pl.ds(0, 4)], ("gain", "y"), place.across)
 
     gain_a = lambda: gain_row[0:1, :width]
     gain_b = lambda: gain_row[1:2, :width]
@@ -821,15 +844,15 @@
             at = lead_rows(i)
             source = tok_all[at, :].astype(f32)
             n1_all[at, :] = (source * norm(source) * gain_a()).astype(low)
-            pq[i] = nn(n1_all[at, :], w_qkv[...])
             return carry
 
         lax.fori_loop(0, 4, body, 0)
+        pq[...] = nn(n1_all[...], w_qkv[...]).reshape(pq.shape)
         pq_in[ctx] = pq[ctx]
         swap_start("pq", lambda peer: pq.at[peer], lambda sender: pq_in.at[sender])
 
     def pq_end():
-        swap_end("pq", lambda sender: pq_in.at[sender])
+        swap_end("pq", pq_in.at[pl.ds(0, 3)])
         proj[...] = jnp.zeros(proj.shape, f32)
         for j in range(4):
             part = jnp.concatenate([pq_in[j], jnp.zeros((own_rows, 128), f32)], axis=1)
@@ -865,7 +888,7 @@
         stack_heads(query_slab, q_st, score_scale)
 
     def kv_end():
-        swap_end("kv", slot_view)
+        swap_end("kv", kv_all.at[:, :, pl.ds(0, 3 * slots_here)])
 
     stack = q_st.shape[1]
     slots = kv_all.shape[2]
@@ -905,7 +928,7 @@
 
     def feed(tile):
         def body(i, carry):
-            at = pl.ds(pl.multiple_of(i * tall, tall), tall)
+            at = pl.ds(0, 4 * own_rows)
             gate = nn(n2_all[at, :], w_ff[:, tile * span : tile * span + half])
             up = nn(n2_all[at, :], w_ff[:, tile * span + half : tile * span + 2 * half])
             back = nn(g_all[at, :], w_ff[:, tile * span + 2 * half : (tile + 1) * span])
@@ -916,21 +939,21 @@
             d_gu[tile, at, half:] = (back * swish).astype(low)
             return carry
 
-        lax.fori_loop(0, 4 * own_rows // tall, body, 0)
+        body(0, 0)
 
     def grad_ff(tile):
         def body(m, carry):
-            at = pl.ds(pl.multiple_of(m * 128, 128), 128)
+            at = pl.ds(pl.multiple_of(m * width, 128), width)
             d_ff[at, tile * span : tile * span + 2 * half] = tn(n2_all[:, at], d_gu[tile]).astype(low)
             d_ff[at, tile * span + 2 * half : (tile + 1) * span] = tn(g_all[:, at], act[tile]).astype(low)
             return carry
 
-        lax.fori_loop(0, width // 128, body, 0)
+        lax.fori_loop(0, 1, body, 0)
 
     across_core = (1 - x) * 2 + 1 - c
     across_own = (1 - x) * 2 + c
     beside = x * 2 + 1 - c
-    wide_tile = 384
+    wide_tile = width
 
     def group_send(name, ref, box, which):
         lead, mark = ((across_core, "cx"), (beside, "cc"))[which]
@@ -1023,71 +1046,63 @@
         def __init__(self, name, view, side, inbox):
             self.name, self.view, self.side, self.inbox = name, view, side, inbox
 
-        def send(self, dist):
-            for way, dist in KEYS[dist]:
-                here, pos = key_pos(way, dist)
-                wires.send(
-                    self.view(pos + flip), self.side.at[way, dist],
-                    (self.name, "y", way, dist), place.across, here,
-                )
-
-        def send_all(self):
-            for dist in (3, 2, 1, 0):
-                self.send(dist)
-
-        def add(self, dist):
-            for way, dist in KEYS[dist]:
-                z_add(self.name, self.view, self.side, self.inbox, way, dist)
-
-    gu_sides, gu_inboxes = (gu_side_a, gu_side_b), (gu_inbox_a, gu_inbox_b)
+        def send(self, dist, way):
+            way = Way(way) if dist else way
+            here, pos = key_pos(way, dist)
+            wires.send(
+                self.view(pos + flip), self.side.at[way, dist],
+                (self.name, "y", way, dist), place.across, here,
+            )
+
+        def add(self, dist, way):
+            way = Way(way) if dist else way
+            z_add(self.name, self.view, self.side, self.inbox, way, dist)
+
     gu_sinks = [
-        Sink(("dgu", tile), functools.partial(gu_view, d_ff, tile), gu_sides[tile], gu_inboxes[tile])
-        for tile in TILES
+        Sink(("dgu", number), functools.partial(gu_view, d_ff, number), gu_side.at[number], gu_inbox.at[number])
+        for number in range(3)
     ]
     out_sink = Sink("dout", lambda pos: d_out.at[block_rows(pos)], out_side, out_inbox)
     qkv_sink = Sink("dqkv", lambda pos: d_qkv.at[block_rows(pos)], qkv_side, qkv_inbox)
     d_strips, d_other_strips = strips_of(d_ff, lanes), strips_of(d_ff, other_lanes)
 
-    def down_send(tile):
-        for j in range(4):
-            wires.send(d_other_strips[j], down_side.at[j], ("ddown_y", j), place.across, (1 - y) == tile)
-
-    def down_add(dist):
+    def down_send(tile, j):
+        wires.send(d_other_strips[j], down_side.at[j], ("ddown_y", j), place.across, (1 - y) == tile)
+
+    def down_add(dist, j):
         if dist == 0:
-            for j in range(4):
-
-                def finish():
-                    wires.take(down_side.at[j], ("ddown_y", j), place.across)
-                    add_rows(d_strips[j], [down_side.at[j]])
-                    for end, fed, feeder in ((BELOW, place.has_up, place.up), (ABOVE, place.has_down, place.down)):
-
-                        def more():
-                            wires.take(down_inbox.at[end, j], ("ddown", j, end, 0), feeder)
-                            add_rows(d_strips[j], [down_inbox.at[end, j]])
-
-                        pl.when(fed)(more)
-
-                pl.when(at_home)(finish)
+
+            def finish():
+                wires.take(down_side.at[j], ("ddown_y", j), place.across)
+                add_rows(d_strips[j], [down_side.at[j]])
+                for end, fed, feeder in ((BELOW, place.has_up, place.up), (ABOVE, place.has_down, place.down)):
+
+                    def more():
+                        wires.take(down_inbox.at[end, j], ("ddown", j, end, 0), feeder)
+                        add_rows(d_strips[j], [down_inbox.at[end, j]])
+
+                    pl.when(fed)(more)
+
+            pl.when(at_home)(finish)
             return
         for way in (BELOW, ABOVE):
             here = (z - ctx if way == BELOW else ctx - z) == dist
             fed = place.has_up if way == BELOW else place.has_down
             feeder = place.up if way == BELOW else place.down
             onward = place.down if way == BELOW else place.up
-            for j in range(4):
-
-                def first():
-                    wires.take(down_side.at[j], ("ddown_y", j), place.across)
-                    add_rows(d_strips[j], [down_side.at[j]])
-
-                def more():
-                    wires.take(down_side.at[j], ("ddown_y", j), place.across)
-                    wires.take(down_inbox.at[way, j], ("ddown", j, way, dist), feeder)
-                    add_rows(d_strips[j], [down_side.at[j], down_inbox.at[way, j]])
-
-                pl.when(jnp.logical_and(here, jnp.logical_not(fed)))(first)
-                pl.when(jnp.logical_and(here, fed))(more)
-                wires.send(d_strips[j], down_inbox.at[way, j], ("ddown", j, way, dist - 1), onward, here)
+
+            def first():
+                wires.take(down_side.at[j], ("ddown_y", j), place.across)
+                add_rows(d_strips[j], [down_side.at[j]])
+
+            def more():
+                wires.take(down_side.at[j], ("ddown_y", j), place.across)
+                wires.take(down_inbox.at[way, j], ("ddown", j, way, dist), feeder)
+                add_rows(d_strips[j], [down_side.at[j], down_inbox.at[way, j]])
+
+            pl.when(jnp.logical_and(here, jnp.logical_not(fed)))(first)
+            pl.when(jnp.logical_and(here, fed))(more)
+            wires.send(d_strips[j], down_inbox.at[way, j], ("ddown", j, way, dist - 1), onward, here)
 
     class PairSink:
         def __init__(self, name, ref, cols, inbox, side):
@@ -1099,7 +1114,7 @@
         def one(self, pos):
             return self.ref.at[block_rows(pos), self.cols]
 
-        def add(self, dist):
+        def add(self, dist, way):
             if dist == 0:
                 mine = self.pair(z)
                 for end, fed, feeder in ((BELOW, place.has_up, place.up), (ABOVE, place.has_down, place.down)):
@@ -1111,41 +1126,41 @@
                     pl.when(fed)(more)
                 wires.send(self.one(place.across[0]), self.side, (self.name, "y"), place.across)
                 return
-            for way, dist in KEYS[dist]:
-                here = source_valid(place, way, dist)
-                mine = self.pair(z - dist if way == BELOW else z + dist)
-                fed = place.has_up if way == BELOW else place.has_down
-                feeder = place.up if way == BELOW else place.down
-                onward = place.down if way == BELOW else place.up
-                if dist < 3:
-
-                    def more():
-                        wires.take(self.inbox.at[way, dist], (self.name, "z", way, dist), feeder)
-                        add_rows(mine, [self.inbox.at[way, dist]])
-
-                    pl.when(jnp.logical_and(here, fed))(more)
-                wires.send(mine, self.inbox.at[way, dist - 1], (self.name, "z", way, dist - 1), onward, here)
+            way = Way(way)
+            here = source_valid(place, way, dist)
+            mine = self.pair(z - dist if way == BELOW else z + dist)
+            fed = place.has_up if way == BELOW else place.has_down
+            feeder = place.up if way == BELOW else place.down
+            onward = place.down if way == BELOW else place.up
+            if dist < 3:
+
+                def more():
+                    wires.take(self.inbox.at[way, dist], (self.name, "z", way, dist), feeder)
+                    add_rows(mine, [self.inbox.at[way, dist]])
+
+                pl.when(jnp.logical_and(here, fed))(more)
+            wires.send(mine, self.inbox.at[way, dist - 1], (self.name, "z", way, dist - 1), onward, here)
 
         def end(self):
             wires.take(self.side, (self.name, "y"), place.across)
             add_rows(self.one(dp), [self.side])
 
-    up_sink = PairSink("dup", d_ff, up_cols, up_inbox, up_side)
-
-    def gu_finish(tile):
-        for part in range(2):
-            target = part * 2 + x
-            block = d_ff.at[my_rows, pl.ds(tile * span + part * half, half)]
-            wires.send(block, gu_mix.at[c, tile], ("dgu_mix", tile, 0), (dp, target), target != ctx, extra=c)
-            pl.when(target == ctx)(lambda: add_rows(block, [], out=gu_mix.at[c, tile]))
-        wires.slot(("dgu_mix", tile, 1))
-
-    def gu_end(tile):
-        for part in range(2):
-            origin = 2 * c + part
-            box = gu_mix.at[part, tile]
-            pl.when(origin != ctx)(lambda: wires.take(box, ("dgu_mix", tile, part), (dp, origin)))
-            add_rows(box, [], out=gu_out.at[:, pl.ds((2 * part + tile) * half, half)])
+    up_sink = PairSink("dup", d_ff, part_cols(3), up_inbox, up_side)
+
+    def gu_finish(number):
+        tile, part = PARTS[number]
+        target = part * 2 + x
+        block = gu_view(d_ff, number, dp)
+        wires.slot(("dgu_mix", tile), 2)
+        wires.send(block, gu_mix.at[c, tile], ("dgu_mix", tile), (dp, target), target != ctx, extra=c)
+        pl.when(target == ctx)(lambda: add_rows(block, [], out=gu_mix.at[c, tile]))
+
+    def gu_end(number):
+        tile, part = PARTS[number]
+        origin = 2 * c + part
+        box = gu_mix.at[part, tile]
+        pl.when(origin != ctx)(lambda: wires.take(box, ("dgu_mix", tile), (dp, origin), extra=part))
+        add_rows(box, [], out=gu_out.at[:, pl.ds((2 * part + tile) * half, half)])
 
     def down_finish():
         for j in range(4):
@@ -1220,15 +1235,15 @@
         group_send("dkv", dkv, dkv_box, 1)
 
     def gb_end():
-        swap_end("gb", lambda sender: gb_all.at[lead_rows(sender)])
+        swap_end("gb", gb_all.at[pl.ds(0, 3 * own_rows)])
 
     def grad_out(m, carry):
-        at = pl.ds(pl.multiple_of(m * 128, 128), 128)
+        at = pl.ds(pl.multiple_of(m * width, 128), width)
         d_out[at, :] = tn(ctx_all[:, at], gb_all[...]).astype(low)
         return carry
 
     def grad_out_all():
-        lax.fori_loop(0, width // 128, grad_out, 0)
+        lax.fori_loop(0, 1, grad_out, 0)
 
     def grad_mixed():
         sums = group_end("dkv", dkv, dkv_box)
@@ -1252,15 +1267,15 @@
         swap_start("gm", lambda peer: gm.at[peer], lambda sender: gm_all.at[lead_rows(sender)])
 
     def gm_end():
-        swap_end("gm", lambda sender: gm_all.at[lead_rows(sender)])
+        swap_end("gm", gm_all.at[pl.ds(0, 3 * own_rows)])
 
     def grad_qkv(m, carry):
-        at = pl.ds(pl.multiple_of(m * 128, 128), 128)
+        at = pl.ds(pl.multiple_of(m * width, 128), width)
         d_qkv[at, :] = tn(n1_all[:, at], gm_all[...]).astype(low)
         return carry
 
     def grad_qkv_all():
-        lax.fori_loop(0, width // 128, grad_qkv, 0)
+        lax.fori_loop(0, 1, grad_qkv, 0)
 
     tokens_terms = [(lambda at: gm_all[at, :], lambda at: w_qkv[at, :])]
 
@@ -1340,167 +1355,276 @@
     qkv_start()
     out_start()
     tokens_start()
-    out_chip(0, 0)
-    qkv_flood.hop(1)
+    out_chip(0, 0, 0)
+    qkv_flood.hop(1, 0)
+    qkv_flood.hop(1, 1)
     down_mix_start()
     mix_start(1)
     tables()
     locals_end()
     mix_end(0)
+    mix_end(1)
     gu_floods[0].start()
+    gu_floods[1].start()
     cot_start()
     gain_start()
-    gain_flood.hop(1)
-    out_flood.hop(1)
-    gain_flood.hop(2)
-    gain_flood.hop(3)
-    qkv_flood.hop(2)
-    qkv_flood.side(1)
-    qkv_flood.hop(3)
+    gain_flood.hop(1, 0)
+    gain_flood.hop(1, 1)
+    out_flood.hop(1, 0)
+    out_flood.hop(1, 1)
+    gain_flood.hop(2, 0)
+    gain_flood.hop(2, 1)
+    gain_flood.hop(3, 0)
+    gain_flood.hop(3, 1)
+    qkv_flood.hop(2, 0)
+    qkv_flood.hop(2, 1)
+    qkv_flood.side(1, 0)
+    qkv_flood.side(1, 1)
+    qkv_flood.hop(3, 0)
+    qkv_flood.hop(3, 1)
     share_on("tok", tok_all)
-    out_flood.side(0)
-    down_start()
-    out_flood.hop(2)
-    qkv_flood.side(3)
+    out_flood.side(0, 0)
+    down_start(0)
+    down_start(1)
+    down_start(2)
+    down_start(3)
+    out_flood.hop(2, 0)
+    out_flood.hop(2, 1)
+    qkv_flood.side(3, 0)
+    qkv_flood.side(3, 1)
     gain_sides()
-    mix_end(1)
+    mix_end(2)
+    mix_end(3)
     up_flood.start()
-    gu_floods[1].start()
-    qkv_flood.side(0)
-    qkv_flood.side(2)
+    gu_floods[2].start()
+    qkv_flood.side(0, 0)
+    qkv_flood.side(2, 0)
+    qkv_flood.side(2, 1)
     share_end("tok", tok_all)
     project()
-    gu_floods[0].side(0)
-    out_flood.hop(3)
-    down_hop(1)
+    out_flood.hop(3, 0)
+    out_flood.hop(3, 1)
+    down_hop(1, 0)
+    down_hop(1, 1)
+    down_hop(1, 2)
+    down_hop(1, 3)
     share_on("cot", g_all)
-    gu_floods[1].hop(1)
+    gu_floods[2].hop(1, 0)
+    gu_floods[2].hop(1, 1)
     share_end("cot", g_all)
-    gu_floods[0].hop(1)
-    out_chip(0, 2)
-    out_chip(0, 1)
+    gu_floods[0].hop(1, 0)
+    gu_floods[1].hop(1, 0)
+    gu_floods[0].hop(1, 1)
+    gu_floods[1].hop(1, 1)
+    out_chip(0, 2, 0)
+    out_chip(0, 2, 1)
+    out_chip(0, 1, 0)
+    out_chip(0, 1, 1)
     pq_end()
     kv_start()
-    out_flood.side(1)
-    down_hop(2)
-    out_flood.side(3)
+    out_flood.side(1, 0)
+    out_flood.side(1, 1)
+    down_hop(2, 0)
+    down_hop(2, 1)
+    down_hop(2, 2)
+    down_hop(2, 3)
+    out_flood.side(3, 0)
+    out_flood.side(3, 1)
     queries()
-    down_hop(3)
-    out_flood.side(2)
+    down_hop(3, 0)
+    down_hop(3, 1)
+    down_hop(3, 2)
+    down_hop(3, 3)
+    out_flood.side(2, 0)
+    out_flood.side(2, 1)
     kv_end()
     up_flood.side()
     attention()
-    gu_floods[1].side(1)
-    out_chip(1, 2)
-    gu_floods[0].hop(2)
-    out_chip(1, 0)
-    out_chip(0, 3)
-    out_chip(1, 1)
-    out_chip(1, 3)
+    out_chip(1, 2, 0)
+    out_chip(1, 2, 1)
+    gu_floods[0].hop(2, 0)
+    gu_floods[1].hop(2, 0)
+    gu_floods[0].hop(2, 1)
+    gu_floods[1].hop(2, 1)
+    out_chip(1, 0, 0)
+    out_chip(0, 3, 0)
+    out_chip(0, 3, 1)
+    out_chip(1, 1, 0)
+    out_chip(1, 1, 1)
+    out_chip(1, 3, 0)
+    out_chip(1, 3, 1)
     out_core()
     out_project()
-    up_flood.hop(1)
-    gu_floods[0].side(1)
-    gu_floods[0].hop(3)
+    up_flood.hop(1, 0)
+    up_flood.hop(1, 1)
+    gu_floods[0].hop(3, 0)
+    gu_floods[1].hop(3, 0)
+    gu_floods[0].hop(3, 1)
+    gu_floods[1].hop(3, 1)
     down_side_end()
-    gu_floods[1].hop(2)
+    gu_floods[2].hop(2, 0)
+    gu_floods[2].hop(2, 1)
     share_on("n2", n2_all)
-    up_flood.hop(2)
-    gu_floods[1].side(0)
-    gu_floods[0].side(2)
-    gu_floods[0].side(3)
+    up_flood.hop(2, 0)
+    up_flood.hop(2, 1)
+    gu_sides(0)
+    gu_sides(1)
     share_end("n2", n2_all)
     feed(0)
-    gu_floods[1].hop(3)
+    gu_floods[2].hop(3, 0)
+    gu_floods[2].hop(3, 1)
     grad_ff(0)
-    gu_sinks[0].send(3)
-    gu_sinks[0].send(2)
-    gu_floods[1].side(3)
-    gu_floods[1].side(2)
-    up_flood.hop(3)
+    gu_sinks[0].send(3, 0)
+    gu_sinks[1].send(3, 0)
+    gu_sinks[0].send(3, 1)
+    gu_sinks[1].send(3, 1)
+    gu_sinks[0].send(2, 0)
+    gu_sinks[1].send(2, 0)
+    gu_sinks[0].send(2, 1)
+    gu_sinks[1].send(2, 1)
+    gu_sides(2)
+    up_flood.hop(3, 0)
+    up_flood.hop(3, 1)
     feed(1)
     grad_ff(1)
-    up_sink.add(3)
-    gu_sinks[1].send(3)
-    down_send(1)
-    down_send(0)
-    gu_sinks[0].send(1)
-    gu_sinks[1].send(2)
-    gu_sinks[0].add(3)
-    gu_sinks[1].send(0)
+    up_sink.add(3, 0)
+    up_sink.add(3, 1)
+    gu_sinks[2].send(3, 0)
+    gu_sinks[2].send(3, 1)
+    down_send(1, 0)
+    down_send(1, 1)
+    down_send(1, 2)
+    down_send(1, 3)
+    down_send(0, 0)
+    down_send(0, 1)
+    down_send(0, 2)
+    down_send(0, 3)
+    gu_sinks[0].send(1, 0)
+    gu_sinks[1].send(1, 0)
+    gu_sinks[0].send(1, 1)
+    gu_sinks[1].send(1, 1)
+    gu_sinks[2].send(2, 0)
+    gu_sinks[2].send(2, 1)
+    gu_sinks[0].add(3, 0)
+    gu_sinks[1].add(3, 0)
+    gu_sinks[0].add(3, 1)
+    gu_sinks[1].add(3, 1)
+    gu_sinks[2].send(0, 0)
     gp_block(0)
     share_on("ctx", ctx_all)
     group_on("gp", gp, gp_box)
-    gu_sinks[0].send(0)
+    gu_sinks[0].send(0, 0)
+    gu_sinks[1].send(0, 0)
     op_block(1)
     op_block(0)
-    up_sink.add(2)
+    up_sink.add(2, 0)
+    up_sink.add(2, 1)
     gp_block(1)
-    gu_sinks[1].add(3)
-    gu_sinks[0].add(2)
+    gu_sinks[2].add(3, 0)
+    gu_sinks[2].add(3, 1)
+    gu_sinks[0].add(2, 0)
+    gu_sinks[1].add(2, 0)
+    gu_sinks[0].add(2, 1)
+    gu_sinks[1].add(2, 1)
     hidden_back()
     grad_context()
     attention_back()
-    up_sink.add(1)
+    up_sink.add(1, 0)
+    up_sink.add(1, 1)
     group_on("dkv", dkv, dkv_box)
     gb_end()
     share_end("ctx", ctx_all)
     grad_out_all()
-    gu_sinks[1].send(1)
-    out_sink.send(3)
-    down_add(3)
+    gu_sinks[2].send(1, 0)
+    gu_sinks[2].send(1, 1)
+    out_sink.send(3, 0)
+    out_sink.send(3, 1)
+    down_add(3, 0)
+    down_add(3, 1)
+    down_add(3, 2)
+    down_add(3, 3)
     grad_mixed()
-    gu_sinks[0].add(1)
-    down_add(2)
-    out_sink.send(1)
+    gu_sinks[0].add(1, 0)
+    gu_sinks[1].add(1, 0)
+    gu_sinks[0].add(1, 1)
+    gu_sinks[1].add(1, 1)
+    down_add(2, 0)
+    down_add(2, 1)
+    down_add(2, 2)
+    down_add(2, 3)
+    out_sink.send(1, 0)
+    out_sink.send(1, 1)
     group_on("op", op, op_box)
-    gu_sinks[1].add(2)
+    gu_sinks[2].add(2, 0)
+    gu_sinks[2].add(2, 1)
     gm_end()
     gt_block(0)
     gt_block(1)
-    up_sink.add(0)
+    up_sink.add(0, 0)
     grad_qkv_all()
-    qkv_sink.send(3)
-    out_sink.send(2)
+    qkv_sink.send(3, 0)
+    qkv_sink.send(3, 1)
+    out_sink.send(2, 0)
+    out_sink.send(2, 1)
     group_on("gt", gp, gp_box)
-    qkv_sink.send(2)
-    down_add(1)
-    gu_sinks[0].add(0)
+    qkv_sink.send(2, 0)
+    qkv_sink.send(2, 1)
+    down_add(1, 0)
+    down_add(1, 1)
+    down_add(1, 2)
+    down_add(1, 3)
+    gu_sinks[0].add(0, 0)
+    gu_sinks[1].add(0, 0)
     gu_finish(0)
+    gu_finish(1)
     tokens_end()
     gain_send(0)
     gain_take(0)
-    gu_sinks[1].add(1)
+    gu_sinks[2].add(1, 0)
+    gu_sinks[2].add(1, 1)
     gain_send(1)
     gain_take(1)
-    out_sink.add(3)
+    out_sink.add(3, 0)
+    out_sink.add(3, 1)
     gain_send(2)
-    qkv_sink.send(1)
-    qkv_sink.add(3)
-    out_sink.add(2)
-    qkv_sink.add(2)
-    down_add(0)
+    qkv_sink.send(1, 0)
+    qkv_sink.send(1, 1)
+    qkv_sink.add(3, 0)
+    qkv_sink.add(3, 1)
+    out_sink.add(2, 0)
+    out_sink.add(2, 1)
+    qkv_sink.add(2, 0)
+    qkv_sink.add(2, 1)
+    down_add(0, 0)
+    down_add(0, 1)
+    down_add(0, 2)
+    down_add(0, 3)
     down_finish()
     gain_take(2)
-    gu_sinks[1].add(0)
-    out_sink.send(0)
-    qkv_sink.send(0)
+    gu_sinks[2].add(0, 0)
+    out_sink.send(0, 0)
+    qkv_sink.send(0, 0)
     output_end()
     up_sink.end()
     gain_send(3)
-    out_sink.add(1)
+    out_sink.add(1, 0)
+    out_sink.add(1, 1)
     gain_take(3)
-    gu_finish(1)
+    gu_finish(2)
+    gu_finish(3)
     gain_send(4)
-    qkv_sink.add(1)
-    out_sink.add(0)
+    qkv_sink.add(1, 0)
+    qkv_sink.add(1, 1)
+    out_sink.add(0, 0)
     gain_take(4)
     gain_send(5)
     out_end()
     gu_end(0)
+    gu_end(1)
     down_end()
-    gu_end(1)
-    qkv_sink.add(0)
+    gu_end(2)
+    gu_end(3)
+    qkv_sink.add(0, 0)
     qkv_end()
     gain_take(5)
     wires.drain()
@@ -1569,14 +1693,14 @@
         box(4, own_rows, width), box(3, own_rows, width),
         box(4, seq_count, 2 * slabs, row_count, 128), box(3, seq_count, 2 * slabs, row_count, 128),
         box(2, 4, rows, qkv_wide), box(2, 4, rows, out_wide),
-        box(2, 4, rows, 2 * half), box(2, 4, rows, half), box(4, strip, half),
+        box(3, 2, 4, rows, half), box(4, strip, half),
         box(2, 3, rows, qkv_wide), box(2, 3, rows, out_wide),
-        box(2, 3, rows, 2 * half), box(2, 3, rows, half), box(2, 4, strip, half),
+        box(3, 2, 3, rows, half), box(2, 4, strip, half),
         box(2, 3, 2 * rows, half), box(rows, half),
         box(2, 2, rows, half), box(strip, half),
         box(6, 8, width, dtype=f32), box(6, 8, width, dtype=f32),
-        pltpu.SemaphoreType.DMA((400,)),
-        pltpu.SemaphoreType.DMA((400,)),
+        pltpu.SemaphoreType.DMA((SENDS,)),
+        pltpu.SemaphoreType.DMA((180,)),
         pltpu.SemaphoreType.DMA((8,)),
     ]
     vmem = pl.BlockSpec(memory_space=pltpu.MemorySpace.VMEM)

time: 182 us -> 175 us (0.962)
  Pallas kernels: 181 us -> 173 us
    pallas_call x1, Pallas kernels: 178 us -> 171 us  [on_device_fast(): pl.pallas_call(functools.partial(layer_kernel, {}), out_shape=shapes, in_...]
where the time goes in v6:
time: 175 us; the launch traced here: 174 us
  Pallas kernels  173 us (99%)
    pallas_call x1, Pallas kernels, on_device_fast(): pl.pallas_call(functools.partial(layer_kernel, {}), out_shape=shapes, in_...  171 us

profile of v6, /device:TPU:0, one launch (start us, length us, event | category | flops | bytes accessed | tf_op | source)
XLA Modules:
  0.0 174.1 jit_solution(779187877168057965)
XLA Ops:
  0.6 170.6 %layer.1 = (bf16[128,1152]{1,0:T(8,128)(2,1)}, bf16[128,1152]{1,0:T(8,128)(2,1)}, f32[8,1152]{1,0:T(8,128)}, bf16[144,512]{1,0:T(8,128)(2,1)}, bf16[144,384]{1,0...) custom-call(bf16[128,1152]{1,0:T(8,128)(2,1)} %bitcast.6, bf16[128,1152]{1,0:T(8,128)(2,1)} %bitcast.7, ...), custom_call_target="tpu_custom_call" | custom-call | tf_op jit(solution)/shard_map/layer/pallas_call | solution.py:1717
  171.3 2.8 %finish.1 = (bf16[128,1152]{1,0:T(8,128)(2,1)}, bf16[128,1152]{1,0:T(8,128)(2,1)}, f32[144,480]{1,0:T(8,128)}, f32[144,288]{1,0:T(8,128)}, f32[144,1536]{1,0:T(8...) custom-call(bf16[128,1152]{1,0:T(8,128)(2,1)} %get-tuple-element.23.output, ...), custom_call_target="tpu_custom_call" | custom-call | tf_op jit(solution)/shard_map/finish/pallas_call | solution.py:1732

commit v7 on v6

--- a/solution.py
+++ b/solution.py
@@ -351,17 +351,19 @@
 
 
 BELOW, ABOVE = Way.BELOW, Way.ABOVE
-SENDS = 80
+RINGS = (12, 16, 28, 24, 16)
+SENDS = sum(RINGS)
 
 
 class Wires:
-    def __init__(self, send_sems, recv_sems, names):
+    def __init__(self, send_sems, recv_sems, names, place):
+        self.kinds = ((place.core,), (place.chip,), (place.across,), (place.up, place.down))
+        self.counts = [0] * len(RINGS)
         self.send_sems = send_sems
         self.recv_sems = recv_sems
         self.index = names
         self.total = sum(names.values()) if names else 0
         self.base = {}
-        self.count = 0
         self.live = {}
 
     def slot(self, name, size=1):
@@ -386,16 +388,20 @@
         return self.slot(name)
 
     def send(self, src, dst, name, device, cond=None, extra=None):
-        number = self.count
-        self.count += 1
-        self.settle(number - SENDS)
+        kind = 4
+        for at, devices in enumerate(self.kinds):
+            if any(device is known for known in devices):
+                kind = at
+        number = (kind, self.counts[kind])
+        self.counts[kind] += 1
+        self.settle((kind, number[1] - RINGS[kind]))
         at = self.spot(name, lax.div(device[0], 2))
         if extra is not None:
             at = at + extra
         copy = pltpu.make_async_remote_copy(
             src_ref=src,
             dst_ref=dst,
-            send_sem=self.send_sems.at[number % SENDS],
+            send_sem=self.send_sems.at[sum(RINGS[:kind]) + number[1] % RINGS[kind]],
             recv_sem=self.recv_sems.at[at],
             device_id=device,
             device_id_type=MESH,
@@ -492,7 +498,8 @@
 def add_rows(dst, srcs, out=None, cast=None, chunk=48):
     out = dst if out is None else out
     total_rows = dst.shape[0]
-    assert total_rows % chunk == 0
+    if total_rows % chunk:
+        chunk = total_rows
 
     def body(i, carry):
         at = pl.ds(pl.multiple_of(i * chunk, 16), chunk)
@@ -531,7 +538,7 @@
     names,
     tokens, cot, lengths, qkv_in, out_in, gu_in, dt_in, gain_one, gain_two, cos_table, sin_table,
     output, grad_tokens, gain_out, qkv_out, out_out, gu_out, dt_out,
-    w_qkv, w_out, w_ff, d_qkv, d_out, d_ff, gain_all, gain_row, cos, sin,
+    w_qkv, w_out, w_rest, out_pad, w_ff, d_qkv, d_out, d_ff, gain_all, gain_row, cos, sin,
     tok_all, n1_all, n2_all, g_all, ctx_all, hidden, grad_hidden, proj, q_st, kv_all, p_st, att, go_st,
     wide, gm, pq, pq_in, gb_all, gm_all, act, d_gu, gp, gp_box, op, op_box, dkv, dkv_box,
     qkv_side, out_side, gu_side, down_side, qkv_inbox, out_inbox, gu_inbox, down_inbox,
@@ -540,7 +547,7 @@
 ):
     f32, low = jnp.float32, jnp.bfloat16
     place = Place()
-    wires = Wires(send_sems, recv_sems, names)
+    wires = Wires(send_sems, recv_sems, names, place)
     dp, ctx, z, y, x, c = place.dp, place.ctx, place.z, place.y, place.x, place.c
     rows = qkv_in.shape[0]
     strip, half = dt_in.shape
@@ -548,7 +555,12 @@
     own_rows = tokens.shape[0]
     slots_here = own_rows // 2
     qkv_cols, out_cols = qkv_in.shape[1], out_in.shape[1]
-    qkv_wide, out_wide = w_qkv.shape[1], w_out.shape[2]
+    qkv_wide, out_wide = w_qkv.shape[1], out_pad.shape[1]
+    main = w_out.shape[2]
+    packed = w_out.shape[1] // 8
+    spare = packed - rows
+    rest = out_cols - main
+    pieces = -(-rows // spare)
     group = QH // KVH
     slabs = KVH // 2
     q_slabs = QH // 2
@@ -645,8 +657,39 @@
                 more = place.has_up if way == BELOW else place.has_down
                 wires.send(view, view, (self.name, way, dist + 1), onward, jnp.logical_and(here, more))
 
+    def packed_rows(pos):
+        return pl.ds(pl.multiple_of(pos * packed, 16), packed)
+
+    def pack(values, dest):
+        dest[:rows, :] = values[:, :main].astype(low)
+        for slab in range(0, main, 128):
+            total = jnp.zeros((spare, 128), f32)
+            for number in range(slab // rest, min(pieces, (slab + 128) // rest)):
+                height = min(spare, rows - number * spare)
+                piece = values[number * spare : number * spare + height, main : main + 128]
+                if height < spare:
+                    piece = jnp.concatenate([piece, jnp.zeros((spare - height, 128), f32)], axis=0)
+                shift = number * rest - slab
+                total = total + (pltpu.roll(piece, shift, 1) if shift else piece)
+            dest[rows:, slab : slab + 128] = total.astype(low)
+
+    def unpack(view, dest):
+        keep = lax.broadcasted_iota(jnp.int32, (spare, 128), 1) < rest
+        for number in range(pieces):
+            slab = number * rest // 128 * 128
+            shift = number * rest - slab
+            piece = view[rows:, slab : slab + 128].astype(f32)
+            piece = pltpu.roll(piece, 128 - shift, 1) if shift else piece
+            height = min(spare, rows - number * spare)
+            piece = jnp.where(keep, piece, 0.0).astype(low)
+            dest[number * spare : number * spare + height, :] = piece[:height]
+
+    def out_weights(j):
+        first = jnp.concatenate([w_out[j, pos * packed : pos * packed + rows, :] for pos in range(8)], axis=0)
+        return jnp.concatenate([first, w_rest[j]], axis=1)
+
     def out_block(lead, pos):
-        return w_out.at[lead, block_rows(pos)]
+        return w_out.at[lead, packed_rows(pos)]
 
     def out_spread(view, pos, key, cond):
         wires.send(view, out_block(ctx, pos), ("out", "x") + key, place.chip, cond)
@@ -775,8 +818,9 @@
         gain_flood.start()
 
     def out_start():
-        w_out[ctx, my_rows, :] = jnp.zeros((rows, out_wide), low)
-        w_out[ctx, my_rows, :out_cols] = out_in[...]
+        out_pad[...] = jnp.zeros(out_pad.shape, low)
+        out_pad[:, :out_cols] = out_in[...]
+        pack(out_pad[...].astype(f32), out_block(ctx, dp))
         out_flood.start()
 
     def cot_start():
@@ -914,9 +958,12 @@
         share("ctx", ctx_all)
 
     def out_project():
+        for j in range(4):
+            for pos in range(8):
+                unpack(w_out.at[j, packed_rows(pos)], w_rest.at[j, block_rows(pos)])
         hidden[...] = tokens[...].astype(f32)
         for j in range(4):
-            part = nn(ctx_all[here_rows, :], w_out[j])
+            part = nn(ctx_all[here_rows, :], out_weights(j))
             at = out_cols * j
             if at % 128:
                 part = pltpu.roll(part, at % 128, 1)
@@ -1062,7 +1109,7 @@
         Sink(("dgu", number), functools.partial(gu_view, d_ff, number), gu_side.at[number], gu_inbox.at[number])
         for number in range(3)
     ]
-    out_sink = Sink("dout", lambda pos: d_out.at[block_rows(pos)], out_side, out_inbox)
+    out_sink = Sink("dout", lambda pos: d_out.at[packed_rows(pos)], out_side, out_inbox)
     qkv_sink = Sink("dqkv", lambda pos: d_qkv.at[block_rows(pos)], qkv_side, qkv_inbox)
     d_strips, d_other_strips = strips_of(d_ff, lanes), strips_of(d_ff, other_lanes)
 
@@ -1203,10 +1250,10 @@
         swap_start("gb", lambda peer: wide.at[peer], lambda sender: gb_all.at[lead_rows(sender)])
 
     def context_back(n, carry):
-        at = pl.ds(pl.multiple_of(n * wide_tile, 128), wide_tile)
-        total = nt(wide[0], w_out[0, at, :])
+        at = pl.ds(0, width)
+        total = nt(wide[0], out_weights(0))
         for j in range(1, 4):
-            total = total + nt(wide[j], w_out[j, at, :])
+            total = total + nt(wide[j], out_weights(j))
         proj[:, at] = total
         return carry
 
@@ -1237,13 +1284,10 @@
     def gb_end():
         swap_end("gb", gb_all.at[pl.ds(0, 3 * own_rows)])
 
-    def grad_out(m, carry):
-        at = pl.ds(pl.multiple_of(m * width, 128), width)
-        d_out[at, :] = tn(ctx_all[:, at], gb_all[...]).astype(low)
-        return carry
-
     def grad_out_all():
-        lax.fori_loop(0, 1, grad_out, 0)
+        result = tn(ctx_all[...], gb_all[...])
+        for pos in range(8):
+            pack(result[pos * rows : (pos + 1) * rows], d_out.at[packed_rows(pos)])
 
     def grad_mixed():
         sums = group_end("dkv", dkv, dkv_box)
@@ -1342,7 +1386,9 @@
             pl.when(mid_high)(done)
 
     def out_end():
-        out_out[...] = d_out[my_rows, :]
+        mine = d_out.at[packed_rows(dp)]
+        out_out[:, :main] = mine[:rows, :]
+        unpack(mine, out_out.at[:, pl.ds(main, 128)])
 
     def qkv_end():
         qkv_out[...] = d_qkv[my_rows, :]
@@ -1354,276 +1400,276 @@
     mix_start(0)
     qkv_start()
     out_start()
+    down_mix_start()
+    tables()
     tokens_start()
+    mix_start(1)
+    cot_start()
     out_chip(0, 0, 0)
+    mix_end(0)
+    locals_end()
+    gu_floods[0].start()
+    qkv_flood.hop(1, 1)
+    mix_end(1)
+    out_flood.hop(1, 1)
+    out_flood.side(0, 0)
     qkv_flood.hop(1, 0)
-    qkv_flood.hop(1, 1)
-    down_mix_start()
-    mix_start(1)
-    tables()
-    locals_end()
-    mix_end(0)
-    mix_end(1)
-    gu_floods[0].start()
-    gu_floods[1].start()
-    cot_start()
+    qkv_flood.hop(2, 0)
     gain_start()
     gain_flood.hop(1, 0)
+    gain_flood.hop(2, 0)
+    gain_flood.hop(3, 0)
+    out_flood.hop(1, 0)
+    gu_floods[1].start()
     gain_flood.hop(1, 1)
-    out_flood.hop(1, 0)
-    out_flood.hop(1, 1)
-    gain_flood.hop(2, 0)
     gain_flood.hop(2, 1)
-    gain_flood.hop(3, 0)
     gain_flood.hop(3, 1)
-    qkv_flood.hop(2, 0)
     qkv_flood.hop(2, 1)
+    qkv_flood.hop(3, 1)
+    out_flood.hop(2, 0)
     qkv_flood.side(1, 0)
-    qkv_flood.side(1, 1)
     qkv_flood.hop(3, 0)
-    qkv_flood.hop(3, 1)
+    down_start(1)
     share_on("tok", tok_all)
-    out_flood.side(0, 0)
+    out_flood.hop(2, 1)
+    out_flood.hop(3, 1)
+    mix_end(2)
+    gu_floods[2].start()
     down_start(0)
-    down_start(1)
-    down_start(2)
-    down_start(3)
-    out_flood.hop(2, 0)
-    out_flood.hop(2, 1)
+    gain_sides()
     qkv_flood.side(3, 0)
-    qkv_flood.side(3, 1)
-    gain_sides()
-    mix_end(2)
-    mix_end(3)
-    up_flood.start()
-    gu_floods[2].start()
-    qkv_flood.side(0, 0)
     qkv_flood.side(2, 0)
     qkv_flood.side(2, 1)
+    down_start(3)
     share_end("tok", tok_all)
+    gu_floods[0].hop(1, 0)
+    qkv_flood.side(3, 1)
+    qkv_flood.side(0, 0)
+    qkv_flood.side(1, 1)
     project()
+    down_hop(1, 1)
+    down_hop(2, 1)
+    down_hop(1, 0)
+    down_hop(2, 0)
     out_flood.hop(3, 0)
-    out_flood.hop(3, 1)
-    down_hop(1, 0)
-    down_hop(1, 1)
+    mix_end(3)
+    out_chip(0, 1, 0)
+    up_flood.start()
+    down_start(2)
+    down_hop(1, 3)
     down_hop(1, 2)
-    down_hop(1, 3)
-    share_on("cot", g_all)
+    down_hop(2, 2)
+    gu_floods[0].hop(2, 0)
     gu_floods[2].hop(1, 0)
-    gu_floods[2].hop(1, 1)
-    share_end("cot", g_all)
-    gu_floods[0].hop(1, 0)
-    gu_floods[1].hop(1, 0)
-    gu_floods[0].hop(1, 1)
-    gu_floods[1].hop(1, 1)
-    out_chip(0, 2, 0)
-    out_chip(0, 2, 1)
-    out_chip(0, 1, 0)
-    out_chip(0, 1, 1)
     pq_end()
     kv_start()
+    gu_floods[0].hop(1, 1)
+    out_flood.side(3, 0)
+    down_hop(3, 2)
+    out_chip(0, 3, 0)
+    gu_floods[0].hop(3, 0)
+    share_on("cot", g_all)
+    gu_floods[1].hop(1, 1)
+    queries()
+    out_flood.side(1, 1)
+    down_hop(2, 3)
+    gu_floods[2].hop(1, 1)
     out_flood.side(1, 0)
-    out_flood.side(1, 1)
-    down_hop(2, 0)
-    down_hop(2, 1)
-    down_hop(2, 2)
-    down_hop(2, 3)
-    out_flood.side(3, 0)
+    out_chip(0, 1, 1)
+    down_hop(3, 1)
+    out_flood.side(2, 0)
     out_flood.side(3, 1)
-    queries()
+    down_hop(3, 3)
+    out_flood.side(2, 1)
+    out_chip(0, 2, 0)
     down_hop(3, 0)
-    down_hop(3, 1)
-    down_hop(3, 2)
-    down_hop(3, 3)
-    out_flood.side(2, 0)
-    out_flood.side(2, 1)
+    up_flood.side()
+    gu_floods[1].hop(1, 0)
+    gu_floods[1].hop(2, 1)
     kv_end()
-    up_flood.side()
     attention()
+    gu_floods[0].hop(2, 1)
+    out_chip(1, 0, 0)
+    out_chip(1, 3, 0)
+    out_chip(1, 1, 1)
+    out_chip(0, 2, 1)
+    out_chip(1, 1, 0)
+    up_flood.hop(1, 0)
+    out_chip(0, 3, 1)
+    out_chip(1, 2, 1)
+    out_chip(1, 3, 1)
+    share_end("cot", g_all)
     out_chip(1, 2, 0)
-    out_chip(1, 2, 1)
-    gu_floods[0].hop(2, 0)
+    gu_floods[1].hop(3, 1)
+    out_core()
+    up_flood.hop(1, 1)
     gu_floods[1].hop(2, 0)
-    gu_floods[0].hop(2, 1)
-    gu_floods[1].hop(2, 1)
-    out_chip(1, 0, 0)
-    out_chip(0, 3, 0)
-    out_chip(0, 3, 1)
-    out_chip(1, 1, 0)
-    out_chip(1, 1, 1)
-    out_chip(1, 3, 0)
-    out_chip(1, 3, 1)
-    out_core()
     out_project()
-    up_flood.hop(1, 0)
-    up_flood.hop(1, 1)
-    gu_floods[0].hop(3, 0)
+    gu_floods[0].hop(3, 1)
+    gu_floods[2].hop(2, 0)
+    down_side_end()
+    up_flood.hop(2, 0)
+    gu_floods[2].hop(2, 1)
+    up_flood.hop(2, 1)
     gu_floods[1].hop(3, 0)
-    gu_floods[0].hop(3, 1)
-    gu_floods[1].hop(3, 1)
-    down_side_end()
-    gu_floods[2].hop(2, 0)
-    gu_floods[2].hop(2, 1)
+    gu_floods[2].hop(3, 1)
     share_on("n2", n2_all)
-    up_flood.hop(2, 0)
-    up_flood.hop(2, 1)
     gu_sides(0)
     gu_sides(1)
     share_end("n2", n2_all)
+    gu_floods[2].hop(3, 0)
     feed(0)
-    gu_floods[2].hop(3, 0)
-    gu_floods[2].hop(3, 1)
     grad_ff(0)
-    gu_sinks[0].send(3, 0)
     gu_sinks[1].send(3, 0)
     gu_sinks[0].send(3, 1)
+    gu_sinks[0].send(2, 1)
+    up_flood.hop(3, 1)
+    gu_sides(2)
     gu_sinks[1].send(3, 1)
     gu_sinks[0].send(2, 0)
-    gu_sinks[1].send(2, 0)
-    gu_sinks[0].send(2, 1)
-    gu_sinks[1].send(2, 1)
-    gu_sides(2)
     up_flood.hop(3, 0)
-    up_flood.hop(3, 1)
     feed(1)
     grad_ff(1)
+    gu_sinks[1].send(2, 0)
+    gu_sinks[1].send(2, 1)
+    up_sink.add(3, 1)
     up_sink.add(3, 0)
-    up_sink.add(3, 1)
+    gu_sinks[0].send(3, 0)
+    gu_sinks[2].send(3, 1)
+    gp_block(0)
+    down_send(0, 0)
     gu_sinks[2].send(3, 0)
-    gu_sinks[2].send(3, 1)
+    gu_sinks[1].send(1, 0)
     down_send(1, 0)
+    op_block(0)
+    down_send(0, 1)
+    down_send(0, 3)
+    group_on("gp", gp, gp_box)
+    group_on("op", op, op_box)
+    gp_block(1)
+    down_send(0, 2)
+    gu_sinks[1].add(3, 0)
+    gu_sinks[1].add(2, 0)
     down_send(1, 1)
-    down_send(1, 2)
     down_send(1, 3)
-    down_send(0, 0)
-    down_send(0, 1)
-    down_send(0, 2)
-    down_send(0, 3)
-    gu_sinks[0].send(1, 0)
-    gu_sinks[1].send(1, 0)
+    gu_sinks[0].send(0, 0)
     gu_sinks[0].send(1, 1)
-    gu_sinks[1].send(1, 1)
     gu_sinks[2].send(2, 0)
-    gu_sinks[2].send(2, 1)
+    up_sink.add(2, 1)
     gu_sinks[0].add(3, 0)
-    gu_sinks[1].add(3, 0)
-    gu_sinks[0].add(3, 1)
+    up_sink.add(1, 1)
+    gu_sinks[0].add(2, 0)
     gu_sinks[1].add(3, 1)
-    gu_sinks[2].send(0, 0)
-    gp_block(0)
     share_on("ctx", ctx_all)
-    group_on("gp", gp, gp_box)
-    gu_sinks[0].send(0, 0)
-    gu_sinks[1].send(0, 0)
-    op_block(1)
-    op_block(0)
-    up_sink.add(2, 0)
-    up_sink.add(2, 1)
-    gp_block(1)
-    gu_sinks[2].add(3, 0)
-    gu_sinks[2].add(3, 1)
-    gu_sinks[0].add(2, 0)
-    gu_sinks[1].add(2, 0)
-    gu_sinks[0].add(2, 1)
-    gu_sinks[1].add(2, 1)
     hidden_back()
     grad_context()
+    up_sink.add(2, 0)
+    gu_sinks[0].add(3, 1)
     attention_back()
+    group_on("dkv", dkv, dkv_box)
+    share_end("ctx", ctx_all)
+    down_send(1, 2)
+    down_add(3, 0)
+    gu_sinks[2].add(3, 0)
+    gb_end()
+    gu_sinks[2].send(1, 0)
+    down_add(3, 1)
+    gu_sinks[2].send(2, 1)
+    gu_sinks[0].add(2, 1)
+    grad_out_all()
+    out_sink.send(3, 0)
+    down_add(3, 3)
+    gu_sinks[2].add(3, 1)
+    gu_sinks[0].send(1, 0)
+    gu_sinks[1].send(1, 1)
+    gu_sinks[1].add(2, 1)
+    gu_sinks[1].add(1, 0)
+    grad_mixed()
+    out_sink.send(3, 1)
+    down_add(3, 2)
     up_sink.add(1, 0)
-    up_sink.add(1, 1)
-    group_on("dkv", dkv, dkv_box)
-    gb_end()
-    share_end("ctx", ctx_all)
-    grad_out_all()
-    gu_sinks[2].send(1, 0)
+    down_add(2, 1)
+    down_add(2, 3)
+    gm_end()
+    grad_qkv_all()
+    out_sink.send(1, 1)
     gu_sinks[2].send(1, 1)
-    out_sink.send(3, 0)
-    out_sink.send(3, 1)
-    down_add(3, 0)
-    down_add(3, 1)
-    down_add(3, 2)
-    down_add(3, 3)
-    grad_mixed()
+    out_sink.send(1, 0)
+    gu_sinks[0].add(1, 1)
+    gu_sinks[2].send(0, 0)
+    qkv_sink.send(3, 1)
+    down_add(1, 1)
+    gu_sinks[2].add(2, 0)
+    gt_block(0)
+    down_add(1, 3)
+    gu_sinks[1].send(0, 0)
+    down_add(0, 1)
+    down_add(2, 0)
+    gt_block(1)
+    down_add(2, 2)
+    gu_sinks[2].add(2, 1)
+    gu_sinks[1].add(1, 1)
+    out_sink.send(2, 0)
+    group_on("gt", gp, gp_box)
+    out_sink.add(3, 1)
+    qkv_sink.send(3, 0)
     gu_sinks[0].add(1, 0)
-    gu_sinks[1].add(1, 0)
-    gu_sinks[0].add(1, 1)
-    gu_sinks[1].add(1, 1)
-    down_add(2, 0)
-    down_add(2, 1)
-    down_add(2, 2)
-    down_add(2, 3)
-    out_sink.send(1, 0)
-    out_sink.send(1, 1)
-    group_on("op", op, op_box)
-    gu_sinks[2].add(2, 0)
-    gu_sinks[2].add(2, 1)
-    gm_end()
-    gt_block(0)
-    gt_block(1)
     up_sink.add(0, 0)
-    grad_qkv_all()
-    qkv_sink.send(3, 0)
-    qkv_sink.send(3, 1)
-    out_sink.send(2, 0)
+    qkv_sink.send(2, 0)
     out_sink.send(2, 1)
-    group_on("gt", gp, gp_box)
-    qkv_sink.send(2, 0)
+    down_add(1, 0)
     qkv_sink.send(2, 1)
-    down_add(1, 0)
-    down_add(1, 1)
-    down_add(1, 2)
-    down_add(1, 3)
-    gu_sinks[0].add(0, 0)
-    gu_sinks[1].add(0, 0)
-    gu_finish(0)
-    gu_finish(1)
     tokens_end()
     gain_send(0)
     gain_take(0)
-    gu_sinks[2].add(1, 0)
+    out_sink.add(3, 0)
     gu_sinks[2].add(1, 1)
     gain_send(1)
+    down_add(1, 2)
+    gu_sinks[2].add(1, 0)
+    gu_sinks[0].add(0, 0)
+    gu_finish(0)
     gain_take(1)
-    out_sink.add(3, 0)
-    out_sink.add(3, 1)
+    qkv_sink.add(3, 1)
+    out_sink.add(2, 1)
     gain_send(2)
+    down_add(0, 0)
+    op_block(1)
     qkv_sink.send(1, 0)
+    qkv_sink.add(3, 0)
+    gu_sinks[1].add(0, 0)
+    gu_finish(1)
+    down_add(0, 3)
     qkv_sink.send(1, 1)
-    qkv_sink.add(3, 0)
-    qkv_sink.add(3, 1)
+    qkv_sink.send(0, 0)
+    up_sink.end()
+    gu_sinks[2].add(0, 0)
+    gu_finish(3)
     out_sink.add(2, 0)
-    out_sink.add(2, 1)
+    output_end()
+    gu_finish(2)
+    gain_take(2)
+    gain_send(3)
+    qkv_sink.add(2, 1)
     qkv_sink.add(2, 0)
-    qkv_sink.add(2, 1)
-    down_add(0, 0)
-    down_add(0, 1)
+    gain_take(3)
+    gain_send(4)
+    out_sink.send(0, 0)
     down_add(0, 2)
-    down_add(0, 3)
     down_finish()
-    gain_take(2)
-    gu_sinks[2].add(0, 0)
-    out_sink.send(0, 0)
-    qkv_sink.send(0, 0)
-    output_end()
-    up_sink.end()
-    gain_send(3)
+    out_sink.add(1, 1)
     out_sink.add(1, 0)
-    out_sink.add(1, 1)
-    gain_take(3)
-    gu_finish(2)
-    gu_finish(3)
-    gain_send(4)
+    gu_end(0)
     qkv_sink.add(1, 0)
     qkv_sink.add(1, 1)
-    out_sink.add(0, 0)
     gain_take(4)
     gain_send(5)
+    out_sink.add(0, 0)
     out_end()
-    gu_end(0)
+    gu_end(3)
     gu_end(1)
     down_end()
     gu_end(2)
-    gu_end(3)
     qkv_sink.add(0, 0)
     qkv_end()
     gain_take(5)
@@ -1667,6 +1713,8 @@
     qkv_wide = -(-qkv_cols // 128) * 128
     out_wide = -(-out_cols // 128) * 128
     deep = 8 * rows
+    main = out_cols // 128 * 128
+    packed = rows + 32
     slabs = KVH // 2
     stack = 2 * QH // KVH * row_count
 
@@ -1674,8 +1722,8 @@
         return pltpu.VMEM(shape, dtype)
 
     scratch = [
-        box(deep, qkv_wide), box(4, deep, out_wide), box(deep, 3 * units),
-        box(deep, qkv_wide), box(deep, out_wide), box(deep, 3 * units),
+        box(deep, qkv_wide), box(4, 8 * packed, main), box(4, deep, 128), box(rows, out_wide), box(deep, 3 * units),
+        box(deep, qkv_wide), box(8 * packed, main), box(deep, 3 * units),
         box(8, 8, 256, dtype=f32), box(8, deep + 128, dtype=f32),
         box(own_rows, 128, dtype=f32), box(own_rows, 128, dtype=f32),
         box(4 * own_rows, width), box(4 * own_rows, width), box(4 * own_rows, width),
@@ -1692,9 +1740,9 @@
         box(4, own_rows, width), box(3, own_rows, width),
         box(4, own_rows, width), box(3, own_rows, width),
         box(4, seq_count, 2 * slabs, row_count, 128), box(3, seq_count, 2 * slabs, row_count, 128),
-        box(2, 4, rows, qkv_wide), box(2, 4, rows, out_wide),
+        box(2, 4, rows, qkv_wide), box(2, 4, packed, main),
         box(3, 2, 4, rows, half), box(4, strip, half),
-        box(2, 3, rows, qkv_wide), box(2, 3, rows, out_wide),
+        box(2, 3, rows, qkv_wide), box(2, 3, packed, main),
         box(3, 2, 3, rows, half), box(2, 4, strip, half),
         box(2, 3, 2 * rows, half), box(rows, half),
         box(2, 2, rows, half), box(strip, half),
@@ -1704,6 +1752,7 @@
         pltpu.SemaphoreType.DMA((8,)),
     ]
     vmem = pl.BlockSpec(memory_space=pltpu.MemorySpace.VMEM)
+    hbm = pl.BlockSpec(memory_space=pltpu.MemorySpace.HBM)
     smem = pl.BlockSpec(memory_space=pltpu.MemorySpace.SMEM)
     shapes = (
         jax.ShapeDtypeStruct((own_rows, width), low),
@@ -1717,7 +1766,7 @@
     results = pl.pallas_call(
         functools.partial(layer_kernel, {}),
         out_shape=shapes,
-        in_specs=[vmem, vmem, smem] + [vmem] * 8,
+        in_specs=[vmem, vmem, smem, vmem, vmem, hbm, hbm] + [vmem] * 4,
         out_specs=[vmem] * 7,
         scratch_shapes=scratch,
         compiler_params=pltpu.CompilerParams(

time: 175 us -> 171 us (0.977)
  Pallas kernels: 173 us -> 170 us
    pallas_call x1, Pallas kernels: 171 us -> 168 us  [on_device_fast(): pl.pallas_call(functools.partial(layer_kernel, {}), out_shape=shapes, in_...]
where the time goes in v7:
time: 171 us
  Pallas kernels  170 us (99%)
    pallas_call x1, Pallas kernels, on_device_fast(): pl.pallas_call(functools.partial(layer_kernel, {}), out_shape=shapes, in_...  168 us

profile of v7, /device:TPU:0, one launch (start us, length us, event | category | flops | bytes accessed | tf_op | source)
XLA Modules:
  0.0 171.1 jit_solution(11497961255649985862)
XLA Ops:
  0.6 167.6 %layer.1 = (bf16[128,1152]{1,0:T(8,128)(2,1)}, bf16[128,1152]{1,0:T(8,128)(2,1)}, f32[8,1152]{1,0:T(8,128)}, bf16[144,512]{1,0:T(8,128)(2,1)}, bf16[144,384]{1,0...) custom-call(bf16[128,1152]{1,0:T(8,128)(2,1)} %bitcast.6, bf16[128,1152]{1,0:T(8,128)(2,1)} %bitcast.7, ...), custom_call_target="tpu_custom_call" | custom-call | tf_op jit(solution)/shard_map/layer/pallas_call | solution.py:1766
  168.3 2.8 %finish.1 = (bf16[128,1152]{1,0:T(8,128)(2,1)}, bf16[128,1152]{1,0:T(8,128)(2,1)}, f32[144,480]{1,0:T(8,128)}, f32[144,288]{1,0:T(8,128)}, f32[144,1536]{1,0:T(8...) custom-call(bf16[128,1152]{1,0:T(8,128)(2,1)} %get-tuple-element.23.output, ...), custom_call_target="tpu_custom_call" | custom-call | tf_op jit(solution)/shard_map/finish/pallas_call | solution.py:1781

commit v8 on v7

--- a/solution.py
+++ b/solution.py
@@ -1398,281 +1398,281 @@
             when(cond, copy.wait)
 
     mix_start(0)
+    tables()
     qkv_start()
     out_start()
+    mix_start(1)
+    tokens_start()
+    out_chip(0, 0, 0)
     down_mix_start()
-    tables()
-    tokens_start()
-    mix_start(1)
-    cot_start()
-    out_chip(0, 0, 0)
+    locals_end()
     mix_end(0)
-    locals_end()
     gu_floods[0].start()
+    mix_end(1)
+    gu_floods[1].start()
+    qkv_flood.hop(1, 0)
     qkv_flood.hop(1, 1)
-    mix_end(1)
-    out_flood.hop(1, 1)
-    out_flood.side(0, 0)
-    qkv_flood.hop(1, 0)
-    qkv_flood.hop(2, 0)
     gain_start()
     gain_flood.hop(1, 0)
+    qkv_flood.hop(2, 0)
+    out_flood.hop(1, 1)
+    out_flood.hop(1, 0)
     gain_flood.hop(2, 0)
-    gain_flood.hop(3, 0)
-    out_flood.hop(1, 0)
-    gu_floods[1].start()
     gain_flood.hop(1, 1)
     gain_flood.hop(2, 1)
+    qkv_flood.hop(2, 1)
+    gu_floods[0].hop(1, 0)
+    out_flood.side(0, 0)
+    gain_flood.hop(3, 0)
     gain_flood.hop(3, 1)
-    qkv_flood.hop(2, 1)
+    qkv_flood.hop(3, 0)
+    qkv_flood.side(1, 0)
+    mix_end(3)
+    out_flood.hop(2, 1)
     qkv_flood.hop(3, 1)
+    down_start(1)
     out_flood.hop(2, 0)
-    qkv_flood.side(1, 0)
-    qkv_flood.hop(3, 0)
-    down_start(1)
+    cot_start()
     share_on("tok", tok_all)
-    out_flood.hop(2, 1)
-    out_flood.hop(3, 1)
     mix_end(2)
     gu_floods[2].start()
+    qkv_flood.side(2, 0)
+    out_flood.hop(3, 1)
     down_start(0)
-    gain_sides()
+    out_chip(0, 1, 0)
+    qkv_flood.side(0, 0)
+    qkv_flood.side(3, 1)
     qkv_flood.side(3, 0)
-    qkv_flood.side(2, 0)
     qkv_flood.side(2, 1)
     down_start(3)
+    qkv_flood.side(1, 1)
     share_end("tok", tok_all)
-    gu_floods[0].hop(1, 0)
-    qkv_flood.side(3, 1)
-    qkv_flood.side(0, 0)
-    qkv_flood.side(1, 1)
+    gain_sides()
     project()
+    out_flood.hop(3, 0)
     down_hop(1, 1)
     down_hop(2, 1)
     down_hop(1, 0)
     down_hop(2, 0)
-    out_flood.hop(3, 0)
-    mix_end(3)
-    out_chip(0, 1, 0)
+    out_flood.side(1, 0)
     up_flood.start()
+    down_hop(1, 3)
     down_start(2)
-    down_hop(1, 3)
     down_hop(1, 2)
-    down_hop(2, 2)
-    gu_floods[0].hop(2, 0)
     gu_floods[2].hop(1, 0)
+    gu_floods[0].hop(1, 1)
     pq_end()
     kv_start()
-    gu_floods[0].hop(1, 1)
+    out_chip(0, 3, 1)
+    out_chip(0, 2, 1)
+    gu_floods[0].hop(2, 0)
+    gu_floods[0].hop(2, 1)
+    out_chip(1, 0, 0)
+    gu_floods[2].hop(1, 1)
+    down_hop(3, 1)
+    gu_floods[1].hop(1, 1)
+    down_hop(2, 3)
+    share_on("cot", g_all)
+    out_chip(0, 3, 0)
     out_flood.side(3, 0)
-    down_hop(3, 2)
-    out_chip(0, 3, 0)
+    gu_floods[1].hop(1, 0)
+    out_flood.side(3, 1)
+    out_chip(1, 1, 0)
+    queries()
+    out_flood.side(2, 0)
+    out_flood.side(1, 1)
+    down_hop(2, 2)
+    out_chip(0, 2, 0)
+    up_flood.side()
+    down_hop(3, 0)
+    out_flood.side(2, 1)
     gu_floods[0].hop(3, 0)
-    share_on("cot", g_all)
-    gu_floods[1].hop(1, 1)
-    queries()
-    out_flood.side(1, 1)
-    down_hop(2, 3)
-    gu_floods[2].hop(1, 1)
-    out_flood.side(1, 0)
-    out_chip(0, 1, 1)
-    down_hop(3, 1)
-    out_flood.side(2, 0)
-    out_flood.side(3, 1)
-    down_hop(3, 3)
-    out_flood.side(2, 1)
-    out_chip(0, 2, 0)
-    down_hop(3, 0)
-    up_flood.side()
-    gu_floods[1].hop(1, 0)
-    gu_floods[1].hop(2, 1)
     kv_end()
     attention()
-    gu_floods[0].hop(2, 1)
-    out_chip(1, 0, 0)
+    down_hop(3, 3)
+    down_hop(3, 2)
     out_chip(1, 3, 0)
     out_chip(1, 1, 1)
-    out_chip(0, 2, 1)
-    out_chip(1, 1, 0)
+    gu_floods[0].hop(3, 1)
+    out_chip(1, 2, 0)
+    gu_floods[1].hop(2, 0)
     up_flood.hop(1, 0)
-    out_chip(0, 3, 1)
     out_chip(1, 2, 1)
     out_chip(1, 3, 1)
+    gu_floods[1].hop(2, 1)
+    out_chip(0, 1, 1)
     share_end("cot", g_all)
-    out_chip(1, 2, 0)
+    out_core()
+    out_project()
     gu_floods[1].hop(3, 1)
-    out_core()
     up_flood.hop(1, 1)
-    gu_floods[1].hop(2, 0)
-    out_project()
-    gu_floods[0].hop(3, 1)
+    gu_floods[1].hop(3, 0)
+    gu_floods[2].hop(2, 1)
     gu_floods[2].hop(2, 0)
-    down_side_end()
+    gu_floods[2].hop(3, 0)
+    gu_floods[2].hop(3, 1)
     up_flood.hop(2, 0)
-    gu_floods[2].hop(2, 1)
     up_flood.hop(2, 1)
-    gu_floods[1].hop(3, 0)
-    gu_floods[2].hop(3, 1)
     share_on("n2", n2_all)
+    share_end("n2", n2_all)
     gu_sides(0)
     gu_sides(1)
-    share_end("n2", n2_all)
-    gu_floods[2].hop(3, 0)
+    down_side_end()
     feed(0)
     grad_ff(0)
+    gu_sinks[0].send(3, 1)
+    gu_sinks[1].send(2, 1)
+    gu_sinks[0].send(3, 0)
     gu_sinks[1].send(3, 0)
-    gu_sinks[0].send(3, 1)
-    gu_sinks[0].send(2, 1)
+    gu_sinks[1].send(2, 0)
+    down_send(0, 0)
     up_flood.hop(3, 1)
+    up_flood.hop(3, 0)
     gu_sides(2)
-    gu_sinks[1].send(3, 1)
-    gu_sinks[0].send(2, 0)
-    up_flood.hop(3, 0)
     feed(1)
     grad_ff(1)
-    gu_sinks[1].send(2, 0)
-    gu_sinks[1].send(2, 1)
     up_sink.add(3, 1)
+    down_send(1, 0)
     up_sink.add(3, 0)
-    gu_sinks[0].send(3, 0)
+    gu_sinks[0].send(2, 0)
+    gu_sinks[1].send(3, 1)
+    gp_block(0)
+    op_block(0)
+    group_on("gp", gp, gp_box)
+    gp_block(1)
+    gu_sinks[0].send(2, 1)
+    down_send(1, 1)
+    down_send(0, 1)
+    up_sink.add(2, 1)
+    gu_sinks[2].send(2, 1)
+    gu_sinks[0].add(3, 0)
+    gu_sinks[1].add(3, 0)
+    gu_sinks[1].add(2, 0)
+    up_sink.add(2, 0)
     gu_sinks[2].send(3, 1)
-    gp_block(0)
-    down_send(0, 0)
+    group_on("op", op, op_box)
     gu_sinks[2].send(3, 0)
     gu_sinks[1].send(1, 0)
-    down_send(1, 0)
-    op_block(0)
-    down_send(0, 1)
+    gu_sinks[0].add(2, 0)
     down_send(0, 3)
-    group_on("gp", gp, gp_box)
-    group_on("op", op, op_box)
-    gp_block(1)
+    down_send(1, 3)
+    down_add(3, 0)
+    gu_sinks[2].send(2, 0)
+    gu_sinks[0].send(1, 1)
+    up_sink.add(1, 1)
+    hidden_back()
     down_send(0, 2)
-    gu_sinks[1].add(3, 0)
-    gu_sinks[1].add(2, 0)
-    down_send(1, 1)
-    down_send(1, 3)
+    gu_sinks[0].add(3, 1)
+    share_on("ctx", ctx_all)
+    grad_context()
+    attention_back()
+    down_add(3, 1)
+    down_send(1, 2)
+    gu_sinks[1].add(3, 1)
+    group_on("dkv", dkv, dkv_box)
+    gu_sinks[0].add(2, 1)
+    share_end("ctx", ctx_all)
+    gb_end()
+    grad_out_all()
+    down_add(3, 3)
+    gu_sinks[2].send(1, 1)
+    out_sink.send(3, 0)
+    gu_sinks[1].send(1, 1)
+    gu_sinks[1].add(1, 0)
+    gu_sinks[1].add(2, 1)
+    down_add(2, 1)
+    grad_mixed()
+    gu_sinks[2].add(3, 1)
+    gu_sinks[2].send(0, 0)
+    gu_sinks[2].add(3, 0)
+    gu_sinks[2].send(1, 0)
+    down_add(2, 3)
+    down_add(1, 1)
+    up_sink.add(1, 0)
+    gu_sinks[0].add(1, 1)
+    out_sink.send(3, 1)
+    out_sink.send(1, 1)
+    gu_sinks[0].send(1, 0)
+    gm_end()
+    down_add(2, 0)
     gu_sinks[0].send(0, 0)
-    gu_sinks[0].send(1, 1)
-    gu_sinks[2].send(2, 0)
-    up_sink.add(2, 1)
-    gu_sinks[0].add(3, 0)
-    up_sink.add(1, 1)
-    gu_sinks[0].add(2, 0)
-    gu_sinks[1].add(3, 1)
-    share_on("ctx", ctx_all)
-    hidden_back()
-    grad_context()
-    up_sink.add(2, 0)
-    gu_sinks[0].add(3, 1)
-    attention_back()
-    group_on("dkv", dkv, dkv_box)
-    share_end("ctx", ctx_all)
-    down_send(1, 2)
-    down_add(3, 0)
-    gu_sinks[2].add(3, 0)
-    gb_end()
-    gu_sinks[2].send(1, 0)
-    down_add(3, 1)
-    gu_sinks[2].send(2, 1)
-    gu_sinks[0].add(2, 1)
-    grad_out_all()
-    out_sink.send(3, 0)
-    down_add(3, 3)
-    gu_sinks[2].add(3, 1)
-    gu_sinks[0].send(1, 0)
-    gu_sinks[1].send(1, 1)
-    gu_sinks[1].add(2, 1)
-    gu_sinks[1].add(1, 0)
-    grad_mixed()
-    out_sink.send(3, 1)
+    gt_block(0)
+    group_on("gt", gp, gp_box)
+    grad_qkv_all()
+    qkv_sink.send(2, 1)
+    qkv_sink.send(3, 0)
     down_add(3, 2)
-    up_sink.add(1, 0)
-    down_add(2, 1)
-    down_add(2, 3)
-    gm_end()
-    grad_qkv_all()
-    out_sink.send(1, 1)
-    gu_sinks[2].send(1, 1)
-    out_sink.send(1, 0)
-    gu_sinks[0].add(1, 1)
-    gu_sinks[2].send(0, 0)
     qkv_sink.send(3, 1)
-    down_add(1, 1)
     gu_sinks[2].add(2, 0)
-    gt_block(0)
+    gu_sinks[2].add(2, 1)
     down_add(1, 3)
     gu_sinks[1].send(0, 0)
-    down_add(0, 1)
-    down_add(2, 0)
     gt_block(1)
+    gu_sinks[1].add(1, 1)
     down_add(2, 2)
-    gu_sinks[2].add(2, 1)
-    gu_sinks[1].add(1, 1)
+    down_add(1, 0)
+    qkv_sink.send(2, 0)
+    gu_sinks[0].add(1, 0)
+    out_sink.send(1, 0)
+    gu_sinks[2].add(1, 1)
+    up_sink.add(0, 0)
+    out_sink.add(3, 1)
+    out_sink.send(2, 1)
+    gu_sinks[2].add(1, 0)
+    tokens_end()
     out_sink.send(2, 0)
-    group_on("gt", gp, gp_box)
-    out_sink.add(3, 1)
-    qkv_sink.send(3, 0)
-    gu_sinks[0].add(1, 0)
-    up_sink.add(0, 0)
-    qkv_sink.send(2, 0)
-    out_sink.send(2, 1)
-    down_add(1, 0)
-    qkv_sink.send(2, 1)
-    tokens_end()
     gain_send(0)
     gain_take(0)
+    gain_send(1)
+    gain_take(1)
+    gain_send(2)
     out_sink.add(3, 0)
-    gu_sinks[2].add(1, 1)
-    gain_send(1)
+    op_block(1)
     down_add(1, 2)
-    gu_sinks[2].add(1, 0)
+    qkv_sink.add(3, 1)
     gu_sinks[0].add(0, 0)
     gu_finish(0)
-    gain_take(1)
-    qkv_sink.add(3, 1)
+    qkv_sink.add(3, 0)
+    qkv_sink.send(1, 1)
+    out_sink.add(2, 0)
     out_sink.add(2, 1)
-    gain_send(2)
-    down_add(0, 0)
-    op_block(1)
+    gu_sinks[1].add(0, 0)
+    down_add(0, 1)
+    gu_sinks[2].add(0, 0)
+    gu_finish(1)
+    up_sink.end()
     qkv_sink.send(1, 0)
-    qkv_sink.add(3, 0)
-    gu_sinks[1].add(0, 0)
-    gu_finish(1)
-    down_add(0, 3)
-    qkv_sink.send(1, 1)
-    qkv_sink.send(0, 0)
-    up_sink.end()
-    gu_sinks[2].add(0, 0)
-    gu_finish(3)
-    out_sink.add(2, 0)
-    output_end()
-    gu_finish(2)
     gain_take(2)
     gain_send(3)
     qkv_sink.add(2, 1)
     qkv_sink.add(2, 0)
+    down_add(0, 0)
+    down_add(0, 2)
+    down_add(0, 3)
+    down_finish()
+    out_sink.add(1, 0)
+    gu_finish(3)
+    out_sink.add(1, 1)
+    gu_finish(2)
+    output_end()
     gain_take(3)
+    gu_end(0)
+    gu_end(1)
     gain_send(4)
+    qkv_sink.send(0, 0)
+    qkv_sink.add(1, 1)
+    qkv_sink.add(1, 0)
     out_sink.send(0, 0)
-    down_add(0, 2)
-    down_finish()
-    out_sink.add(1, 1)
-    out_sink.add(1, 0)
-    gu_end(0)
-    qkv_sink.add(1, 0)
-    qkv_sink.add(1, 1)
     gain_take(4)
     gain_send(5)
+    gu_end(3)
     out_sink.add(0, 0)
     out_end()
-    gu_end(3)
-    gu_end(1)
-    down_end()
-    gu_end(2)
     qkv_sink.add(0, 0)
     qkv_end()
+    gu_end(2)
     gain_take(5)
+    down_end()
     wires.drain()
 
 

time: 171 us -> 169 us (0.988)
  Pallas kernels: 170 us -> 168 us
    pallas_call x1, Pallas kernels: 168 us -> 165 us  [on_device_fast(): pl.pallas_call(functools.partial(layer_kernel, {}), out_shape=shapes, in_...]
where the time goes in v8:
time: 169 us
  Pallas kernels  168 us (99%)
    pallas_call x1, Pallas kernels, on_device_fast(): pl.pallas_call(functools.partial(layer_kernel, {}), out_shape=shapes, in_...  165 us

profile of v8, /device:TPU:0, one launch (start us, length us, event | category | flops | bytes accessed | tf_op | source)
XLA Modules:
  0.0 168.7 jit_solution(12406161817732742122)
XLA Ops:
  0.6 165.3 %layer.1 = (bf16[128,1152]{1,0:T(8,128)(2,1)}, bf16[128,1152]{1,0:T(8,128)(2,1)}, f32[8,1152]{1,0:T(8,128)}, bf16[144,512]{1,0:T(8,128)(2,1)}, bf16[144,384]{1,0...) custom-call(bf16[128,1152]{1,0:T(8,128)(2,1)} %bitcast.6, bf16[128,1152]{1,0:T(8,128)(2,1)} %bitcast.7, ...), custom_call_target="tpu_custom_call" | custom-call | tf_op jit(solution)/shard_map/layer/pallas_call | solution.py:1766
  165.9 2.8 %finish.1 = (bf16[128,1152]{1,0:T(8,128)(2,1)}, bf16[128,1152]{1,0:T(8,128)(2,1)}, f32[144,480]{1,0:T(8,128)}, f32[144,288]{1,0:T(8,128)}, f32[144,1536]{1,0:T(8...) custom-call(bf16[128,1152]{1,0:T(8,128)(2,1)} %get-tuple-element.23.output, ...), custom_call_target="tpu_custom_call" | custom-call | tf_op jit(solution)/shard_map/finish/pallas_call | solution.py:1781

commit v9 on v8

--- a/solution.py
+++ b/solution.py
@@ -351,7 +351,7 @@
 
 
 BELOW, ABOVE = Way.BELOW, Way.ABOVE
-RINGS = (12, 16, 28, 24, 16)
+RINGS = (8, 14, 24, 20, 12)
 SENDS = sum(RINGS)
 
 
@@ -1748,7 +1748,7 @@
         box(2, 2, rows, half), box(strip, half),
         box(6, 8, width, dtype=f32), box(6, 8, width, dtype=f32),
         pltpu.SemaphoreType.DMA((SENDS,)),
-        pltpu.SemaphoreType.DMA((180,)),
+        pltpu.SemaphoreType.DMA((178,)),
         pltpu.SemaphoreType.DMA((8,)),
     ]
     vmem = pl.BlockSpec(memory_space=pltpu.MemorySpace.VMEM)

time: 169 us -> 169 us (level)
  no operation moved by 1% of the time
where the time goes in v9:
time: 169 us
  Pallas kernels  168 us (99%)
    pallas_call x1, Pallas kernels, on_device_fast(): pl.pallas_call(functools.partial(layer_kernel, {}), out_shape=shapes, in_...  165 us

profile of v9, /device:TPU:0, one launch (start us, length us, event | category | flops | bytes accessed | tf_op | source)
XLA Modules:
  0.0 168.6 jit_solution(14167419643791272013)
XLA Ops:
  0.6 165.1 %layer.1 = (bf16[128,1152]{1,0:T(8,128)(2,1)}, bf16[128,1152]{1,0:T(8,128)(2,1)}, f32[8,1152]{1,0:T(8,128)}, bf16[144,512]{1,0:T(8,128)(2,1)}, bf16[144,384]{1,0...) custom-call(bf16[128,1152]{1,0:T(8,128)(2,1)} %bitcast.6, bf16[128,1152]{1,0:T(8,128)(2,1)} %bitcast.7, ...), custom_call_target="tpu_custom_call" | custom-call | tf_op jit(solution)/shard_map/layer/pallas_call | solution.py:1766
  165.8 2.8 %finish.1 = (bf16[128,1152]{1,0:T(8,128)(2,1)}, bf16[128,1152]{1,0:T(8,128)(2,1)}, f32[144,480]{1,0:T(8,128)}, f32[144,288]{1,0:T(8,128)}, f32[144,1536]{1,0:T(8...) custom-call(bf16[128,1152]{1,0:T(8,128)(2,1)} %get-tuple-element.23.output, ...), custom_call_target="tpu_custom_call" | custom-call | tf_op jit(solution)/shard_map/finish/pallas_call | solution.py:1781
